TPU v7x, 128 devices: a whole 4x4x4 slice. The times are simulated.
128 devices in a mesh: batch: 32 (over z, x, core), tile: 4 (over y).
Axes of the slice: x: 4, y: 4, z: 4, core: 2. Of those that a mesh axis runs over, the one named last changes fastest.
Arguments:
- slot_state_vectors: bfloat16 [128, 256, 768], P(('batch', 'tile')), may hold values from -6 to 6
- sequence_token_counts: int32 [128], P(('batch', 'tile')), may hold values from 8 to 256, as said below
- positive_companion: int32 [128], replicated, may hold values from 0 to 127, as said below
- leading_dimension_counts: int32 [4], replicated, may hold values from 64 to 768, as said below
- affinity_divisor: float32 [1], replicated, may hold values from 0.02 to 0.08
- triple_projection_matrix: bfloat16 [2, 768, 2304], replicated, may hold values from -0.21875 to 0.21875
- probe_payload_shift: bfloat16 [2, 1536], replicated, may hold values from -1.5 to 1.5
- mixer_projection_matrix: bfloat16 [2, 768, 768], replicated, may hold values from -0.875 to 0.875
- mixer_projection_shift: bfloat16 [2, 768], replicated, may hold values from -1.5 to 1.5
- mixer_scale_factor: bfloat16 [2, 768], replicated, may hold values from 0.5 to 1.5
- mixer_shift_term: bfloat16 [2, 768], replicated, may hold values from -1.5 to 1.5
- expand_layer_matrix: bfloat16 [2, 768, 3072], replicated, may hold values from -0.21875 to 0.21875
- expand_layer_shift: bfloat16 [2, 3072], replicated, may hold values from -1.5 to 1.5
- shrink_layer_matrix: bfloat16 [2, 3072, 768], replicated, may hold values from -0.109375 to 0.109375
- shrink_layer_shift: bfloat16 [2, 768], replicated, may hold values from -1.5 to 1.5
- closing_scale_factor: bfloat16 [2, 768], replicated, may hold values from 0.5 to 1.5
- closing_shift_term: bfloat16 [2, 768], replicated, may hold values from -1.5 to 1.5
Outputs:
- loss: float32 [128], P('batch')
- embeddings: float32 [128, 2, 768], P(('batch', 'tile'))
- input_grad: float32 [128, 256, 768], P(('batch', 'tile'))
- query_key_value_gradient: float32 [2, 768, 2304], P(None, ('batch', 'tile'))
- grad_qvbias: float32 [2, 1536], P(None, ('batch', 'tile'))
- grad_outproj: float32 [2, 768, 768], P(None, ('batch', 'tile'))
- grad_outbias: float32 [2, 768], P(None, ('batch', 'tile'))
- grad_attgain: float32 [2, 768], P(None, ('batch', 'tile'))
- grad_attshift: float32 [2, 768], P(None, ('batch', 'tile'))
- feedforward_input_gradient: float32 [2, 768, 3072], P(None, ('batch', 'tile'))
- grad_ffnbias: float32 [2, 3072], P(None, ('batch', 'tile'))
- grad_downproj: float32 [2, 3072, 768], P(None, ('batch', 'tile'))
- grad_downbias: float32 [2, 768], P(None, ('batch', 'tile'))
- grad_fingain: float32 [2, 768], P(None, ('batch', 'tile'))
- grad_finshift: float32 [2, 768], P(None, ('batch', 'tile'))
Inputs may be any that keep to these rules, and one draw needn't show every extreme that they name: The first sequence_token_counts[i] slots of sequence i are real, the rest padding; some sequence has 256 and some has 8. positive_companion[positive_companion[i]] == i and positive_companion[i] != i. `leading_dimension_counts`: strictly increasing multiples of 32, none under 64, the last equal to 768.
All inputs are finite; a program needn't handle non-finite values.
Results may differ from a plain program's by a relative error of at most 0.012.
Values sent between devices are 32-bit elements; how exact they have to be, the bound alone decides.
A program may use at most 320 MiB of HBM per device.

v0:
```python
from functools import partial

import jax
import jax.numpy as jnp
from jax import lax
from jax.sharding import PartitionSpec as P

HEADS = 12


eps_norm = 1e-06
exact_arithmetic_mode = lax.Precision.HIGHEST


def combined_all(part, axis, combine):
    gathered = jax.tree.map(lambda a: lax.all_gather(a, axis), part)

    def take(source):
        return jax.tree.map(lambda a: lax.dynamic_index_in_dim(a, source, 0, False), gathered)

    return lax.fori_loop(
        1, lax.axis_size(axis), lambda source, state: combine(state, take(source)), take(0)
    )


def norm_forward(total_loss, gain, shift):
    center = total_loss - jnp.mean(total_loss, axis=-1, keepdims=True)
    spread = jnp.mean(center * center, axis=-1, keepdims=True)
    scaled = lax.rsqrt(spread + eps_norm)
    normed = center * scaled
    return (normed * gain + shift, normed, scaled)


def norm_backward(grad, normed, scaled, gain):
    grad_gain = jnp.sum(grad * normed, axis=(0, 1))
    grad_shift = jnp.sum(grad, axis=(0, 1))
    dnormed = grad * gain
    inside = (
        dnormed
        - jnp.mean(dnormed, axis=-1, keepdims=True)
        - normed * jnp.mean(dnormed * normed, axis=-1, keepdims=True)
    )
    return (scaled * inside, grad_gain, grad_shift)


def layer_forward(hidden, params, keymask):
    (
        triple_projection_matrix,
        probe_payload_shift,
        mixer_projection_matrix,
        mixer_projection_shift,
        mixer_scale_factor,
        mixer_shift_term,
        expand_layer_matrix,
        expand_layer_shift,
        shrink_layer_matrix,
        shrink_layer_shift,
        closing_scale_factor,
        closing_shift_term,
    ) = params
    count, length, width = hidden.shape
    heads_size = width // HEADS
    bias = probe_payload_shift.astype(jnp.float32)
    full_bias = jnp.concatenate([bias[:width], jnp.zeros((width,), jnp.float32), bias[width:]])
    hidden_reduced = hidden.astype(jnp.bfloat16)
    mixed = (
        jnp.einsum(
            "gwk,km->gwm",
            hidden_reduced,
            triple_projection_matrix,
            preferred_element_type=jnp.float32,
        )
        + full_bias
    )
    mixed_low = mixed.astype(jnp.bfloat16)
    query = mixed_low[..., :width].reshape(count, length, HEADS, heads_size)
    keys = mixed_low[..., width : 2 * width].reshape(count, length, HEADS, heads_size)
    values = mixed_low[..., 2 * width :].reshape(count, length, HEADS, heads_size)
    scores = jnp.einsum(
        "sqhd,skhd->shqk", query, keys, preferred_element_type=jnp.float32
    ) * heads_size ** (-0.5)
    scores = scores + keymask[:, None, None, :]
    expo = jnp.exp(scores - jnp.max(scores, axis=-1, keepdims=True))
    probs = expo / jnp.sum(expo, axis=-1, keepdims=True)
    probs_low = probs.astype(jnp.bfloat16)
    context = jnp.einsum("shqk,skhd->sqhd", probs_low, values, preferred_element_type=jnp.float32)
    context_reduced = context.astype(jnp.bfloat16).reshape(count, length, width)
    attended = jnp.einsum(
        "bry,yt->brt", context_reduced, mixer_projection_matrix, preferred_element_type=jnp.float32
    ) + mixer_projection_shift.astype(jnp.float32)
    middle, normed_one, scaled_one = norm_forward(
        hidden + attended,
        mixer_scale_factor.astype(jnp.float32),
        mixer_shift_term.astype(jnp.float32),
    )
    middle_reduced = middle.astype(jnp.bfloat16)
    inner = jnp.einsum(
        "ncm,mj->ncj", middle_reduced, expand_layer_matrix, preferred_element_type=jnp.float32
    ) + expand_layer_shift.astype(jnp.float32)
    activation_reduced = jax.nn.gelu(inner, approximate=False).astype(jnp.bfloat16)
    outer = jnp.einsum(
        "pcx,xj->pcj", activation_reduced, shrink_layer_matrix, preferred_element_type=jnp.float32
    ) + shrink_layer_shift.astype(jnp.float32)
    result, normed_two, scaled_two = norm_forward(
        middle + outer,
        closing_scale_factor.astype(jnp.float32),
        closing_shift_term.astype(jnp.float32),
    )
    saved = (
        hidden_reduced,
        query,
        keys,
        values,
        probs,
        probs_low,
        context_reduced,
        normed_one,
        scaled_one,
        middle_reduced,
        inner,
        activation_reduced,
        normed_two,
        scaled_two,
    )
    return (result, saved)


def layer_backward(grad_out, saved, params):
    (
        triple_projection_matrix,
        probe_payload_shift,
        mixer_projection_matrix,
        mixer_projection_shift,
        mixer_scale_factor,
        mixer_shift_term,
        expand_layer_matrix,
        expand_layer_shift,
        shrink_layer_matrix,
        shrink_layer_shift,
        closing_scale_factor,
        closing_shift_term,
    ) = params
    (
        hidden_reduced,
        query,
        keys,
        values,
        probs,
        probs_low,
        context_reduced,
        normed_one,
        scaled_one,
        middle_reduced,
        inner,
        activation_reduced,
        normed_two,
        scaled_two,
    ) = saved
    count, length, width = grad_out.shape
    heads_size = query.shape[-1]
    dsum_two, grad_fingain, grad_finshift = norm_backward(
        grad_out, normed_two, scaled_two, closing_scale_factor.astype(jnp.float32)
    )
    outer_gradient = dsum_two.astype(jnp.bfloat16)
    grad_downbias = jnp.sum(outer_gradient.astype(jnp.float32), axis=(0, 1))
    grad_downproj = jnp.einsum(
        "eqo,eqk->ok", activation_reduced, outer_gradient, preferred_element_type=jnp.float32
    )
    activation_gradient = jnp.einsum(
        "cov,gv->cog", outer_gradient, shrink_layer_matrix, preferred_element_type=jnp.float32
    )
    unused, gelu_pull = jax.vjp(partial(jax.nn.gelu, approximate=False), inner)
    inner_gradient = gelu_pull(activation_gradient)[0].astype(jnp.bfloat16)
    grad_ffnbias = jnp.sum(inner_gradient.astype(jnp.float32), axis=(0, 1))
    feedforward_input_gradient = jnp.einsum(
        "uik,uie->ke", middle_reduced, inner_gradient, preferred_element_type=jnp.float32
    )
    dmiddle = dsum_two + jnp.einsum(
        "qec,pc->qep", inner_gradient, expand_layer_matrix, preferred_element_type=jnp.float32
    )
    dsum_one, grad_attgain, grad_attshift = norm_backward(
        dmiddle, normed_one, scaled_one, mixer_scale_factor.astype(jnp.float32)
    )
    attention_gradient = dsum_one.astype(jnp.bfloat16)
    grad_outbias = jnp.sum(attention_gradient.astype(jnp.float32), axis=(0, 1))
    grad_outproj = jnp.einsum(
        "rkv,rkb->vb", context_reduced, attention_gradient, preferred_element_type=jnp.float32
    )
    context_gradient = jnp.einsum(
        "cqu,wu->cqw",
        attention_gradient,
        mixer_projection_matrix,
        preferred_element_type=jnp.float32,
    )
    context_gradient = context_gradient.astype(jnp.bfloat16).reshape(
        count, length, HEADS, heads_size
    )
    dprobs = jnp.einsum(
        "sqhd,skhd->shqk", context_gradient, values, preferred_element_type=jnp.float32
    )
    dvalues = jnp.einsum(
        "shqk,sqhd->skhd", probs_low, context_gradient, preferred_element_type=jnp.float32
    )
    dscores = probs * (dprobs - jnp.sum(dprobs * probs, axis=-1, keepdims=True))
    dscores = dscores.astype(jnp.bfloat16)
    factor = heads_size ** (-0.5)
    dquery = (
        jnp.einsum("shqk,skhd->sqhd", dscores, keys, preferred_element_type=jnp.float32) * factor
    )
    dkeys = (
        jnp.einsum("shqk,sqhd->skhd", dscores, query, preferred_element_type=jnp.float32) * factor
    )
    mixed_gradient = jnp.concatenate(
        [
            dquery.reshape(count, length, width),
            dkeys.reshape(count, length, width),
            dvalues.reshape(count, length, width),
        ],
        axis=-1,
    )
    mixed_gradient = mixed_gradient.astype(jnp.bfloat16)
    bias_sums = jnp.sum(mixed_gradient.astype(jnp.float32), axis=(0, 1))
    grad_qvbias = jnp.concatenate([bias_sums[:width], bias_sums[2 * width :]])
    query_key_value_gradient = jnp.einsum(
        "uaz,uan->zn", hidden_reduced, mixed_gradient, preferred_element_type=jnp.float32
    )
    dhidden = dsum_one + jnp.einsum(
        "inu,tu->int", mixed_gradient, triple_projection_matrix, preferred_element_type=jnp.float32
    )
    grads = (
        query_key_value_gradient,
        grad_qvbias,
        grad_outproj,
        grad_outbias,
        grad_attgain,
        grad_attshift,
        feedforward_input_gradient,
        grad_ffnbias,
        grad_downproj,
        grad_downbias,
        grad_fingain,
        grad_finshift,
    )
    return (dhidden, grads)


def pairing_cost_term(
    averaged_layer_states, positive_companion, leading_dimension_counts, affinity_divisor
):
    batches = lax.axis_size("batch")
    tiles = lax.axis_size("tile")
    per_dev = averaged_layer_states.shape[0]
    width = averaged_layer_states.shape[-1]
    nested_level_count = leading_dimension_counts.shape[0]
    rows = lax.all_gather(averaged_layer_states, "tile", axis=0, tiled=True)
    cols = lax.all_gather(averaged_layer_states, "batch", axis=0, tiled=True)
    columns = lax.broadcasted_iota(jnp.int32, (nested_level_count, width), 1)
    keep = (columns < leading_dimension_counts[:, None]).astype(jnp.float32)

    def unit_of(embed):
        masked = embed[:, :, None, :] * keep
        inverse = lax.rsqrt(jnp.sum(masked * masked, axis=-1, keepdims=True) + eps_norm)
        return (masked * inverse, inverse)

    def unit_back(normalized_direction, inverse, dunit):
        inside = dunit - normalized_direction * jnp.sum(
            normalized_direction * dunit, axis=-1, keepdims=True
        )
        return jnp.sum(keep * inside * inverse, axis=2)

    row_unit, row_inv = unit_of(rows)
    col_unit, col_inv = unit_of(cols)
    logit_divisor_scalar = affinity_divisor[0]
    affinity_matrix = (
        jnp.einsum("zwfq,xwfq->wfzx", row_unit, col_unit, precision=exact_arithmetic_mode)
        / logit_divisor_scalar
    )
    batch_idx = lax.axis_index("batch")
    tile_idx = lax.axis_index("tile")
    row_ids = batch_idx * tiles * per_dev + jnp.arange(tiles * per_dev, dtype=jnp.int32)
    col_pos = jnp.arange(batches * per_dev, dtype=jnp.int32)
    col_ids = (col_pos // per_dev * tiles + tile_idx) * per_dev + col_pos % per_dev
    selfs = row_ids[:, None] == col_ids[None, :]
    latent_affinity_matrix = jnp.where(selfs, -1e30, affinity_matrix)
    top = jnp.max(latent_affinity_matrix, axis=-1)
    total_exp = jnp.sum(jnp.exp(latent_affinity_matrix - top[..., None]), axis=-1)
    targets = jnp.take(positive_companion, row_ids)
    matching_indicator = (col_ids[None, :] == targets[:, None]).astype(jnp.float32)
    target_part = jnp.sum(affinity_matrix * matching_indicator, axis=-1)

    def combine(first, second):
        upper = jnp.maximum(first[0], second[0])
        return (
            upper,
            first[1] * jnp.exp(first[0] - upper) + second[1] * jnp.exp(second[0] - upper),
            first[2] + second[2],
        )

    top, total_exp, target_sims = combined_all((top, total_exp, target_part), "tile", combine)
    logsumexp_values = top + jnp.log(total_exp)
    row_losses = jnp.sum(logsumexp_values - target_sims, axis=(0, 1)) / (2 * nested_level_count)
    affinity_grad_matrix = (
        (jnp.exp(latent_affinity_matrix - logsumexp_values[..., None]) - matching_indicator)
        / (2 * nested_level_count)
        / logit_divisor_scalar
    )
    drow_unit = jnp.einsum(
        "lpij,jlpd->ilpd", affinity_grad_matrix, col_unit, precision=exact_arithmetic_mode
    )
    dcol_unit = jnp.einsum(
        "lpij,ilpd->jlpd", affinity_grad_matrix, row_unit, precision=exact_arithmetic_mode
    )
    drows = lax.psum_scatter(
        unit_back(row_unit, row_inv, drow_unit), "tile", scatter_dimension=0, tiled=True
    )
    dcols = lax.psum_scatter(
        unit_back(col_unit, col_inv, dcol_unit), "batch", scatter_dimension=0, tiled=True
    )
    return (row_losses, drows + dcols)


def body(
    slot_state_vectors,
    sequence_token_counts,
    positive_companion,
    leading_dimension_counts,
    affinity_divisor,
    triple_projection_matrix,
    probe_payload_shift,
    mixer_projection_matrix,
    mixer_projection_shift,
    mixer_scale_factor,
    mixer_shift_term,
    expand_layer_matrix,
    expand_layer_shift,
    shrink_layer_matrix,
    shrink_layer_shift,
    closing_scale_factor,
    closing_shift_term,
):
    weights = (
        triple_projection_matrix,
        probe_payload_shift,
        mixer_projection_matrix,
        mixer_projection_shift,
        mixer_scale_factor,
        mixer_shift_term,
        expand_layer_matrix,
        expand_layer_shift,
        shrink_layer_matrix,
        shrink_layer_shift,
        closing_scale_factor,
        closing_shift_term,
    )
    first = tuple((w[0] for w in weights))
    second = tuple((w[1] for w in weights))
    places = lax.broadcasted_iota(jnp.int32, slot_state_vectors.shape[:2], 1)
    valid = (places < sequence_token_counts[:, None]).astype(jnp.float32)
    keymask = (valid - 1.0) * 1000000000.0
    counts = sequence_token_counts.astype(jnp.float32)[:, None]
    inputs = slot_state_vectors.astype(jnp.float32)
    front, saved_front = layer_forward(inputs, first, keymask)
    behind, saved_behind = layer_forward(front, second, keymask)
    averaged_layer_states = jnp.stack(
        [
            jnp.sum(front * valid[:, :, None], axis=1) / counts,
            jnp.sum(behind * valid[:, :, None], axis=1) / counts,
        ],
        axis=1,
    )
    row_losses, embedding_gradient = pairing_cost_term(
        averaged_layer_states, positive_companion, leading_dimension_counts, affinity_divisor
    )
    spread = valid[:, :, None] / counts[:, :, None]
    saved_behind = layer_forward(lax.optimization_barrier(front), second, keymask)[1]
    dfront, grads_behind = layer_backward(
        spread * embedding_gradient[:, 1][:, None, :], saved_behind, second
    )
    dfront = dfront + spread * embedding_gradient[:, 0][:, None, :]
    saved_front = layer_forward(lax.optimization_barrier(inputs), first, keymask)[1]
    dinputs, grads_front = layer_backward(dfront, saved_front, first)
    stacked = [jnp.stack([gf, gb]) for gf, gb in zip(grads_front, grads_behind)]
    reduced = (
        lax.psum_scatter(stacked[0], ("batch", "tile"), scatter_dimension=1, tiled=True),
        lax.psum_scatter(stacked[1], ("batch", "tile"), scatter_dimension=1, tiled=True),
        lax.psum_scatter(stacked[2], ("batch", "tile"), scatter_dimension=1, tiled=True),
        lax.psum_scatter(stacked[3], ("batch", "tile"), scatter_dimension=1, tiled=True),
        lax.psum_scatter(stacked[4], ("batch", "tile"), scatter_dimension=1, tiled=True),
        lax.psum_scatter(stacked[5], ("batch", "tile"), scatter_dimension=1, tiled=True),
        lax.psum_scatter(stacked[6], ("batch", "tile"), scatter_dimension=1, tiled=True),
        lax.psum_scatter(stacked[7], ("batch", "tile"), scatter_dimension=1, tiled=True),
        lax.psum_scatter(stacked[8], ("batch", "tile"), scatter_dimension=1, tiled=True),
        lax.psum_scatter(stacked[9], ("batch", "tile"), scatter_dimension=1, tiled=True),
        lax.psum_scatter(stacked[10], ("batch", "tile"), scatter_dimension=1, tiled=True),
        lax.psum_scatter(stacked[11], ("batch", "tile"), scatter_dimension=1, tiled=True),
    )
    return (
        row_losses,
        averaged_layer_states,
        dinputs,
        reduced[0],
        reduced[1],
        reduced[2],
        reduced[3],
        reduced[4],
        reduced[5],
        reduced[6],
        reduced[7],
        reduced[8],
        reduced[9],
        reduced[10],
        reduced[11],
    )


def solution(mesh):
    return jax.shard_map(
        body,
        mesh=mesh,
        in_specs=(
            P(("batch", "tile"), None, None),
            P(("batch", "tile")),
            P(),
            P(),
            P(),
            P(),
            P(),
            P(),
            P(),
            P(),
            P(),
            P(),
            P(),
            P(),
            P(),
            P(),
            P(),
        ),
        out_specs=(
            P("batch"),
            P(("batch", "tile"), None, None),
            P(("batch", "tile"), None, None),
            P(None, ("batch", "tile"), None),
            P(None, ("batch", "tile")),
            P(None, ("batch", "tile"), None),
            P(None, ("batch", "tile")),
            P(None, ("batch", "tile")),
            P(None, ("batch", "tile")),
            P(None, ("batch", "tile"), None),
            P(None, ("batch", "tile")),
            P(None, ("batch", "tile"), None),
            P(None, ("batch", "tile")),
            P(None, ("batch", "tile")),
            P(None, ("batch", "tile")),
        ),
        check_vma=False,
    )
```

profile of v0, /device:TPU:0, one launch (start us, length us, event | category | flops | bytes accessed | tf_op | source)
XLA Modules:
  0.0 1172.4 jit_solution(15719532853607736135)
XLA Ops:
  12.9 3.2 fusion.51
  16.8 2.8 fusion.511
  19.6 2.5 fusion.303
  23.8 13.5 %fusion.513 = (f32[256]{0:T(256)S(1)}, f32[1,256,768]{2,1,0:T(8,128)S(1)}) fusion(f32[768]{0:T(1024)S(1)} %get-tuple-element.280, bf16[2,3072,768]{2,1,0:T(8,128)(2,1)} %param.32, bf16[2,768,3072]{2,1,0:T(8,128)(2,1)} %param.30, f32[3072]{0:T(1024)S(1)} %bitcast.534, f32[1,256,768]{2,1,0:T(8,128)} %copy-done.54, f32[768]{0:T(1024)S(1)} %get-tuple-element.393, ...), kind=kOutput, calls=%fused_computation.633 | convolution fusion | flops 2470182656 | bytes 11834368 | tf_op jit(solution)/shard_map/pcx,xj->pcj/dot_general | solution.py:101
  39.6 3.1 fusion.50
  43.7 1.9 copy.120
  45.6 1.9 copy.119
  48.4 4.6 fusion.518
  53.1 2.3 fusion.302
  57.2 14.6 %fusion.520 = (f32[256]{0:T(256)S(1)}, f32[1,256,768]{2,1,0:T(8,128)}) fusion(f32[768]{0:T(1024)S(1)} %copy-done.127, bf16[2,3072,768]{2,1,0:T(8,128)(2,1)} %param.32, bf16[2,768,3072]{2,1,0:T(8,128)(2,1)} %param.30, f32[3072]{0:T(1024)S(1)} %bitcast.532, f32[1,256,768]{2,1,0:T(8,128)} %copy-done.30, f32[768]{0:T(1024)S(1)} %get-tuple-element.394, ...), kind=kOutput, calls=%fused_computation.636 | convolution fusion | flops 2470182656 | bytes 11834368 | tf_op jit(solution)/shard_map/pcx,xj->pcj/dot_general | solution.py:101
  73.2 1.8 multiply_reduce_fusion.16
  75.1 12.5 %all_gather.24 = f32[4,2,768]{2,1,0:T(2,128)S(1)} all-gather(f32[1,2,768]{2,1,0:T(2,128)S(1)} %pad_maximum_fusion.16), channel_id=1, replica_groups=mesh['batch'=32,'tile'=4] {'tile'}, dimensions={0}, use_global_device_ids=true | all-gather | bytes 30720 | tf_op jit(solution)/shard_map/all_gather | solution.py:255
  87.6 26.0 %all_gather.25 = f32[32,2,768]{2,1,0:T(2,128)S(1)} all-gather(f32[1,2,768]{2,1,0:T(2,128)S(1)} %pad_maximum_fusion.16), channel_id=1, replica_groups=mesh['batch'=32,'tile'=4] {'batch'}, dimensions={0}, use_global_device_ids=true | all-gather | bytes 202752 | tf_op jit(solution)/shard_map/all_gather | solution.py:256
  117.6 12.1 %all-gather = f32[8,4,4]{2,1,0:T(4,128)S(1)} all-gather(f32[2,4,4]{2,1,0:T(4,128)S(1)} %get-tuple-element.362), channel_id=2, replica_groups=mesh['batch'=32,'tile'=4] {'tile'}, dimensions={0}, use_global_device_ids=true | all-gather | bytes 640 | tf_op jit(solution)/shard_map/all_gather | solution.py:16
  129.8 11.9 %all-gather.2 = f32[8,4,4]{2,1,0:T(4,128)S(1)} all-gather(f32[2,4,4]{2,1,0:T(4,128)S(1)} %get-tuple-element.261), channel_id=4, replica_groups=mesh['batch'=32,'tile'=4] {'tile'}, dimensions={0}, use_global_device_ids=true | all-gather | bytes 640 | tf_op jit(solution)/shard_map/all_gather | solution.py:16
  141.8 11.9 %all-gather.1 = f32[8,4,4]{2,1,0:T(4,128)S(1)} all-gather(f32[2,4,4]{2,1,0:T(4,128)S(1)} %get-tuple-element.262), channel_id=3, replica_groups=mesh['batch'=32,'tile'=4] {'tile'}, dimensions={0}, use_global_device_ids=true | all-gather | bytes 640 | tf_op jit(solution)/shard_map/all_gather | solution.py:16
  154.4 1.7 convolution_bitcast_fusion.8
  158.3 1.9 convert_element_type.416
  161.5 3.3 fusion.49
  167.1 2.1 copy.131
  169.1 1.9 copy.130
  171.0 3.1 fusion.48
  175.3 1.9 copy.136
  177.2 1.9 copy.135
  179.1 1.9 copy.134
  181.0 1.6 fusion.321
  184.3 18.2 %all-reduce = f32[4,2,768]{2,1,0:T(2,128)} all-reduce(f32[4,2,768]{2,1,0:T(2,128)} %copy.138), channel_id=5, replica_groups=mesh['batch'=32,'tile'=4] {'tile'}, use_global_device_ids=true, to_apply=%region_36.37.clone | all-reduce | flops 6144 | bytes 49152
  202.4 4.5 fusion.525
  206.9 2.3 convolution_convert_fusion.4
  211.6 4.4 fusion.530
  216.0 2.5 convolution_convert_fusion.5
  220.5 11.5 multiply_convert_fusion.3
  235.5 10.2 multiply_convert_fusion.2
  248.4 8.4 all-reduce.20.cloned.1.call-done
  256.8 2.0 dynamic-slice_add_fusion
  259.4 2.2 fusion.335
  261.6 2.1 convert_reduce_fusion.4
  263.7 7.1 convert_reduce_fusion
  270.8 5.4 multiply_reduce_fusion.4
  278.0 2.0 convolution_bitcast_fusion.6
  281.0 2.7 convolution_convert_fusion.2
  287.8 4.6 multiply_reduce_fusion.3
  293.4 5.3 convert_reduce_fusion.1
  298.7 2.2 multiply_reduce_fusion.5
  302.7 1.9 convolution_bitcast_fusion.7
  304.8 2.7 convolution_convert_fusion
  310.7 3.9 convolution_bitcast_fusion
  320.6 4.0 convolution_bitcast_fusion.5
  324.7 11.1 pad_maximum_fusion.2
  336.0 2.3 pad_maximum_fusion.3
  338.3 5.8 copy.150
  344.2 21.5 %copy.149 = f32[2,768,2304]{2,0,1:T(2,128)} copy(f32[2,768,2304]{1,2,0:T(8,128)} %pad_maximum_fusion.2) | data formatting | bytes 28311552 | tf_op jit(solution)/shard_map/stack | solution.py:382
  366.8 3.1 convolution_bitcast_fusion.4
  369.9 5.2 convolution_bitcast_fusion.3
  375.2 5.5 pad_maximum_fusion
  380.6 37.0 %copy.151 = f32[2,768,3072]{2,0,1:T(2,128)} copy(f32[2,768,3072]{2,1,0:T(8,128)S(1)} %pad_maximum_fusion) | data formatting | bytes 37748736 | tf_op jit(solution)/shard_map/stack | solution.py:382
  418.6 2.9 convolution_bitcast_fusion.1
  423.0 6.6 pad_maximum_fusion.1
  430.9 4.1 fusion.268
  435.0 37.8 %all-reduce.24.cloned.1.call-done = (f32[2,1536]{1,0:T(2,128)}, f32[2,768]{1,0:T(2,128)}, f32[2,768]{1,0:T(2,128)}, f32[2,768]{1,0:T(2,128)}, f32[2,3072]{1,0:T(...) async-done(((f32[2,1536]{1,0:T(2,128)}, f32[2,768]{1,0:T(2,128)}, f32[2,768]{1,0:T(2,128)}, f32[2,768]{1,0:T(2,128)}, f32[2,3072]{1,0:T(2,128)}, ...) | async-done | bytes 73744
  483.2 216.1 %all-reduce.26.cloned.1.call-done = (f32[2,768,2304]{2,0,1:T(2,128)}, f32[2,768,768]{2,0,1:T(2,128)}) async-done(((f32[2,768,2304]{2,0,1:T(2,128)}, f32[2,768,768]{2,0,1:T(2,128)}), (f32[2,768,2304]{2,0,1:T(2,128)}, f32[2,768,768]{2,0,1:T(2,128)})) %all-reduce.26.cloned.1.call-update) | async-done | bytes 18874384
  702.3 222.5 %all-reduce.22.cloned.1.call-done = f32[2,768,3072]{2,0,1:T(2,128)} async-done(((f32[2,768,3072]{2,0,1:T(2,128)}), f32[2,768,3072]{2,0,1:T(2,128)}) %all-reduce.22.cloned.1.call-update) | async-done | bytes 18874384
  924.8 1.6 constant_dynamic-slice_fusion.3
  926.4 239.3 %reduce-scatter.10.cloned.1.call-done = f32[2,24,768]{2,1,0:T(8,128)} async-done(((f32[2,3072,768]{2,1,0:T(8,128)}), f32[2,24,768]{2,1,0:T(8,128)}) %reduce-scatter.10.cloned.1.call-update) | async-done | bytes 147472 | tf_op jit(solution)/shard_map/reduce_scatter | solution.py:392
  (482 shorter events, 74.5 us)
Async XLA Ops:
  7.2 107.6 %copy-start = (s32[128]{0:T(128)S(1)}, s32[128]{0:T(128)}, u32[]{:S(2)}) copy-start(s32[128]{0:T(128)} %param.21) | copy-start | bytes 1540
  7.2 249.6 %all-reduce.20.cloned.1.call-start = ((), (), s32[]{:S(2)}) async-start(), calls=%async_computation.2 | async-start | bytes 393216
  7.9 8.9 copy-start.142
  9.9 12.3 %copy-start.89 = (f32[768]{0:T(1024)}, f32[768]{0:T(1024)S(1)}, u32[]{:S(2)}) copy-start(f32[768]{0:T(1024)S(1)} %get-tuple-element.282) | copy-start | bytes 9220
  10.6 13.1 %copy-start.64 = (f32[768]{0:T(1024)}, f32[768]{0:T(1024)S(1)}, u32[]{:S(2)}) copy-start(f32[768]{0:T(1024)S(1)} %get-tuple-element.276) | copy-start | bytes 9220
  10.7 46.4 %copy-start.62 = (f32[768]{0:T(1024)}, f32[768]{0:T(1024)S(1)}, u32[]{:S(2)}) copy-start(f32[768]{0:T(1024)S(1)} %get-tuple-element.275) | copy-start | bytes 9220
  12.9 10.9 copy-start.112
  12.9 26.7 %copy-start.114 = (f32[2304]{0:T(1024)}, f32[2304]{0:T(1024)S(1)}, u32[]{:S(2)}) copy-start(f32[2304]{0:T(1024)S(1)} %get-tuple-element.346) | copy-start | bytes 27652
  23.8 13.5 %copy-start.68 = (f32[768]{0:T(1024)}, f32[768]{0:T(1024)S(1)}, u32[]{:S(2)}) copy-start(f32[768]{0:T(1024)S(1)} %get-tuple-element.393) | copy-start | bytes 9220
  23.8 13.6 %copy-start.129 = (f32[768]{0:T(1024)}, f32[768]{0:T(1024)S(1)}, u32[]{:S(2)}) copy-start(f32[768]{0:T(1024)S(1)} %get-tuple-element.280) | copy-start | bytes 9220
  23.8 33.3 %copy-start.66 = (f32[768]{0:T(1024)}, f32[768]{0:T(1024)S(1)}, u32[]{:S(2)}) copy-start(f32[768]{0:T(1024)S(1)} %get-tuple-element.394) | copy-start | bytes 9220
  23.8 13.8 %copy-start.108 = (bf16[2,768]{1,0:T(2,128)(2,1)S(1)}, bf16[2,768]{1,0:T(2,128)(2,1)}, u32[]{:S(2)}) copy-start(bf16[2,768]{1,0:T(2,128)(2,1)} %param.35) | copy-start | bytes 9220
  23.8 13.8 %copy-start.109 = (bf16[2,768]{1,0:T(2,128)(2,1)S(1)}, bf16[2,768]{1,0:T(2,128)(2,1)}, u32[]{:S(2)}) copy-start(bf16[2,768]{1,0:T(2,128)(2,1)} %param.34) | copy-start | bytes 9220
  38.3 34.9 %copy-start.70 = (f32[768]{0:T(1024)}, f32[768]{0:T(1024)S(1)}, u32[]{:S(2)}) copy-start(f32[768]{0:T(1024)S(1)} %get-tuple-element.395) | copy-start | bytes 9220
  57.1 16.0 %copy-start.72 = (f32[768]{0:T(1024)S(1)}, f32[768]{0:T(1024)}, u32[]{:S(2)}) copy-start(f32[768]{0:T(1024)} %get-tuple-element.396) | copy-start | bytes 9220
  57.1 16.0 %copy-start.79 = (f32[768]{0:T(1024)S(1)}, f32[768]{0:T(1024)}, u32[]{:S(2)}) copy-start(f32[768]{0:T(1024)} %copy-done.78) | copy-start | bytes 9220
  57.2 16.0 %copy-start.91 = (f32[768]{0:T(1024)S(1)}, f32[768]{0:T(1024)}, u32[]{:S(2)}) copy-start(f32[768]{0:T(1024)} %get-tuple-element.273) | copy-start | bytes 9220
  57.2 16.0 %copy-start.101 = (f32[256]{0:T(256)S(1)}, f32[256]{0:T(256)}, u32[]{:S(2)}) copy-start(f32[256]{0:T(256)} %copy-done.100) | copy-start | bytes 3076
  57.2 16.0 %copy-start.124 = (f32[256]{0:T(256)S(1)}, f32[256]{0:T(256)}, u32[]{:S(2)}) copy-start(f32[256]{0:T(256)} %copy-done.123) | copy-start | bytes 3076
  57.2 16.0 %copy-start.139 = (f32[256]{0:T(256)S(1)}, f32[256]{0:T(256)}, u32[]{:S(2)}) copy-start(f32[256]{0:T(256)} %fusion.422) | copy-start | bytes 3076
  71.8 43.7 %copy-start.140 = (s32[4]{0:T(128)S(1)}, s32[4]{0:T(128)}, u32[]{:S(2)}) copy-start(s32[4]{0:T(128)} %param.22) | copy-start | bytes 52
  75.1 40.6 %copy-start.75 = (f32[1,2,768]{2,1,0:T(2,128)}, f32[1,2,768]{2,1,0:T(2,128)S(1)}, u32[]{:S(2)}) copy-start(f32[1,2,768]{2,1,0:T(2,128)S(1)} %pad_maximum_fusion.16) | copy-start | bytes 18436
  115.7 38.0 %copy-start.98 = (f32[4,2,4]{0,2,1:T(4,128)}, f32[4,2,4]{0,2,1:T(4,128)S(1)}, u32[]{:S(2)}) copy-start(f32[4,2,4]{0,2,1:T(4,128)S(1)} %add_rsqrt_fusion.1) | copy-start | bytes 388
  115.7 44.5 %copy-start.55 = (f32[32,2,768]{2,0,1:T(8,128)}, f32[32,2,768]{2,0,1:T(8,128)S(1)}, u32[]{:S(2)}) copy-start(f32[32,2,768]{2,0,1:T(8,128)S(1)} %copy.123) | copy-start | bytes 589828
  115.9 44.3 %copy-start.138 = (f32[32,2,4]{0,2,1:T(4,128)}, f32[32,2,4]{0,2,1:T(4,128)S(1)}, u32[]{:S(2)}) copy-start(f32[32,2,4]{0,2,1:T(4,128)S(1)} %add_rsqrt_fusion) | copy-start | bytes 3076
  116.6 43.6 %copy-start.85 = (f32[4,32]{1,0:T(4,128)}, f32[4,32]{1,0:T(4,128)S(1)}, u32[]{:S(2)}) copy-start(f32[4,32]{1,0:T(4,128)S(1)} %get-tuple-element.348) | copy-start | bytes 1540
  116.6 43.6 %copy-start.125 = (pred[4,32]{1,0:T(4,128)(4,1)}, pred[4,32]{1,0:T(4,128)(4,1)S(1)}, u32[]{:S(2)}) copy-start(pred[4,32]{1,0:T(4,128)(4,1)S(1)} %get-tuple-element.349) | copy-start | bytes 388
  117.6 47.2 %copy-start.74 = (f32[2,4,4,32]{3,2,1,0:T(4,128)}, f32[2,4,4,32]{3,2,1,0:T(4,128)S(1)}, u32[]{:S(2)}) copy-start(f32[2,4,4,32]{3,2,1,0:T(4,128)S(1)} %get-tuple-element.363) | copy-start | bytes 12292
  117.6 42.7 %copy-start.145 = (u32[128]{0:T(128)S(1)}, u32[128]{0:T(128)}, u32[]{:S(2)}) copy-start(u32[128]{0:T(128)} %constant.220) | copy-start | bytes 1540
  117.6 43.3 %copy-start.144 = (u32[128]{0:T(128)S(1)}, u32[128]{0:T(128)}, u32[]{:S(2)}) copy-start(u32[128]{0:T(128)} %constant.216) | copy-start | bytes 1540
  117.6 43.9 %copy-start.116 = (f32[2304]{0:T(1024)S(1)}, f32[2304]{0:T(1024)}, u32[]{:S(2)}) copy-start(f32[2304]{0:T(1024)} %copy-done.115) | copy-start | bytes 27652
  154.4 10.5 copy-start.99
  158.2 314.6 %all-reduce.24.cloned.1.call-start = ((), (), s32[]{:S(2)}) async-start(), calls=%async_computation.4 | async-start | bytes 147456
  167.0 44.5 %copy-start.42 = (bf16[1,256,768]{1,2,0:T(8,128)(2,1)}, bf16[1,256,768]{1,2,0:T(8,128)(2,1)S(1)}, u32[]{:S(2)}) copy-start(bf16[1,256,768]{1,2,0:T(8,128)(2,1)S(1)} %copy.132) | copy-start | bytes 1179652
  174.2 6.9 copy-start.86
  209.9 8.6 copy-start.80
  216.0 16.0 %slice-start = ((s8[9437184]{0:T(1024)(128)(4,1)}), s8[4194304]{0:T(1024)(128)(4,1)S(1)}, s32[]{:S(2)}) async-start(s8[9437184]{0:T(1024)(128)(4,1)} %bitcast.538), calls=%async_computation.6 | async-start | bytes 8388608
  216.0 19.4 %slice-start.6 = ((s8[9437184]{0:T(1024)(128)(4,1)}), s8[4194304]{0:T(1024)(128)(4,1)S(1)}, s32[]{:S(2)}) async-start(s8[9437184]{0:T(1024)(128)(4,1)} %bitcast.542), calls=%async_computation.12 | async-start | bytes 8388608
  219.2 12.9 %copy-start.7 = (f32[1,256,768]{2,1,0:T(8,128)}, f32[1,256,768]{2,1,0:T(8,128)S(1)}, u32[]{:S(2)}) copy-start(f32[1,256,768]{2,1,0:T(8,128)S(1)} %get-tuple-element.377) | copy-start | bytes 2359300
  219.2 12.8 %copy-start.83 = (f32[256]{0:T(256)}, f32[256]{0:T(256)S(1)}, u32[]{:S(2)}) copy-start(f32[256]{0:T(256)S(1)} %broadcast_multiply_fusion.11) | copy-start | bytes 3076
  220.5 11.6 copy-start.104
  220.5 11.6 copy-start.130
  220.5 11.6 slice-start.1
  220.5 11.6 slice-start.2
  220.5 14.9 %slice-start.7 = ((s8[9437184]{0:T(1024)(128)(4,1)}), s8[4194304]{0:T(1024)(128)(4,1)S(1)}, s32[]{:S(2)}) async-start(s8[9437184]{0:T(1024)(128)(4,1)} %bitcast.542), calls=%async_computation.13 | async-start | bytes 8388608
  220.5 14.9 %slice-start.8 = ((s8[9437184]{0:T(1024)(128)(4,1)}), s8[1048576]{0:T(1024)(128)(4,1)S(1)}, s32[]{:S(2)}) async-start(s8[9437184]{0:T(1024)(128)(4,1)} %bitcast.542), calls=%async_computation.14 | async-start | bytes 2097152
  233.7 12.0 %copy-start.119 = (f32[256]{0:T(256)}, f32[256]{0:T(256)S(1)}, u32[]{:S(2)}) copy-start(f32[256]{0:T(256)S(1)} %broadcast_multiply_fusion.10) | copy-start | bytes 3076
  235.5 10.3 copy-start.128
  245.7 13.7 %copy-start.73 = (f32[768]{0:T(1024)S(1)}, f32[768]{0:T(1024)}, u32[]{:S(2)}) copy-start(f32[768]{0:T(1024)} %get-tuple-element.396) | copy-start | bytes 9220
  248.4 22.4 %copy-start.121 = (f32[256]{0:T(256)}, f32[256]{0:T(256)S(1)}, u32[]{:S(2)}) copy-start(f32[256]{0:T(256)S(1)} %fusion.421) | copy-start | bytes 3076
  263.7 7.1 copy-start.36
  263.7 7.1 copy-start.5
  263.7 7.1 copy-start.17
  284.8 8.6 slice-start.3
  285.8 7.5 slice-start.4
  287.8 10.9 slice-start.9
  287.8 10.9 slice-start.10
  307.7 12.9 %copy-start.38 = (bf16[12,64,256]{2,1,0:T(8,128)(2,1)}, bf16[12,64,256]{2,1,0:T(8,128)(2,1)S(1)}, u32[]{:S(2)}) copy-start(bf16[12,64,256]{2,1,0:T(8,128)(2,1)S(1)} %convolution_convert_fusion) | copy-start | bytes 1179652
  310.6 10.0 copy-start.20
  324.7 11.4 copy-start.10
  335.8 363.5 %all-reduce.26.cloned.1.call-start = ((), (), s32[]{:S(2)}) async-start(), calls=%async_computation.5 | async-start | bytes 37748736
  365.7 559.0 %all-reduce.22.cloned.1.call-start = ((), (), s32[]{:S(2)}) async-start(), calls=%async_computation.3 | async-start | bytes 37748736
  417.7 747.9 %reduce-scatter.10.cloned.1.call-start = ((), (), s32[]{:S(2)}) async-start(), calls=%async_computation.1 | async-start | bytes 19021824 | tf_op jit(solution)/shard_map/reduce_scatter | solution.py:392
  430.2 735.4 %copy-start.1 = (s32[128]{0:T(128)S(1)}, s32[128]{0:T(128)}, u32[]{:S(2)}) copy-start(s32[128]{0:T(128)} %param.21) | copy-start | bytes 1540
  (100 other events, 278.2 us)
Sparse Core Ops, SparseCore 0:
  158.3 98.4 all-reduce.19
  335.9 136.8 all-reduce.23
  478.5 220.8 all-reduce.25
  705.4 219.3 all-reduce.21
  930.5 235.1 reduce-scatter.9
where the time goes:
time: 1180 us; the launch traced here: 1170 us
  waiting for transfers between devices  724 us (61%)
  matrix products  161 us (14%)
  local copies, waits for them, and re-layouts  115 us (10%)
  blocking collectives  92.6 us (8%)
  other arithmetic  61.7 us (5%)
  between operations  17.5 us (1%)
    unnamed x9, waiting for transfers between devices  485 us
    reduce_scatter x1, waiting for transfers between devices, body(): lax.psum_scatter(stacked[8], ('batch', 'tile'), scatter_dimension=1, tile...  239 us
    another operation x17, local copies, waits for them, and re-layouts, body(): stacked = [jnp.stack([gf, gb]) for gf, gb in zip(grads_front, grads_behind)]  64.5 us
    all_gather x3, blocking collectives, combined_all(): gathered = jax.tree.map(lambda a: lax.all_gather(a, axis), part)  35.9 us
    dot_general x4, matrix products, layer_forward(): jnp.einsum('pcx,xj->pcj', activation_reduced, shrink_layer_matrix, prefer...  31.1 us
    another operation x12, other arithmetic, body(): stacked = [jnp.stack([gf, gb]) for gf, gb in zip(grads_front, grads_behind)]  30.3 us
    unnamed x331, local copies, waits for them, and re-layouts  27.3 us
    all_gather x1, blocking collectives, pairing_cost_term(): cols = lax.all_gather(averaged_layer_states, 'batch', axis=0, tiled=True)  26 us
  transfers between devices with their start and end apart: 5, of which 5 were waited for; matrix products, arithmetic and copies ran while one was open for 15% of the time, Pallas kernels for 0%

commit v1 on v0

--- a/solution.py
+++ b/solution.py
@@ -2,7 +2,11 @@
 
 import jax
 import jax.numpy as jnp
+import ml_dtypes
+import numpy as np
 from jax import lax
+from jax.experimental import pallas as pl
+from jax.experimental.pallas import tpu as pltpu
 from jax.sharding import PartitionSpec as P
 
 HEADS = 12
@@ -10,6 +14,319 @@
 
 eps_norm = 1e-06
 exact_arithmetic_mode = lax.Precision.HIGHEST
+
+
+f32, bf16 = jnp.float32, jnp.bfloat16
+MESH = pl.DeviceIdType.MESH
+TRIPLES = 12
+SLOTS = 3
+ORDERS = (("x", "y", "z"), ("y", "z", "x"), ("z", "x", "y"))
+
+
+def my_place():
+    b = lax.axis_index("batch")
+    return {"z": b // 8, "x": lax.rem(b // 2, 4), "c": lax.rem(b, 2), "y": lax.axis_index("tile")}
+
+
+def device_at(place):
+    return {"batch": (place["z"] * 4 + place["x"]) * 2 + place["c"], "tile": place["y"]}
+
+
+def neighbour(place, axis, step):
+    there = dict(place)
+    if axis == "c":
+        there["c"] = 1 - place["c"]
+    else:
+        there[axis] = lax.rem(place[axis] + step + 4, 4)
+    return device_at(there)
+
+
+def reduce_kernel(
+    act_t_ref, a_ref, perm_ref, bd_ref, bu_ref, bq_ref, bo_ref, out_ref,
+    apt, half, send, got0, got1a, got1b, half2, got2a, got2b, half3, got3a, got3b, rows24,
+    sems_s, sems_r, sem0_s, sem0_r,
+):
+    place = my_place()
+    core = place["c"]
+    barrier = pltpu.get_barrier_semaphore()
+    for axis, step in (("c", 1), ("x", 1), ("x", -1), ("y", 1), ("y", -1), ("z", 1), ("z", -1)):
+        pl.semaphore_signal(barrier, inc=1, device_id=neighbour(place, axis, step), device_id_type=MESH)
+    pl.semaphore_wait(barrier, 7)
+    half3[...] = jnp.zeros_like(half3)
+
+    def exchange(o, k, slot, src_up, src_down, got):
+        axis = ORDERS[o][k // 2]
+        return [
+            pltpu.make_async_remote_copy(
+                src_ref=src, dst_ref=got.at[o, slot, way],
+                send_sem=sems_s.at[o, k, way, slot], recv_sem=sems_r.at[o, k, way, slot],
+                device_id=neighbour(place, axis, step), device_id_type=MESH,
+            )
+            for way, (src, step) in enumerate(((src_up, 1), (src_down, -1)))
+        ]
+
+    def spots(o, phase):
+        a = place[ORDERS[o][phase]]
+        return a, lax.rem(a + 1, 4), lax.rem(a + 2, 4), lax.rem(a + 3, 4)
+
+    def copy0(o, u):
+        slot = lax.rem(u, 2)
+        return pltpu.make_async_remote_copy(
+            src_ref=send.at[o], dst_ref=got0.at[o, slot], send_sem=sem0_s.at[o], recv_sem=sem0_r.at[o, slot],
+            device_id=neighbour(place, "c", 1), device_id_type=MESH,
+        )
+
+    def step_a(o, phase, u):
+        slot = lax.rem(u, SLOTS)
+        a, up, far, down = spots(o, phase)
+        if phase == 0:
+            src, got = (half.at[o, slot, pl.ds(far * 4, 2)], half.at[o, slot, pl.ds(far * 4 + 2, 2)]), got1a
+        elif phase == 1:
+            src, got = (half2.at[o, slot, far, pl.ds(0, 6)], half2.at[o, slot, far, pl.ds(6, 6)]), got2a
+        else:
+            src, got = (half3.at[o, slot, far, pl.ds(0, 2)], half3.at[o, slot, far, pl.ds(2, 2)]), got3a
+        return exchange(o, 2 * phase, slot, src[0], src[1], got)
+
+    def step_b(o, phase, u):
+        slot = lax.rem(u, SLOTS)
+        a, up, far, down = spots(o, phase)
+        if phase == 0:
+            src, got = (half.at[o, slot, pl.ds(up * 4, 4)], half.at[o, slot, pl.ds(down * 4, 4)]), got1b
+        elif phase == 1:
+            src, got = (half2.at[o, slot, up], half2.at[o, slot, down]), got2b
+        else:
+            src, got = (half3.at[o, slot, up], half3.at[o, slot, down]), got3b
+        return exchange(o, 2 * phase + 1, slot, src[0], src[1], got)
+
+    def add_a(o, phase, u):
+        slot = lax.rem(u, SLOTS)
+        a, up, far, down = spots(o, phase)
+        if phase == 0:
+            for i in range(2):
+                half[o, slot, up * 4 + i] += got1a[o, slot, 0, i]
+                half[o, slot, down * 4 + 2 + i] += got1a[o, slot, 1, i]
+        elif phase == 1:
+            half2[o, slot, up, 0:6] += got2a[o, slot, 0]
+            half2[o, slot, down, 6:12] += got2a[o, slot, 1]
+        else:
+            half3[o, slot, up, 0:2] += got3a[o, slot, 0]
+            half3[o, slot, down, 2:4] += got3a[o, slot, 1]
+
+    def add_b(o, phase, u):
+        slot = lax.rem(u, SLOTS)
+        a, up, far, down = spots(o, phase)
+        if phase == 0:
+            for i in range(4):
+                half2[o, slot, i] = half[o, slot, a * 4 + i] + got1b[o, slot, 0, i] + got1b[o, slot, 1, i]
+        elif phase == 1:
+            total = half2[o, slot, a] + got2b[o, slot, 0] + got2b[o, slot, 1]
+
+            @pl.when(lax.rem(u, 6) < 2)
+            def _():
+                for k in range(4):
+                    half3[o, slot, k, 0:3] = total[3 * k : 3 * k + 3]
+
+            @pl.when(lax.rem(u, 6) >= 2)
+            def _():
+                for ct in range(4):
+                    rows24[o, ct] = total[3 * ct : 3 * ct + 3].reshape(24, 128)
+                for k in range(4):
+                    for ct in range(4):
+                        half3[o, slot, k, ct, 0:6, :] = rows24[o, ct, 6 * k : 6 * k + 6, :]
+        else:
+            out_ref[u, o] = half3[o, slot, a] + got3b[o, slot, 0] + got3b[o, slot, 1]
+
+    def store_rows(o, slot, mine, blocks, tile0, value):
+        n, m = value.shape[0] // 24, value.shape[1] // 128
+        for j in range(m):
+            part = value[:, 128 * j : 128 * (j + 1)].reshape(n, 3, 8, 128)
+            where = pl.ds(blocks, n)
+            if mine:
+                half[o, slot, where, tile0 + 3 * j : tile0 + 3 * j + 3] = part
+            else:
+                send[o, where, tile0 + 3 * j : tile0 + 3 * j + 3] = part
+
+    def product(o, slot, which, ref, layer, at, width, tile0):
+        for mine in (True, False):
+            c = core if mine else 1 - core
+
+            def rows(i, _):
+                lhs = apt[o, which, pl.ds(pl.multiple_of(c * 384 + i * 96, 32), 96), :]
+                for w in range(0, width, 256):
+                    value = jnp.dot(lhs, ref[layer, :, at + w : at + w + 256], preferred_element_type=f32)
+                    store_rows(o, slot, mine, i * 4, tile0 + 3 * (w // 128), value)
+                return 0
+
+            lax.fori_loop(0, 4, rows, 0)
+
+    def produce(u):
+        slot = lax.rem(u, SLOTS)
+        layer = 1 - u // 6
+        kind = lax.rem(u, 6)
+
+        @pl.when(kind == 0)
+        def _():
+            for which in range(3):
+                a = a_ref[layer, which]
+                for o in range(3):
+                    apt[o, which] = lax.dot_general(
+                        perm_ref[o], a, (((1,), (1,)), ((), ())), preferred_element_type=f32
+                    ).astype(bf16)
+
+        for k in range(2):
+            @pl.when(kind == k)
+            def _():
+                def block(zx, _):
+                    z, x = zx // 4, lax.rem(zx, 4)
+                    for mine in (True, False):
+                        c = core if mine else 1 - core
+                        lhs = act_t_ref[layer, pl.ds(pl.multiple_of(zx * 192 + c * 96, 32), 96), :]
+                        value = jnp.dot(
+                            lhs, bd_ref[layer, :, 384 * k : 384 * (k + 1)], preferred_element_type=f32
+                        )
+                        for y in range(4):
+                            for j in range(3):
+                                p = {"x": x, "y": y, "z": z}
+                                d1, d2, d3 = (p[axis] for axis in ORDERS[j])
+                                row = (y * 3 + j) * 8
+                                for ct in range(3):
+                                    tile = value[row : row + 8, 128 * ct : 128 * ct + 128]
+                                    if mine:
+                                        half[j, slot, d1 * 4 + d2, d3 * 3 + ct] = tile
+                                    else:
+                                        send[j, d1 * 4 + d2, d3 * 3 + ct] = tile
+                    return 0
+
+                lax.fori_loop(0, 16, block, 0)
+
+        for k in range(2):
+            @pl.when(kind == 2 + k)
+            def _():
+                for o in range(3):
+                    product(o, slot, 2, bu_ref, layer, (k * 3 + o) * 512, 512, 0)
+
+        @pl.when(kind == 4)
+        def _():
+            for o in range(3):
+                product(o, slot, 0, bq_ref, layer, o * 768, 512, 0)
+
+        @pl.when(kind == 5)
+        def _():
+            for o in range(3):
+                product(o, slot, 0, bq_ref, layer, o * 768 + 512, 256, 0)
+                product(o, slot, 1, bo_ref, layer, o * 256, 256, 6)
+
+    def when(u, job):
+        @pl.when((u >= 0) & (u < TRIPLES))
+        def _():
+            job(u)
+
+    def tick(now, _):
+        t = now - 3
+
+        def enter(u):
+            slot = lax.rem(u, SLOTS)
+            for o in range(3):
+                copy0(o, u).wait()
+
+                def add(i, _):
+                    half[o, slot, i] += got0[o, lax.rem(u, 2), i]
+                    return 0
+
+                lax.fori_loop(0, 16, add, 0)
+                for copy in step_a(o, 0, u):
+                    copy.start()
+
+        when(t + 2, enter)
+
+        def second(phase):
+            def job(u):
+                for o in range(3):
+                    for copy in step_a(o, phase, u):
+                        copy.wait()
+                    add_a(o, phase, u)
+                    for copy in step_b(o, phase, u):
+                        copy.start()
+            return job
+
+        def third(phase):
+            def job(u):
+                for o in range(3):
+                    for copy in step_b(o, phase, u):
+                        copy.wait()
+                    add_b(o, phase, u)
+                    if phase < 2:
+                        for copy in step_a(o, phase + 1, u):
+                            copy.start()
+            return job
+
+        when(t + 1, second(0))
+        when(t, third(0))
+        when(t - 1, second(1))
+        when(t - 2, third(1))
+        when(t - 3, second(2))
+        when(t - 4, third(2))
+
+        def make(u):
+            produce(u)
+            for o in range(3):
+                copy0(o, u).start()
+
+        when(t + 3, make)
+        return 0
+
+    lax.fori_loop(0, TRIPLES + 7, tick, 0)
+
+
+def permutations():
+    rows = np.arange(768).reshape(4, 4, 2, 4, 6)
+    names = {"z": 0, "x": 1, "c": 2, "y": 3}
+    out = np.zeros((3, 768, 768), np.float32)
+    for o, (d1, d2, d3) in enumerate(ORDERS):
+        taken = rows.transpose(2, names[d1], names[d2], names[d3], 4).reshape(-1)
+        out[o, np.arange(768), taken] = 1
+    return out.astype(ml_dtypes.bfloat16)
+
+
+def reduce_gradients(active_t, operands, d_outer, d_inner, d_qkv, d_att):
+    tile = (8, 128)
+    vmem = pl.BlockSpec(memory_space=pltpu.VMEM)
+    out = pl.pallas_call(
+        reduce_kernel,
+        out_shape=jax.ShapeDtypeStruct((TRIPLES, 3, 4) + tile, f32),
+        in_specs=[vmem] * 7,
+        out_specs=vmem,
+        scratch_shapes=[
+            pltpu.VMEM((3, 3, 768, 256), bf16),
+            pltpu.VMEM((3, SLOTS, 16, 12) + tile, f32),
+            pltpu.VMEM((3, 16, 12) + tile, f32),
+            pltpu.VMEM((3, 2, 16, 12) + tile, f32),
+            pltpu.VMEM((3, SLOTS, 2, 2, 12) + tile, f32),
+            pltpu.VMEM((3, SLOTS, 2, 4, 12) + tile, f32),
+            pltpu.VMEM((3, SLOTS, 4, 12) + tile, f32),
+            pltpu.VMEM((3, SLOTS, 2, 6) + tile, f32),
+            pltpu.VMEM((3, SLOTS, 2, 12) + tile, f32),
+            pltpu.VMEM((3, SLOTS, 4, 4) + tile, f32),
+            pltpu.VMEM((3, SLOTS, 2, 2) + tile, f32),
+            pltpu.VMEM((3, SLOTS, 2, 4) + tile, f32),
+            pltpu.VMEM((3, 4, 24, 128), f32),
+            pltpu.SemaphoreType.DMA((3, 6, 2, SLOTS)),
+            pltpu.SemaphoreType.DMA((3, 6, 2, SLOTS)),
+            pltpu.SemaphoreType.DMA((3,)),
+            pltpu.SemaphoreType.DMA((3, 2)),
+        ],
+        compiler_params=pltpu.CompilerParams(
+            collective_id=1, has_side_effects=True, vmem_limit_bytes=60 * 1024 * 1024
+        ),
+    )(active_t, operands, jnp.asarray(permutations()), d_outer, d_inner, d_qkv, d_att)
+    out = out.reshape(2, 6, 3, 4, 8, 128)[::-1]
+    down = out[:, 0:2, :, 0:3].transpose(0, 2, 4, 1, 3, 5).reshape(2, 24, 768)
+    up = out[:, 2:4, :, :, 0:6].transpose(0, 4, 1, 2, 3, 5).reshape(2, 6, 3072)
+    first = out[:, 4, :, :, 0:6].transpose(0, 3, 1, 2, 4)
+    last = out[:, 5, :, :, 0:6].transpose(0, 3, 1, 2, 4)
+    qkv = jnp.concatenate([first, last[:, :, :, 0:2]], axis=3).reshape(2, 6, 2304)
+    mixer = last[:, :, :, 2:4].reshape(2, 6, 768)
+    return qkv, mixer, up, down
 
 
 def combined_all(part, axis, combine):
@@ -163,18 +480,12 @@
     )
     outer_gradient = dsum_two.astype(jnp.bfloat16)
     grad_downbias = jnp.sum(outer_gradient.astype(jnp.float32), axis=(0, 1))
-    grad_downproj = jnp.einsum(
-        "eqo,eqk->ok", activation_reduced, outer_gradient, preferred_element_type=jnp.float32
-    )
     activation_gradient = jnp.einsum(
         "cov,gv->cog", outer_gradient, shrink_layer_matrix, preferred_element_type=jnp.float32
     )
     unused, gelu_pull = jax.vjp(partial(jax.nn.gelu, approximate=False), inner)
     inner_gradient = gelu_pull(activation_gradient)[0].astype(jnp.bfloat16)
     grad_ffnbias = jnp.sum(inner_gradient.astype(jnp.float32), axis=(0, 1))
-    feedforward_input_gradient = jnp.einsum(
-        "uik,uie->ke", middle_reduced, inner_gradient, preferred_element_type=jnp.float32
-    )
     dmiddle = dsum_two + jnp.einsum(
         "qec,pc->qep", inner_gradient, expand_layer_matrix, preferred_element_type=jnp.float32
     )
@@ -183,9 +494,6 @@
     )
     attention_gradient = dsum_one.astype(jnp.bfloat16)
     grad_outbias = jnp.sum(attention_gradient.astype(jnp.float32), axis=(0, 1))
-    grad_outproj = jnp.einsum(
-        "rkv,rkb->vb", context_reduced, attention_gradient, preferred_element_type=jnp.float32
-    )
     context_gradient = jnp.einsum(
         "cqu,wu->cqw",
         attention_gradient,
@@ -221,27 +529,28 @@
     mixed_gradient = mixed_gradient.astype(jnp.bfloat16)
     bias_sums = jnp.sum(mixed_gradient.astype(jnp.float32), axis=(0, 1))
     grad_qvbias = jnp.concatenate([bias_sums[:width], bias_sums[2 * width :]])
-    query_key_value_gradient = jnp.einsum(
-        "uaz,uan->zn", hidden_reduced, mixed_gradient, preferred_element_type=jnp.float32
-    )
     dhidden = dsum_one + jnp.einsum(
         "inu,tu->int", mixed_gradient, triple_projection_matrix, preferred_element_type=jnp.float32
     )
     grads = (
-        query_key_value_gradient,
         grad_qvbias,
-        grad_outproj,
         grad_outbias,
         grad_attgain,
         grad_attshift,
-        feedforward_input_gradient,
         grad_ffnbias,
-        grad_downproj,
         grad_downbias,
         grad_fingain,
         grad_finshift,
     )
-    return (dhidden, grads)
+    products = (
+        activation_reduced[0].T,
+        jnp.stack([hidden_reduced[0], context_reduced[0], middle_reduced[0]]),
+        outer_gradient[0],
+        inner_gradient[0],
+        mixed_gradient[0],
+        attention_gradient[0],
+    )
+    return (dhidden, grads, products)
 
 
 def pairing_cost_term(
@@ -372,44 +681,34 @@
         averaged_layer_states, positive_companion, leading_dimension_counts, affinity_divisor
     )
     spread = valid[:, :, None] / counts[:, :, None]
-    saved_behind = layer_forward(lax.optimization_barrier(front), second, keymask)[1]
-    dfront, grads_behind = layer_backward(
+    dfront, grads_behind, products_behind = layer_backward(
         spread * embedding_gradient[:, 1][:, None, :], saved_behind, second
     )
     dfront = dfront + spread * embedding_gradient[:, 0][:, None, :]
-    saved_front = layer_forward(lax.optimization_barrier(inputs), first, keymask)[1]
-    dinputs, grads_front = layer_backward(dfront, saved_front, first)
+    dinputs, grads_front, products_front = layer_backward(dfront, saved_front, first)
     stacked = [jnp.stack([gf, gb]) for gf, gb in zip(grads_front, grads_behind)]
-    reduced = (
-        lax.psum_scatter(stacked[0], ("batch", "tile"), scatter_dimension=1, tiled=True),
-        lax.psum_scatter(stacked[1], ("batch", "tile"), scatter_dimension=1, tiled=True),
-        lax.psum_scatter(stacked[2], ("batch", "tile"), scatter_dimension=1, tiled=True),
-        lax.psum_scatter(stacked[3], ("batch", "tile"), scatter_dimension=1, tiled=True),
-        lax.psum_scatter(stacked[4], ("batch", "tile"), scatter_dimension=1, tiled=True),
-        lax.psum_scatter(stacked[5], ("batch", "tile"), scatter_dimension=1, tiled=True),
-        lax.psum_scatter(stacked[6], ("batch", "tile"), scatter_dimension=1, tiled=True),
-        lax.psum_scatter(stacked[7], ("batch", "tile"), scatter_dimension=1, tiled=True),
-        lax.psum_scatter(stacked[8], ("batch", "tile"), scatter_dimension=1, tiled=True),
-        lax.psum_scatter(stacked[9], ("batch", "tile"), scatter_dimension=1, tiled=True),
-        lax.psum_scatter(stacked[10], ("batch", "tile"), scatter_dimension=1, tiled=True),
-        lax.psum_scatter(stacked[11], ("batch", "tile"), scatter_dimension=1, tiled=True),
+    qvbias, outbias, attgain, attshift, ffnbias, downbias, fingain, finshift = (
+        lax.psum_scatter(s, ("batch", "tile"), scatter_dimension=1, tiled=True) for s in stacked
+    )
+    qkv, mixer, up, down = reduce_gradients(
+        *(jnp.stack([pf, pb]) for pf, pb in zip(products_front, products_behind))
     )
     return (
         row_losses,
         averaged_layer_states,
         dinputs,
-        reduced[0],
-        reduced[1],
-        reduced[2],
-        reduced[3],
-        reduced[4],
-        reduced[5],
-        reduced[6],
-        reduced[7],
-        reduced[8],
-        reduced[9],
-        reduced[10],
-        reduced[11],
+        qkv,
+        qvbias,
+        mixer,
+        outbias,
+        attgain,
+        attshift,
+        up,
+        ffnbias,
+        down,
+        downbias,
+        fingain,
+        finshift,
     )
 
 

time: 1180 us -> 651 us (0.55)
  waiting for transfers between devices: 724 us -> 170 us
  Pallas kernels: 0 us -> 165 us
  matrix products: 161 us -> 81.1 us
  local copies, waits for them, and re-layouts: 115 us -> 44.6 us
    unnamed x9 -> x4, waiting for transfers between devices: 485 us -> 170 us
    reduce_scatter x1 -> x0, waiting for transfers between devices: 239 us -> none  [body(): lax.psum_scatter(stacked[8], ('batch', 'tile'), scatter_dimension=1, tile...]
    pallas_call x0 -> x1, Pallas kernels: none -> 165 us  [reduce_gradients(): pl.pallas_call(reduce_kernel, out_shape=jax.ShapeDtypeStruct((TRIPLES, 3,...]
    another operation x17 -> x14, local copies, waits for them, and re-layouts: 64.5 us -> 0.06 us  [body(): stacked = [jnp.stack([gf, gb]) for gf, gb in zip(grads_front, grads_behind)]]
    another operation x0 -> x10, other arithmetic: none -> 33.7 us  [body(): jnp.stack([pf, pb])]
    dot_general x4 -> x2, matrix products: 31.1 us -> 3.13 us  [layer_forward(): jnp.einsum('pcx,xj->pcj', activation_reduced, shrink_layer_matrix, prefer...]
    another operation x12 -> x8, other arithmetic: 30.3 us -> 4.83 us  [body(): stacked = [jnp.stack([gf, gb]) for gf, gb in zip(grads_front, grads_behind)]]
    dot_general x8 -> x0, matrix products: 24.4 us -> none  [the longest x2 8.29 us: layer_backward(): jnp.einsum('uik,uie->ke', middle_reduced, inner_gradient, preferred_eleme...]
  transfers between devices with their start and end apart: 5 -> 2, of which waited for: 5 -> 2; matrix products, arithmetic and copies ran while one was open for 15% -> 7% of each run, Pallas kernels for 0% -> 0%
where the time goes in v1:
time: 651 us; the launch traced here: 643 us
  waiting for transfers between devices  170 us (26%)
  Pallas kernels  165 us (25%)
  blocking collectives  95.6 us (15%)
  matrix products  81.1 us (12%)
  other arithmetic  68.2 us (10%)
  local copies, waits for them, and re-layouts  44.6 us (7%)
  between operations  17.7 us (3%)
    unnamed x4, waiting for transfers between devices  170 us
    pallas_call x1, Pallas kernels, reduce_gradients(): pl.pallas_call(reduce_kernel, out_shape=jax.ShapeDtypeStruct((TRIPLES, 3,...  165 us
    all_gather x3, blocking collectives, combined_all(): gathered = jax.tree.map(lambda a: lax.all_gather(a, axis), part)  35.8 us
    another operation x10, other arithmetic, body(): jnp.stack([pf, pb])  33.7 us
    all_gather x1, blocking collectives, pairing_cost_term(): cols = lax.all_gather(averaged_layer_states, 'batch', axis=0, tiled=True)  28.5 us
    unnamed x300, local copies, waits for them, and re-layouts  20.9 us
    dot_general x2, matrix products, layer_forward(): jnp.einsum('ncm,mj->ncj', middle_reduced, expand_layer_matrix, preferred_...  19.4 us
    unnamed x1, blocking collectives  18.3 us
  transfers between devices with their start and end apart: 2, of which 2 were waited for; matrix products, arithmetic and copies ran while one was open for 7% of the time, Pallas kernels for 0%

profile of v1, /device:TPU:0, one launch (start us, length us, event | category | flops | bytes accessed | tf_op | source)
XLA Modules:
  0.0 642.5 jit_solution(8552393917026556444)
XLA Ops:
  8.5 1.4 convert_reduce_fusion.10
  9.8 1.4 slice_convert_fusion
  11.2 1.4 convert_reduce_fusion.13
  13.5 3.2 fusion.39
  17.3 2.8 fusion.267
  20.2 2.5 convolution_convert_fusion.5
  24.7 10.0 %fusion.46 = (f32[256,3072]{1,0:T(8,128)S(1)}, f32[256,3072]{1,0:T(8,128)S(1)}) fusion(f32[3072]{0:T(1024)S(1)} %bitcast.524, bf16[2,768,3072]{2,1,0:T(8,128)(2,1)} %param.31, bf16[1,256,768]{2,1,0:T(8,128)(2,1)S(1)} %fusion.208), kind=kOutput, calls=%fused_computation.53 | convolution fusion | flops 1257504768 | bytes 11415552 | tf_op jit(solution)/shard_map/ncm,mj->ncj/dot_general | solution.py:414
  34.8 1.6 fusion.269
  36.4 1.1 copy-done.7
  39.0 1.1 fusion.38
  41.5 4.3 fusion.270
  45.9 2.5 convolution_convert_fusion.4
  49.7 9.4 %fusion.47 = (f32[256,3072]{1,0:T(8,128)S(1)}, f32[256,3072]{1,0:T(8,128)S(1)}) fusion(f32[3072]{0:T(1024)S(1)} %bitcast.523, bf16[2,768,3072]{2,1,0:T(8,128)(2,1)} %param.31, bf16[1,256,768]{2,1,0:T(8,128)(2,1)S(1)} %fusion.209), kind=kOutput, calls=%fused_computation.54 | convolution fusion | flops 1257504768 | bytes 11415552 | tf_op jit(solution)/shard_map/ncm,mj->ncj/dot_general | solution.py:414
  59.2 1.6 fusion.272
  62.6 28.5 %all_gather.25 = f32[32,2,768]{2,1,0:T(2,128)} all-gather(f32[1,2,768]{2,1,0:T(2,128)S(1)} %pad_maximum_fusion.12), channel_id=1, replica_groups=mesh['batch'=32,'tile'=4] {'batch'}, dimensions={0}, use_global_device_ids=true | all-gather | bytes 202752 | tf_op jit(solution)/shard_map/all_gather | solution.py:565
  91.1 13.0 %all_gather.24 = f32[4,2,768]{2,1,0:T(2,128)} all-gather(f32[1,2,768]{2,1,0:T(2,128)S(1)} %pad_maximum_fusion.12), channel_id=1, replica_groups=mesh['batch'=32,'tile'=4] {'tile'}, dimensions={0}, use_global_device_ids=true | all-gather | bytes 30720 | tf_op jit(solution)/shard_map/all_gather | solution.py:564
  105.2 1.3 gather_fusion
  112.2 11.9 %all-gather = f32[8,4,4]{2,1,0:T(4,128)S(1)} all-gather(f32[2,4,4]{2,1,0:T(4,128)S(1)} %get-tuple-element.330), channel_id=2, replica_groups=mesh['batch'=32,'tile'=4] {'tile'}, dimensions={0}, use_global_device_ids=true | all-gather | bytes 640 | tf_op jit(solution)/shard_map/all_gather | solution.py:333
  124.3 11.9 %all-gather.1 = f32[8,4,4]{2,1,0:T(4,128)S(1)} all-gather(f32[2,4,4]{2,1,0:T(4,128)S(1)} %get-tuple-element.232), channel_id=3, replica_groups=mesh['batch'=32,'tile'=4] {'tile'}, dimensions={0}, use_global_device_ids=true | all-gather | bytes 640 | tf_op jit(solution)/shard_map/all_gather | solution.py:333
  136.3 11.9 %all-gather.2 = f32[8,4,4]{2,1,0:T(4,128)S(1)} all-gather(f32[2,4,4]{2,1,0:T(4,128)S(1)} %get-tuple-element.231), channel_id=4, replica_groups=mesh['batch'=32,'tile'=4] {'tile'}, dimensions={0}, use_global_device_ids=true | all-gather | bytes 640 | tf_op jit(solution)/shard_map/all_gather | solution.py:333
  148.8 2.3 while.19
  152.3 1.7 convolution_bitcast_fusion
  154.0 2.4 fusion.273
  157.3 8.7 %fusion.108 = bf16[1,3072,256]{1,2,0:T(8,128)(2,1)} fusion(f32[256,3072]{1,0:T(8,128)} %copy-done.5), kind=kLoop, calls=%fused_computation.157 | loop fusion | flops 51118080 | bytes 4718592 | tf_op jit(solution)/shard_map/stack | solution.py:694
  166.1 7.5 %fusion.109 = bf16[1,3072,256]{1,2,0:T(8,128)(2,1)} fusion(f32[256,3072]{1,0:T(8,128)S(1)} %copy-done.3), kind=kLoop, calls=%fused_computation.158 | loop fusion | flops 51118080 | bytes 4718592 | tf_op jit(solution)/shard_map/stack | solution.py:694
  175.7 18.3 %all-reduce = f32[4,2,768]{2,1,0:T(2,128)} all-reduce(f32[4,2,768]{2,1,0:T(2,128)} %copy.133), channel_id=5, replica_groups=mesh['batch'=32,'tile'=4] {'tile'}, use_global_device_ids=true, to_apply=%region_24.25.clone | all-reduce | flops 6144 | bytes 49152
  194.0 1.2 dynamic-slice.2
  195.2 1.2 dynamic-slice
  196.5 3.8 pad_maximum_fusion
  200.3 4.7 copy.151.act_t_ref
  205.0 1.9 copy.144
  206.9 2.5 maximum_bitcast_fusion.1
  209.4 1.9 copy.143
  211.3 2.5 maximum_bitcast_fusion
  213.8 3.3 pad_maximum_fusion.2.a_ref
  217.6 38.0 %all-reduce.14.cloned.1.call-done = f32[32,2,768]{2,1,0:T(2,128)} async-done(((f32[32,2,768]{2,1,0:T(2,128)}), f32[32,2,768]{2,1,0:T(2,128)}) %all-reduce.14.cloned.1.call-update) | async-done | bytes 196624
  255.6 2.0 dynamic-slice_add_fusion
  258.3 1.7 fusion.203
  260.0 1.6 convert_reduce_fusion.4
  261.6 7.1 %convert_reduce_fusion = (f32[3072]{0:T(1024)}, bf16[256,3072]{1,0:T(8,128)(2,1)S(1)}) fusion(f32[256,3072]{1,0:T(8,128)} %copy-done.10, f32[256,3072]{1,0:T(8,128)} %copy-done.5, bf16[2,3072,768]{2,1,0:T(8,128)(2,1)} %param.33, bf16[1,256,768]{2,1,0:T(8,128)(2,1)S(1)} %get-tuple-element.282), kind=kOutput, calls=%fused_computation.73 | convolution fusion | flops 1220539392 | bytes 12988416 | tf_op jit(solution)/shard_map/cov,gv->cog/dot_general | solution.py:483
  268.8 5.5 multiply_reduce_fusion.4
  274.2 1.8 convert_reduce_fusion.6
  276.7 2.7 convolution_convert_fusion.2
  283.2 2.1 multiply_reduce_fusion.3
  286.3 1.0 copy-done.8
  287.3 3.2 convert_reduce_fusion.1
  290.5 5.5 multiply_reduce_fusion.5
  296.0 1.2 convert_reduce_fusion.7
  297.9 3.4 convolution_convert_fusion
  303.8 1.0 pad_maximum_fusion.3.bd_ref
  305.7 1.2 copy.150
  308.0 1.5 maximum_maximum_fusion.bq_ref
  310.7 1.9 pad_maximum_fusion.1.bu_ref
  312.7 164.7 %shard_map.289 = f32[12,3,4,8,128]{4,3,2,1,0:T(8,128)} custom-call(bf16[2,3072,256]{2,1,0:T(8,128)(2,1)} %copy.151.act_t_ref, bf16[2,3,256,768]{3,2,1,0:T(8,128)(2,1)} %pad_maximum_fusion.2.a_ref, bf16[3,768,768]{2,1,0:T(8,128)(2,1)} %constant.206.clone.perm_ref, bf16[2,256,768]{2,1,0:T(8,128)(2,1)} %pad_maximum_fusion.3.bd_ref, ...), custom_call_target="tpu_custom_call" | custom-call | tf_op jit(solution)/shard_map/pallas_call | solution.py:294
  485.6 4.1 fusion.134
  492.6 132.4 %all-reduce.16.cloned.1.call-done = (f32[2,1536]{1,0:T(2,128)}, f32[2,768]{1,0:T(2,128)}, f32[2,768]{1,0:T(2,128)}, f32[2,768]{1,0:T(2,128)}, f32[2,3072]{1,0:T(...) async-done(((f32[2,1536]{1,0:T(2,128)}, f32[2,768]{1,0:T(2,128)}, f32[2,768]{1,0:T(2,128)}, f32[2,768]{1,0:T(2,128)}, f32[2,3072]{1,0:T(2,128)}, ...) | async-done | bytes 73744
  625.0 1.3 constant_dynamic-slice_fusion.5
  626.3 1.3 constant_dynamic-slice_fusion.4
  627.6 1.3 constant_dynamic-slice_fusion.3
  628.9 1.3 constant_dynamic-slice_fusion.1
  630.2 1.3 constant_dynamic-slice_fusion
  631.5 1.3 constant_dynamic-slice_fusion.7
  632.8 1.3 constant_dynamic-slice_fusion.6
  634.1 1.3 constant_dynamic-slice_fusion.2
  (433 shorter events, 46.6 us)
Async XLA Ops:
  7.2 98.0 %copy-start = (s32[128]{0:T(128)S(1)}, s32[128]{0:T(128)}, u32[]{:S(2)}) copy-start(s32[128]{0:T(128)} %param.22) | copy-start | bytes 1540
  7.2 248.4 %all-reduce.14.cloned.1.call-start = ((), (), s32[]{:S(2)}) async-start(), calls=%async_computation | async-start | bytes 393216
  22.7 12.0 %copy-start.43 = (bf16[12,64,256]{2,1,0:T(8,128)(2,1)}, bf16[12,64,256]{2,1,0:T(8,128)(2,1)S(1)}, u32[]{:S(2)}) copy-start(bf16[12,64,256]{2,1,0:T(8,128)(2,1)S(1)} %convolution_convert_fusion.5) | copy-start | bytes 1179652
  23.5 11.2 %copy-start.56 = (f32[256]{0:T(256)}, f32[256]{0:T(256)S(1)}, u32[]{:S(2)}) copy-start(f32[256]{0:T(256)S(1)} %broadcast_multiply_fusion.11) | copy-start | bytes 3076
  23.6 15.5 %slice-start.9 = ((s8[7077888]{0:T(1024)(128)(4,1)}), s8[4194304]{0:T(1024)(128)(4,1)S(1)}, s32[]{:S(2)}) async-start(s8[7077888]{0:T(1024)(128)(4,1)} %bitcast.525), calls=%async_computation.11 | async-start | bytes 8388608
  23.8 10.9 %copy-start.69 = (f32[256]{0:T(256)}, f32[256]{0:T(256)S(1)}, u32[]{:S(2)}) copy-start(f32[256]{0:T(256)S(1)} %add_rsqrt_fusion.5) | copy-start | bytes 3076
  24.4 34.7 %copy-start.51 = (f32[768]{0:T(1024)}, f32[768]{0:T(1024)S(1)}, u32[]{:S(2)}) copy-start(f32[768]{0:T(1024)S(1)} %get-tuple-element.348) | copy-start | bytes 9220
  24.4 10.3 %slice-start = ((s8[9437184]{0:T(1024)(128)(4,1)}), s8[4194304]{0:T(1024)(128)(4,1)S(1)}, s32[]{:S(2)}) async-start(s8[9437184]{0:T(1024)(128)(4,1)} %bitcast.474), calls=%async_computation.2 | async-start | bytes 8388608
  24.6 10.1 %copy-start.17 = (bf16[1,256,768]{2,1,0:T(8,128)(2,1)}, bf16[1,256,768]{2,1,0:T(8,128)(2,1)S(1)}, u32[]{:S(2)}) copy-start(bf16[1,256,768]{2,1,0:T(8,128)(2,1)S(1)} %fusion.208) | copy-start | bytes 1179652
  24.7 10.1 %slice-start.1 = ((s8[9437184]{0:T(1024)(128)(4,1)}), s8[4194304]{0:T(1024)(128)(4,1)S(1)}, s32[]{:S(2)}) async-start(s8[9437184]{0:T(1024)(128)(4,1)} %bitcast.474), calls=%async_computation.3 | async-start | bytes 8388608
  24.7 10.1 %slice-start.2 = ((s8[9437184]{0:T(1024)(128)(4,1)}), s8[1048576]{0:T(1024)(128)(4,1)S(1)}, s32[]{:S(2)}) async-start(s8[9437184]{0:T(1024)(128)(4,1)} %bitcast.474), calls=%async_computation.4 | async-start | bytes 2097152
  24.7 14.4 %slice-start.10 = ((s8[7077888]{0:T(1024)(128)(4,1)}), s8[2883584]{0:T(1024)(128)(4,1)S(1)}, s32[]{:S(2)}) async-start(s8[7077888]{0:T(1024)(128)(4,1)} %bitcast.525), calls=%async_computation.12 | async-start | bytes 5767168
  38.4 9.9 %copy-start.60 = (f32[768]{0:T(1024)}, f32[768]{0:T(1024)S(1)}, u32[]{:S(2)}) copy-start(f32[768]{0:T(1024)S(1)} %get-tuple-element.349) | copy-start | bytes 9220
  48.5 10.6 %slice-start.3 = ((s8[9437184]{0:T(1024)(128)(4,1)}), s8[4194304]{0:T(1024)(128)(4,1)S(1)}, s32[]{:S(2)}) async-start(s8[9437184]{0:T(1024)(128)(4,1)} %bitcast.476), calls=%async_computation.5 | async-start | bytes 8388608
  49.2 10.0 %copy-start.58 = (f32[256]{0:T(256)}, f32[256]{0:T(256)S(1)}, u32[]{:S(2)}) copy-start(f32[256]{0:T(256)S(1)} %broadcast_multiply_fusion.9) | copy-start | bytes 3076
  49.4 9.7 %copy-start.71 = (f32[256]{0:T(256)}, f32[256]{0:T(256)S(1)}, u32[]{:S(2)}) copy-start(f32[256]{0:T(256)S(1)} %add_rsqrt_fusion.3) | copy-start | bytes 3076
  49.6 9.4 %copy-start.19 = (bf16[1,256,768]{2,1,0:T(8,128)(2,1)}, bf16[1,256,768]{2,1,0:T(8,128)(2,1)S(1)}, u32[]{:S(2)}) copy-start(bf16[1,256,768]{2,1,0:T(8,128)(2,1)S(1)} %fusion.209) | copy-start | bytes 1179652
  49.7 9.5 %slice-start.4 = ((s8[9437184]{0:T(1024)(128)(4,1)}), s8[4194304]{0:T(1024)(128)(4,1)S(1)}, s32[]{:S(2)}) async-start(s8[9437184]{0:T(1024)(128)(4,1)} %bitcast.476), calls=%async_computation.6 | async-start | bytes 8388608
  49.7 9.5 %slice-start.5 = ((s8[9437184]{0:T(1024)(128)(4,1)}), s8[1048576]{0:T(1024)(128)(4,1)S(1)}, s32[]{:S(2)}) async-start(s8[9437184]{0:T(1024)(128)(4,1)} %bitcast.476), calls=%async_computation.7 | async-start | bytes 2097152
  49.7 9.5 %copy-start.73 = (f32[768]{0:T(1024)S(1)}, f32[768]{0:T(1024)}, u32[]{:S(2)}) copy-start(f32[768]{0:T(1024)} %get-tuple-element.245) | copy-start | bytes 9220
  62.5 61.8 %copy-start.68 = (f32[1,2,768]{2,1,0:T(2,128)}, f32[1,2,768]{2,1,0:T(2,128)S(1)}, u32[]{:S(2)}) copy-start(f32[1,2,768]{2,1,0:T(2,128)S(1)} %pad_maximum_fusion.12) | copy-start | bytes 18436
  108.5 27.8 %copy-start.49 = (f32[4,768]{1,0:T(4,128)}, f32[4,768]{1,0:T(4,128)S(1)}, u32[]{:S(2)}) copy-start(f32[4,768]{1,0:T(4,128)S(1)} %fusion.248) | copy-start | bytes 36868
  109.7 39.2 %copy-start.122 = (f32[32,2,4]{0,2,1:T(4,128)}, f32[32,2,4]{0,2,1:T(4,128)S(1)}, u32[]{:S(2)}) copy-start(f32[32,2,4]{0,2,1:T(4,128)S(1)} %add_rsqrt_fusion) | copy-start | bytes 3076
  110.6 38.3 %copy-start.93 = (f32[4,2,4]{0,2,1:T(4,128)}, f32[4,2,4]{0,2,1:T(4,128)S(1)}, u32[]{:S(2)}) copy-start(f32[4,2,4]{0,2,1:T(4,128)S(1)} %add_rsqrt_fusion.1) | copy-start | bytes 388
  111.3 37.5 %copy-start.82 = (f32[4,32]{1,0:T(4,128)}, f32[4,32]{1,0:T(4,128)S(1)}, u32[]{:S(2)}) copy-start(f32[4,32]{1,0:T(4,128)S(1)} %get-tuple-element.312) | copy-start | bytes 1540
  111.3 37.5 %copy-start.112 = (pred[4,32]{1,0:T(4,128)(4,1)}, pred[4,32]{1,0:T(4,128)(4,1)S(1)}, u32[]{:S(2)}) copy-start(pred[4,32]{1,0:T(4,128)(4,1)S(1)} %get-tuple-element.313) | copy-start | bytes 388
  112.2 36.6 %copy-start.66 = (f32[2,4,4,32]{3,2,1,0:T(4,128)}, f32[2,4,4,32]{3,2,1,0:T(4,128)S(1)}, u32[]{:S(2)}) copy-start(f32[2,4,4,32]{3,2,1,0:T(4,128)S(1)} %get-tuple-element.331) | copy-start | bytes 12292
  124.2 24.1 %copy-start.53 = (f32[8,4,4]{2,1,0:T(4,128)}, f32[8,4,4]{2,1,0:T(4,128)S(1)}, u32[]{:S(2)}) copy-start(f32[8,4,4]{2,1,0:T(4,128)S(1)} %all-gather) | copy-start | bytes 1540
  136.3 12.0 %copy-start.54 = (f32[8,4,4]{2,1,0:T(4,128)}, f32[8,4,4]{2,1,0:T(4,128)S(1)}, u32[]{:S(2)}) copy-start(f32[8,4,4]{2,1,0:T(4,128)S(1)} %all-gather.1) | copy-start | bytes 1540
  157.2 467.8 %all-reduce.16.cloned.1.call-start = ((), (), s32[]{:S(2)}) async-start(), calls=%async_computation.1 | async-start | bytes 147456
  157.3 8.8 %copy-start.3 = (f32[256,3072]{1,0:T(8,128)S(1)}, f32[256,3072]{1,0:T(8,128)}, u32[]{:S(2)}) copy-start(f32[256,3072]{1,0:T(8,128)} %copy-done.2) | copy-start | bytes 9437188
  166.0 7.6 %copy-start.125 = (f32[4]{0:T(128)S(1)}, f32[4]{0:T(128)}, u32[]{:S(2)}) copy-start(f32[4]{0:T(128)} %get-tuple-element.289) | copy-start | bytes 52
  166.0 8.1 %copy-start.35 = (f32[32,2,768]{2,0,1:T(8,128)S(1)}, f32[32,2,768]{2,0,1:T(8,128)}, u32[]{:S(2)}) copy-start(f32[32,2,768]{2,0,1:T(8,128)} %copy-done.34) | copy-start | bytes 589828
  166.0 8.1 %copy-start.50 = (f32[4,768]{1,0:T(4,128)S(1)}, f32[4,768]{1,0:T(4,128)}, u32[]{:S(2)}) copy-start(f32[4,768]{1,0:T(4,128)} %copy-done.49) | copy-start | bytes 36868
  166.1 8.1 %copy-start.67 = (f32[2,4,4,32]{3,2,1,0:T(4,128)S(1)}, f32[2,4,4,32]{3,2,1,0:T(4,128)}, u32[]{:S(2)}) copy-start(f32[2,4,4,32]{3,2,1,0:T(4,128)} %copy-done.66) | copy-start | bytes 12292
  166.1 8.1 %copy-start.83 = (f32[4,32]{1,0:T(4,128)S(1)}, f32[4,32]{1,0:T(4,128)}, u32[]{:S(2)}) copy-start(f32[4,32]{1,0:T(4,128)} %copy-done.82) | copy-start | bytes 1540
  166.1 8.1 %copy-start.96 = (f32[2,4,4]{2,1,0:T(4,128)S(1)}, f32[2,4,4]{2,1,0:T(4,128)}, u32[]{:S(2)}) copy-start(f32[2,4,4]{2,1,0:T(4,128)} %copy-done.95) | copy-start | bytes 388
  166.1 8.1 %copy-start.113 = (pred[4,32]{1,0:T(4,128)(4,1)S(1)}, pred[4,32]{1,0:T(4,128)(4,1)}, u32[]{:S(2)}) copy-start(pred[4,32]{1,0:T(4,128)(4,1)} %copy-done.112) | copy-start | bytes 388
  166.1 8.1 %copy-start.123 = (f32[32,2,4]{0,2,1:T(4,128)S(1)}, f32[32,2,4]{0,2,1:T(4,128)}, u32[]{:S(2)}) copy-start(f32[32,2,4]{0,2,1:T(4,128)} %copy-done.122) | copy-start | bytes 3076
  166.1 8.7 %copy-start.48 = (f32[4,2,768]{2,0,1:T(4,128)S(1)}, f32[4,2,768]{2,0,1:T(4,128)}, u32[]{:S(2)}) copy-start(f32[4,2,768]{2,0,1:T(4,128)} %copy-done.47) | copy-start | bytes 73732
  166.1 8.7 %copy-start.94 = (f32[4,2,4]{0,2,1:T(4,128)S(1)}, f32[4,2,4]{0,2,1:T(4,128)}, u32[]{:S(2)}) copy-start(f32[4,2,4]{0,2,1:T(4,128)} %copy-done.93) | copy-start | bytes 388
  211.3 47.0 %copy-start.64 = (f32[768]{0:T(1024)S(1)}, f32[768]{0:T(1024)}, u32[]{:S(2)}) copy-start(f32[768]{0:T(1024)} %get-tuple-element.350) | copy-start | bytes 9220
  211.3 47.0 %copy-start.80 = (f32[256]{0:T(256)S(1)}, f32[256]{0:T(256)}, u32[]{:S(2)}) copy-start(f32[256]{0:T(256)} %copy-done.79) | copy-start | bytes 3076
  211.3 47.0 %copy-start.101 = (f32[256]{0:T(256)S(1)}, f32[256]{0:T(256)}, u32[]{:S(2)}) copy-start(f32[256]{0:T(256)} %copy-done.100) | copy-start | bytes 3076
  261.6 7.1 %copy-start.72 = (f32[256]{0:T(256)S(1)}, f32[256]{0:T(256)}, u32[]{:S(2)}) copy-start(f32[256]{0:T(256)} %copy-done.71) | copy-start | bytes 3076
  261.6 7.1 %copy-start.81 = (f32[256]{0:T(256)S(1)}, f32[256]{0:T(256)}, u32[]{:S(2)}) copy-start(f32[256]{0:T(256)} %copy-done.79) | copy-start | bytes 3076
  261.6 7.1 %copy-start.102 = (f32[256]{0:T(256)S(1)}, f32[256]{0:T(256)}, u32[]{:S(2)}) copy-start(f32[256]{0:T(256)} %copy-done.100) | copy-start | bytes 3076
  261.6 7.1 %copy-start.110 = (f32[256]{0:T(256)S(1)}, f32[256]{0:T(256)}, u32[]{:S(2)}) copy-start(f32[256]{0:T(256)} %fusion.249) | copy-start | bytes 3076
  268.8 7.2 %copy-start.128 = (bf16[2,768,768]{2,1,0:T(8,128)(2,1)S(1)}, bf16[2,768,768]{2,1,0:T(8,128)(2,1)}, u32[]{:S(2)}) copy-start(bf16[2,768,768]{2,1,0:T(8,128)(2,1)} %param.27) | copy-start | bytes 7077892
  312.6 167.9 %copy-start.91 = (f32[768]{0:T(1024)S(1)}, f32[768]{0:T(1024)}, u32[]{:S(2)}) copy-start(f32[768]{0:T(1024)} %get-tuple-element.286) | copy-start | bytes 9220
  312.6 167.9 %copy-start.117 = (f32[768]{0:T(1024)S(1)}, f32[768]{0:T(1024)}, u32[]{:S(2)}) copy-start(f32[768]{0:T(1024)} %get-tuple-element.221) | copy-start | bytes 9220
  312.6 167.9 %copy-start.121 = (f32[768]{0:T(1024)S(1)}, f32[768]{0:T(1024)}, u32[]{:S(2)}) copy-start(f32[768]{0:T(1024)} %get-tuple-element.219) | copy-start | bytes 9220
  312.6 168.0 %copy-start.116 = (f32[768]{0:T(1024)S(1)}, f32[768]{0:T(1024)}, u32[]{:S(2)}) copy-start(f32[768]{0:T(1024)} %get-tuple-element.230) | copy-start | bytes 9220
  312.6 168.0 %copy-start.120 = (f32[768]{0:T(1024)S(1)}, f32[768]{0:T(1024)}, u32[]{:S(2)}) copy-start(f32[768]{0:T(1024)} %get-tuple-element.229) | copy-start | bytes 9220
  312.6 168.0 %copy-start.90 = (f32[768]{0:T(1024)S(1)}, f32[768]{0:T(1024)}, u32[]{:S(2)}) copy-start(f32[768]{0:T(1024)} %get-tuple-element.281) | copy-start | bytes 9220
  312.7 168.0 %copy-start.92 = (f32[768]{0:T(1024)S(1)}, f32[768]{0:T(1024)}, u32[]{:S(2)}) copy-start(f32[768]{0:T(1024)} %get-tuple-element.279) | copy-start | bytes 9220
  312.7 168.0 %copy-start.89 = (f32[768]{0:T(1024)S(1)}, f32[768]{0:T(1024)}, u32[]{:S(2)}) copy-start(f32[768]{0:T(1024)} %get-tuple-element.223) | copy-start | bytes 9220
  312.7 168.0 %copy-start.119 = (f32[768]{0:T(1024)S(1)}, f32[768]{0:T(1024)}, u32[]{:S(2)}) copy-start(f32[768]{0:T(1024)} %get-tuple-element.217) | copy-start | bytes 9220
  312.7 168.0 %copy-start.88 = (f32[768]{0:T(1024)S(1)}, f32[768]{0:T(1024)}, u32[]{:S(2)}) copy-start(f32[768]{0:T(1024)} %get-tuple-element.240) | copy-start | bytes 9220
  312.7 168.0 %copy-start.118 = (f32[768]{0:T(1024)S(1)}, f32[768]{0:T(1024)}, u32[]{:S(2)}) copy-start(f32[768]{0:T(1024)} %get-tuple-element.228) | copy-start | bytes 9220
  312.7 170.5 %copy-start.107 = (f32[3072]{0:T(1024)S(1)}, f32[3072]{0:T(1024)}, u32[]{:S(2)}) copy-start(f32[3072]{0:T(1024)} %get-tuple-element.339) | copy-start | bytes 36868
  312.7 170.5 %copy-start.108 = (f32[3072]{0:T(1024)S(1)}, f32[3072]{0:T(1024)}, u32[]{:S(2)}) copy-start(f32[3072]{0:T(1024)} %get-tuple-element.341) | copy-start | bytes 36868
  312.7 172.9 %copy-start.36 = (f32[1,256,768]{2,1,0:T(8,128)S(1)}, f32[1,256,768]{2,1,0:T(8,128)}, u32[]{:S(2)}) copy-start(f32[1,256,768]{2,1,0:T(8,128)} %get-tuple-element.285) | copy-start | bytes 2359300
  485.6 149.8 %copy-start.1 = (s32[128]{0:T(128)S(1)}, s32[128]{0:T(128)}, u32[]{:S(2)}) copy-start(s32[128]{0:T(128)} %param.22) | copy-start | bytes 1540
  (82 other events, 235.6 us)
Sparse Core Ops, SparseCore 0:
  157.3 98.2 all-reduce.13
  489.8 135.1 all-reduce.15

commit v2 on v1

--- a/solution.py
+++ b/solution.py
@@ -13,7 +13,6 @@
 
 
 eps_norm = 1e-06
-exact_arithmetic_mode = lax.Precision.HIGHEST
 
 
 f32, bf16 = jnp.float32, jnp.bfloat16
@@ -41,17 +40,32 @@
     return device_at(there)
 
 
+GROUP = tuple((flip, step) for flip in (0, 1) for step in range(4) if flip or step)
+VECTORS = tuple((768 * k, 768, 6) for k in range(6)) + ((4608, 1536, 12), (6144, 3072, 24))
+
+
+def in_group(place, flip, step):
+    there = dict(place)
+    there["c"] = lax.rem(place["c"] + flip, 2)
+    there["y"] = lax.rem(place["y"] + step, 4)
+    return device_at(there)
+
+
 def reduce_kernel(
-    act_t_ref, a_ref, perm_ref, bd_ref, bu_ref, bq_ref, bo_ref, out_ref,
+    act_t_ref, a_ref, perm_ref, bd_ref, bu_ref, bq_ref, bo_ref, vec_ref, spread_ref, out_ref, vec_out_ref,
     apt, half, send, got0, got1a, got1b, half2, got2a, got2b, half3, got3a, got3b, rows24,
-    sems_s, sems_r, sem0_s, sem0_r,
+    vec_src, vec_z, vec_x, vec_mid, vec_cy,
+    sems_s, sems_r, sem0_s, sem0_r, vec_s, vec_r,
 ):
     place = my_place()
     core = place["c"]
     barrier = pltpu.get_barrier_semaphore()
-    for axis, step in (("c", 1), ("x", 1), ("x", -1), ("y", 1), ("y", -1), ("z", 1), ("z", -1)):
-        pl.semaphore_signal(barrier, inc=1, device_id=neighbour(place, axis, step), device_id_type=MESH)
-    pl.semaphore_wait(barrier, 7)
+    for axis in ("x", "z"):
+        for step in (1, 2, 3):
+            pl.semaphore_signal(barrier, inc=1, device_id=neighbour(place, axis, step), device_id_type=MESH)
+    for flip, step in GROUP:
+        pl.semaphore_signal(barrier, inc=1, device_id=in_group(place, flip, step), device_id_type=MESH)
+    pl.semaphore_wait(barrier, 13)
     half3[...] = jnp.zeros_like(half3)
 
     def exchange(o, k, slot, src_up, src_down, got):
@@ -216,6 +230,75 @@
                 product(o, slot, 0, bq_ref, layer, o * 768 + 512, 256, 0)
                 product(o, slot, 1, bo_ref, layer, o * 256, 256, 6)
 
+    def spread_vectors():
+        for layer in range(2):
+            total = jnp.zeros((128, 128), f32)
+            for start, width, keep in VECTORS:
+                d = lax.broadcasted_iota(jnp.int32, (128, width), 0) * keep
+                q = lax.broadcasted_iota(jnp.int32, (128, width), 1)
+                own = jnp.where((q >= d) & (q < d + keep), vec_ref[layer : layer + 1, start : start + width], 0.0)
+                high = own.astype(bf16)
+                low = (own - high.astype(f32)).astype(bf16)
+                lanes = spread_ref[start : start + width, :]
+                total += jnp.dot(high, lanes, preferred_element_type=f32)
+                total += jnp.dot(low, lanes, preferred_element_type=f32)
+            total = total.reshape(4, 4, 8, 128)
+            for z in range(4):
+                for x in range(4):
+                    vec_src[z, x, layer] = total[z, x]
+
+    def vector_copy(k, src, dst, device):
+        return pltpu.make_async_remote_copy(
+            src_ref=src, dst_ref=dst, send_sem=vec_s.at[k], recv_sem=vec_r.at[k], device_id=device, device_id_type=MESH
+        )
+
+    def copies_z():
+        return [
+            vector_copy(i, vec_src.at[lax.rem(place["z"] + i + 1, 4)], vec_z.at[i], neighbour(place, "z", i + 1))
+            for i in range(3)
+        ]
+
+    def copies_x():
+        return [
+            vector_copy(3 + i, vec_src.at[place["z"], lax.rem(place["x"] + i + 1, 4)], vec_x.at[i], neighbour(place, "x", i + 1))
+            for i in range(3)
+        ]
+
+    def copies_group():
+        return [
+            vector_copy(6 + i, vec_mid, vec_cy.at[i], in_group(place, flip, step))
+            for i, (flip, step) in enumerate(GROUP)
+        ]
+
+    def vectors_start():
+        spread_vectors()
+        for copy in copies_z():
+            copy.start()
+
+    def vectors_second():
+        for copy in copies_z():
+            copy.wait()
+        for x in range(4):
+            vec_src[place["z"], x] += vec_z[0, x] + vec_z[1, x] + vec_z[2, x]
+        for copy in copies_x():
+            copy.start()
+
+    def vectors_third():
+        for copy in copies_x():
+            copy.wait()
+        vec_mid[...] = vec_src[place["z"], place["x"]] + vec_x[0] + vec_x[1] + vec_x[2]
+        for copy in copies_group():
+            copy.start()
+
+    def vectors_last():
+        for copy in copies_group():
+            copy.wait()
+        total = vec_mid[...]
+        for i in range(7):
+            total += vec_cy[i]
+        mine = lax.broadcasted_iota(jnp.int32, (2, 8, 128), 1) == core * 4 + place["y"]
+        vec_out_ref[...] = jnp.sum(jnp.where(mine, total, 0.0), axis=1)
+
     def when(u, job):
         @pl.when((u >= 0) & (u < TRIPLES))
         def _():
@@ -273,6 +356,8 @@
                 copy0(o, u).start()
 
         when(t + 3, make)
+        for k, job in enumerate((vectors_start, vectors_second, vectors_third, vectors_last)):
+            pl.when(now == TRIPLES + k)(job)
         return 0
 
     lax.fori_loop(0, TRIPLES + 7, tick, 0)
@@ -288,14 +373,24 @@
     return out.astype(ml_dtypes.bfloat16)
 
 
-def reduce_gradients(active_t, operands, d_outer, d_inner, d_qkv, d_att):
+def lane_places():
+    out = np.zeros((9216, 128), np.float32)
+    lane = 0
+    for start, width, keep in VECTORS:
+        q = np.arange(width)
+        out[start + q, lane + q % keep] = 1
+        lane += keep
+    return out.astype(ml_dtypes.bfloat16)
+
+
+def reduce_gradients(vectors, active_t, operands, d_outer, d_inner, d_qkv, d_att):
     tile = (8, 128)
     vmem = pl.BlockSpec(memory_space=pltpu.VMEM)
-    out = pl.pallas_call(
+    out, vec_out = pl.pallas_call(
         reduce_kernel,
-        out_shape=jax.ShapeDtypeStruct((TRIPLES, 3, 4) + tile, f32),
-        in_specs=[vmem] * 7,
-        out_specs=vmem,
+        out_shape=(jax.ShapeDtypeStruct((TRIPLES, 3, 4) + tile, f32), jax.ShapeDtypeStruct((2, 128), f32)),
+        in_specs=[vmem] * 9,
+        out_specs=(vmem, vmem),
         scratch_shapes=[
             pltpu.VMEM((3, 3, 768, 256), bf16),
             pltpu.VMEM((3, SLOTS, 16, 12) + tile, f32),
@@ -310,15 +405,29 @@
             pltpu.VMEM((3, SLOTS, 2, 2) + tile, f32),
             pltpu.VMEM((3, SLOTS, 2, 4) + tile, f32),
             pltpu.VMEM((3, 4, 24, 128), f32),
+            pltpu.VMEM((4, 4, 2) + tile, f32),
+            pltpu.VMEM((3, 4, 2) + tile, f32),
+            pltpu.VMEM((3, 2) + tile, f32),
+            pltpu.VMEM((2,) + tile, f32),
+            pltpu.VMEM((7, 2) + tile, f32),
             pltpu.SemaphoreType.DMA((3, 6, 2, SLOTS)),
             pltpu.SemaphoreType.DMA((3, 6, 2, SLOTS)),
             pltpu.SemaphoreType.DMA((3,)),
             pltpu.SemaphoreType.DMA((3, 2)),
+            pltpu.SemaphoreType.DMA((13,)),
+            pltpu.SemaphoreType.DMA((13,)),
         ],
         compiler_params=pltpu.CompilerParams(
             collective_id=1, has_side_effects=True, vmem_limit_bytes=60 * 1024 * 1024
         ),
-    )(active_t, operands, jnp.asarray(permutations()), d_outer, d_inner, d_qkv, d_att)
+    )(
+        active_t, operands, jnp.asarray(permutations()), d_outer, d_inner, d_qkv, d_att,
+        vectors, jnp.asarray(lane_places()),
+    )
+    kept, lane = [], 0
+    for _, _, keep in VECTORS:
+        kept.append(vec_out[:, lane : lane + keep])
+        lane += keep
     out = out.reshape(2, 6, 3, 4, 8, 128)[::-1]
     down = out[:, 0:2, :, 0:3].transpose(0, 2, 4, 1, 3, 5).reshape(2, 24, 768)
     up = out[:, 2:4, :, :, 0:6].transpose(0, 4, 1, 2, 3, 5).reshape(2, 6, 3072)
@@ -326,18 +435,7 @@
     last = out[:, 5, :, :, 0:6].transpose(0, 3, 1, 2, 4)
     qkv = jnp.concatenate([first, last[:, :, :, 0:2]], axis=3).reshape(2, 6, 2304)
     mixer = last[:, :, :, 2:4].reshape(2, 6, 768)
-    return qkv, mixer, up, down
-
-
-def combined_all(part, axis, combine):
-    gathered = jax.tree.map(lambda a: lax.all_gather(a, axis), part)
-
-    def take(source):
-        return jax.tree.map(lambda a: lax.dynamic_index_in_dim(a, source, 0, False), gathered)
-
-    return lax.fori_loop(
-        1, lax.axis_size(axis), lambda source, state: combine(state, take(source)), take(0)
-    )
+    return qkv, mixer, up, down, kept
 
 
 def norm_forward(total_loss, gain, shift):
@@ -553,79 +651,122 @@
     return (dhidden, grads, products)
 
 
-def pairing_cost_term(
-    averaged_layer_states, positive_companion, leading_dimension_counts, affinity_divisor
-):
-    batches = lax.axis_size("batch")
-    tiles = lax.axis_size("tile")
-    per_dev = averaged_layer_states.shape[0]
-    width = averaged_layer_states.shape[-1]
-    nested_level_count = leading_dimension_counts.shape[0]
-    rows = lax.all_gather(averaged_layer_states, "tile", axis=0, tiled=True)
-    cols = lax.all_gather(averaged_layer_states, "batch", axis=0, tiled=True)
-    columns = lax.broadcasted_iota(jnp.int32, (nested_level_count, width), 1)
-    keep = (columns < leading_dimension_counts[:, None]).astype(jnp.float32)
-
-    def unit_of(embed):
-        masked = embed[:, :, None, :] * keep
-        inverse = lax.rsqrt(jnp.sum(masked * masked, axis=-1, keepdims=True) + eps_norm)
-        return (masked * inverse, inverse)
-
-    def unit_back(normalized_direction, inverse, dunit):
-        inside = dunit - normalized_direction * jnp.sum(
-            normalized_direction * dunit, axis=-1, keepdims=True
+def pairing_kernel(emb_ref, companion_ref, widths_ref, divisor_ref, demb_ref, loss_ref, every, send_sem, recv_sem, core_s, core_r):
+    place = my_place()
+    core = place["c"]
+    barrier = pltpu.get_barrier_semaphore()
+    for axis in ("x", "y", "z"):
+        for step in (1, 2, 3):
+            pl.semaphore_signal(barrier, inc=1, device_id=neighbour(place, axis, step), device_id_type=MESH)
+    pl.semaphore_signal(barrier, inc=1, device_id=neighbour(place, "c", 1), device_id_type=MESH)
+    pl.semaphore_wait(barrier, 10)
+
+    def slab(o, phase):
+        done = ORDERS[o][:phase]
+        at = tuple(pl.ds(0, 4) if axis in done else place[axis] for axis in ("z", "x", "c", "y"))
+        return every.at[(o,) + at]
+
+    def copies(o, phase):
+        return [
+            pltpu.make_async_remote_copy(
+                src_ref=slab(o, phase), dst_ref=slab(o, phase),
+                send_sem=send_sem.at[o, phase, step - 1], recv_sem=recv_sem.at[o, phase, step - 1],
+                device_id=neighbour(place, ORDERS[o][phase], step), device_id_type=MESH,
+            )
+            for step in (1, 2, 3)
+        ]
+
+    for o in range(3):
+        every[o, place["z"], place["x"], core, place["y"]] = emb_ref[o]
+        for copy in copies(o, 0):
+            copy.start()
+    for phase in range(3):
+        for o in range(3):
+            for copy in copies(o, phase):
+                copy.wait()
+            if phase < 2:
+                for copy in copies(o, phase + 1):
+                    copy.start()
+    mine = every.at[:, :, :, core]
+    swap = pltpu.make_async_remote_copy(
+        src_ref=mine, dst_ref=mine, send_sem=core_s, recv_sem=core_r,
+        device_id=neighbour(place, "c", 1), device_id_type=MESH,
+    )
+    swap.start()
+    swap.wait()
+
+    me = ((place["z"] * 4 + place["x"]) * 2 + core) * 4 + place["y"]
+    row = lax.broadcasted_iota(jnp.int32, (128, 128), 0)
+    col = lax.broadcasted_iota(jnp.int32, (128, 128), 1)
+    rows = lax.broadcasted_iota(jnp.int32, (128, 1), 0)
+    lane = lax.broadcasted_iota(jnp.int32, (1, 768), 1)
+    companion = companion_ref[...]
+    divisor = divisor_ref[0]
+    partner = (col == companion).astype(f32)
+    is_me = rows == me
+    loss = jnp.zeros((128, 1), f32)
+    keeps = [(lane < widths_ref[p]).astype(f32) for p in range(4)]
+    for e in range(2):
+        embed = jnp.concatenate(
+            [every[o].reshape(128, 4, 128)[:, e * 2 + r, :] for o in range(3) for r in range(2)], axis=1
         )
-        return jnp.sum(keep * inside * inverse, axis=2)
-
-    row_unit, row_inv = unit_of(rows)
-    col_unit, col_inv = unit_of(cols)
-    logit_divisor_scalar = affinity_divisor[0]
-    affinity_matrix = (
-        jnp.einsum("zwfq,xwfq->wfzx", row_unit, col_unit, precision=exact_arithmetic_mode)
-        / logit_divisor_scalar
-    )
-    batch_idx = lax.axis_index("batch")
-    tile_idx = lax.axis_index("tile")
-    row_ids = batch_idx * tiles * per_dev + jnp.arange(tiles * per_dev, dtype=jnp.int32)
-    col_pos = jnp.arange(batches * per_dev, dtype=jnp.int32)
-    col_ids = (col_pos // per_dev * tiles + tile_idx) * per_dev + col_pos % per_dev
-    selfs = row_ids[:, None] == col_ids[None, :]
-    latent_affinity_matrix = jnp.where(selfs, -1e30, affinity_matrix)
-    top = jnp.max(latent_affinity_matrix, axis=-1)
-    total_exp = jnp.sum(jnp.exp(latent_affinity_matrix - top[..., None]), axis=-1)
-    targets = jnp.take(positive_companion, row_ids)
-    matching_indicator = (col_ids[None, :] == targets[:, None]).astype(jnp.float32)
-    target_part = jnp.sum(affinity_matrix * matching_indicator, axis=-1)
-
-    def combine(first, second):
-        upper = jnp.maximum(first[0], second[0])
-        return (
-            upper,
-            first[1] * jnp.exp(first[0] - upper) + second[1] * jnp.exp(second[0] - upper),
-            first[2] + second[2],
-        )
-
-    top, total_exp, target_sims = combined_all((top, total_exp, target_part), "tile", combine)
-    logsumexp_values = top + jnp.log(total_exp)
-    row_losses = jnp.sum(logsumexp_values - target_sims, axis=(0, 1)) / (2 * nested_level_count)
-    affinity_grad_matrix = (
-        (jnp.exp(latent_affinity_matrix - logsumexp_values[..., None]) - matching_indicator)
-        / (2 * nested_level_count)
-        / logit_divisor_scalar
-    )
-    drow_unit = jnp.einsum(
-        "lpij,jlpd->ilpd", affinity_grad_matrix, col_unit, precision=exact_arithmetic_mode
-    )
-    dcol_unit = jnp.einsum(
-        "lpij,ilpd->jlpd", affinity_grad_matrix, row_unit, precision=exact_arithmetic_mode
-    )
-    drows = lax.psum_scatter(
-        unit_back(row_unit, row_inv, drow_unit), "tile", scatter_dimension=0, tiled=True
-    )
-    dcols = lax.psum_scatter(
-        unit_back(col_unit, col_inv, dcol_unit), "batch", scatter_dimension=0, tiled=True
-    )
-    return (row_losses, drows + dcols)
+        high = embed.astype(bf16)
+        low = (embed - high.astype(f32)).astype(bf16)
+        own = jnp.sum(jnp.where(is_me, embed, 0.0), axis=0, keepdims=True)
+        total = jnp.zeros((1, 768), f32)
+        for p in range(4):
+            keep = keeps[p]
+            keep_low = keep.astype(bf16)
+            high_p, low_p = high * keep_low, low * keep_low
+            nt = (((1,), (1,)), ((), ()))
+            gram = (
+                lax.dot_general(high_p, high, nt, preferred_element_type=f32)
+                + lax.dot_general(high_p, low, nt, preferred_element_type=f32)
+                + lax.dot_general(low_p, high, nt, preferred_element_type=f32)
+            )
+            diagonal = jnp.where(row == col, gram, 0.0)
+            inverse = lax.rsqrt(jnp.sum(diagonal, axis=1, keepdims=True) + eps_norm)
+            inverse_row = lax.rsqrt(jnp.sum(diagonal, axis=0, keepdims=True) + eps_norm)
+            sims = gram * inverse * inverse_row / divisor
+            sims = jnp.where(row == col, -1e30, sims)
+            top = jnp.max(sims, axis=1, keepdims=True)
+            lse = top + jnp.log(jnp.sum(jnp.exp(sims - top), axis=1, keepdims=True))
+            loss = loss + (lse - jnp.sum(sims * partner, axis=1, keepdims=True))
+            to_me = jnp.sum(jnp.where(col == me, sims, 0.0), axis=1, keepdims=True)
+            lse_me = jnp.sum(jnp.where(is_me, lse, 0.0), axis=0, keepdims=True)
+            chosen = (companion == me).astype(f32)
+            weight = jnp.exp(to_me - lse_me) + jnp.exp(to_me - lse) - 2.0 * chosen
+            dunit = jnp.sum(embed * (weight * inverse), axis=0, keepdims=True) * keep
+            inverse_me = jnp.sum(jnp.where(is_me, inverse, 0.0), axis=0, keepdims=True)
+            unit_me = own * keep * inverse_me
+            inside = dunit - unit_me * jnp.sum(unit_me * dunit, axis=1, keepdims=True)
+            total = total + inside * inverse_me
+        demb_ref[e : e + 1, :] = total / (8.0 * divisor)
+    loss_ref[...] = loss / 8.0
+
+
+def pairing_cost_term(averaged_layer_states, positive_companion, leading_dimension_counts, affinity_divisor):
+    vmem = pl.BlockSpec(memory_space=pltpu.VMEM)
+    smem = pl.BlockSpec(memory_space=pltpu.SMEM)
+    parts = averaged_layer_states.reshape(2, 3, 2, 128).transpose(1, 0, 2, 3).reshape(3, 4, 128)
+    demb, loss = pl.pallas_call(
+        pairing_kernel,
+        out_shape=(jax.ShapeDtypeStruct((2, 768), f32), jax.ShapeDtypeStruct((128, 1), f32)),
+        in_specs=[vmem, vmem, smem, smem],
+        out_specs=(vmem, vmem),
+        scratch_shapes=[
+            pltpu.VMEM((3, 4, 4, 2, 4, 4, 128), f32),
+            pltpu.SemaphoreType.DMA((3, 3, 3)),
+            pltpu.SemaphoreType.DMA((3, 3, 3)),
+            pltpu.SemaphoreType.DMA,
+            pltpu.SemaphoreType.DMA,
+        ],
+        compiler_params=pltpu.CompilerParams(
+            collective_id=2, has_side_effects=True, vmem_limit_bytes=32 * 1024 * 1024
+        ),
+    )(parts, positive_companion[:, None], leading_dimension_counts, affinity_divisor)
+    row_losses = lax.dynamic_slice_in_dim(loss[:, 0], lax.axis_index("batch") * 4, 4)
+    return (row_losses, demb[None])
 
 
 def body(
@@ -686,13 +827,14 @@
     )
     dfront = dfront + spread * embedding_gradient[:, 0][:, None, :]
     dinputs, grads_front, products_front = layer_backward(dfront, saved_front, first)
-    stacked = [jnp.stack([gf, gb]) for gf, gb in zip(grads_front, grads_behind)]
-    qvbias, outbias, attgain, attshift, ffnbias, downbias, fingain, finshift = (
-        lax.psum_scatter(s, ("batch", "tile"), scatter_dimension=1, tiled=True) for s in stacked
-    )
-    qkv, mixer, up, down = reduce_gradients(
-        *(jnp.stack([pf, pb]) for pf, pb in zip(products_front, products_behind))
-    )
+    def joined(qvbias, outbias, attgain, attshift, ffnbias, downbias, fingain, finshift):
+        return jnp.concatenate([outbias, attgain, attshift, downbias, fingain, finshift, qvbias, ffnbias])
+
+    qkv, mixer, up, down, kept = reduce_gradients(
+        jnp.stack([joined(*grads_front), joined(*grads_behind)]),
+        *(jnp.stack([pf, pb]) for pf, pb in zip(products_front, products_behind)),
+    )
+    outbias, attgain, attshift, downbias, fingain, finshift, qvbias, ffnbias = kept
     return (
         row_losses,
         averaged_layer_states,

time: 651 us -> 340 us (0.52)
  waiting for transfers between devices: 170 us -> 0 us
  blocking collectives: 95.6 us -> 0 us
  other arithmetic: 68.2 us -> 40.1 us
  Pallas kernels: 165 us -> 189 us
  local copies, waits for them, and re-layouts: 44.6 us -> 29.5 us
  between operations: 17.7 us -> 3.9 us
  matrix products: 81.1 us -> 73.2 us
    unnamed x4 -> x0, waiting for transfers between devices: 170 us -> none
    all_gather x5 -> x0, blocking collectives: 77.3 us -> none  [the longest x3 35.8 us: combined_all(): gathered = jax.tree.map(lambda a: lax.all_gather(a, axis), part)]
    pallas_call x1 -> x2, Pallas kernels: 165 us -> 189 us  [the longest x1 166 us: reduce_gradients(): pl.pallas_call(reduce_kernel, out_shape=(jax.ShapeDtypeStruct((TRIPLES, 3...]
    unnamed x1 -> x0, blocking collectives: 18.3 us -> none
    another operation x10, other arithmetic: 33.7 us -> 22.3 us  [body(): jnp.stack([pf, pb])]
    unnamed x300 -> x222, local copies, waits for them, and re-layouts: 20.9 us -> 10.4 us
  transfers between devices with their start and end apart: 2 -> 0, of which waited for: 2 -> 0; matrix products, arithmetic and copies ran while one was open for 7% -> 0% of each run, Pallas kernels for 0% -> 0%
where the time goes in v2:
time: 340 us; the launch traced here: 336 us
  Pallas kernels  189 us (56%)
  matrix products  73.2 us (22%)
  other arithmetic  40.1 us (12%)
  local copies, waits for them, and re-layouts  29.5 us (9%)
  between operations  3.9 us (1%)
    pallas_call x1, Pallas kernels, reduce_gradients(): pl.pallas_call(reduce_kernel, out_shape=(jax.ShapeDtypeStruct((TRIPLES, 3...  166 us
    pallas_call x1, Pallas kernels, pairing_cost_term(): pl.pallas_call(pairing_kernel, out_shape=(jax.ShapeDtypeStruct((2, 768),...  22.8 us
    another operation x10, other arithmetic, body(): jnp.stack([pf, pb])  22.3 us
    dot_general x2, matrix products, layer_forward(): jnp.einsum('ncm,mj->ncj', middle_reduced, expand_layer_matrix, preferred_...  19.9 us
    dot_general x2, matrix products, layer_backward(): jnp.einsum('qec,pc->qep', inner_gradient, expand_layer_matrix, preferred_...  11 us
    unnamed x222, local copies, waits for them, and re-layouts  10.4 us
    dot_general x2, matrix products, layer_backward(): jnp.einsum('cov,gv->cog', outer_gradient, shrink_layer_matrix, preferred_...  10 us

profile of v2, /device:TPU:0, one launch (start us, length us, event | category | flops | bytes accessed | tf_op | source)
XLA Modules:
  0.0 335.8 jit_solution(15966351103099408946)
XLA Ops:
  1.9 1.4 convert_reduce_fusion.8
  3.2 1.4 convert_reduce_fusion.10
  4.6 1.4 slice_convert_fusion
  6.0 1.4 convert_reduce_fusion.13
  7.4 0.8 slice_convert_fusion.2
  8.8 3.2 fusion.35
  12.2 0.9 copy.72
  13.9 0.9 copy.74
  14.8 2.8 fusion.222
  17.6 1.8 convolution_convert_fusion.5
  19.5 1.3 copy-done.83
  22.0 10.3 %fusion.42 = (f32[256,3072]{1,0:T(8,128)S(1)}, f32[256,3072]{1,0:T(8,128)S(1)}) fusion(f32[3072]{0:T(1024)S(1)} %bitcast.480, bf16[2,768,3072]{2,1,0:T(8,128)(2,1)} %param.30, bf16[1,256,768]{2,1,0:T(8,128)(2,1)S(1)} %fusion.188), kind=kOutput, calls=%fused_computation.44 | convolution fusion | flops 1257504768 | bytes 11415552 | tf_op jit(solution)/shard_map/ncm,mj->ncj/dot_general | solution.py:512
  32.4 1.6 fusion.224
  34.0 0.9 copy-done.8
  35.4 1.1 fusion.34
  36.6 0.9 copy.76
  37.9 2.8 fusion.225
  40.7 2.5 convolution_convert_fusion.4
  43.3 0.6 fusion.226
  44.5 9.6 %fusion.43 = (f32[256,3072]{1,0:T(8,128)S(1)}, f32[256,3072]{1,0:T(8,128)S(1)}) fusion(f32[3072]{0:T(1024)S(1)} %bitcast.479, bf16[2,768,3072]{2,1,0:T(8,128)(2,1)} %param.30, bf16[1,256,768]{2,1,0:T(8,128)(2,1)S(1)} %fusion.189), kind=kOutput, calls=%fused_computation.45 | convolution fusion | flops 1257504768 | bytes 11415552 | tf_op jit(solution)/shard_map/ncm,mj->ncj/dot_general | solution.py:512
  54.1 1.7 copy-done.4
  55.9 1.6 fusion.227
  59.0 22.8 %shard_map.298 = (f32[2,768]{1,0:T(2,128)S(1)}, f32[128,1]{1,0:T(8,128)S(1)}) custom-call(f32[3,4,128]{2,1,0:T(4,128)S(1)} %bitcast.431, s32[128,1]{1,0:T(8,128)S(1)} %copy.80.companion_ref, s32[4]{0:T(128)S(1)} %copy-done, f32[1]{0:T(128)S(6)} %copy.131.divisor_ref), custom_call_target="tpu_custom_call" | custom-call | tf_op jit(solution)/shard_map/pallas_call | solution.py:752
  81.8 0.6 dynamic-slice_reduce_fusion
  83.6 0.9 convert_reduce_fusion.4
  84.5 7.0 %convert_reduce_fusion = (f32[3072]{0:T(1024)}, bf16[256,3072]{1,0:T(8,128)(2,1)S(1)}) fusion(f32[256,3072]{1,0:T(8,128)} %copy-done.11, f32[256,3072]{1,0:T(8,128)} %copy-done.4, bf16[2,3072,768]{2,1,0:T(8,128)(2,1)} %param.32, bf16[1,256,768]{2,1,0:T(8,128)(2,1)S(1)} %get-tuple-element.65), kind=kOutput, calls=%fused_computation.64 | convolution fusion | flops 1220539392 | bytes 12988416 | tf_op jit(solution)/shard_map/cov,gv->cog/dot_general | solution.py:581
  91.5 5.5 %multiply_reduce_fusion.3 = (f32[768]{0:T(1024)}, f32[256]{0:T(256)S(1)}, f32[256]{0:T(256)S(1)}, f32[768]{0:T(1024)}, f32[1,256,768]{2,1,0:T(8,128)S(1)}) fusion(f32[1,256,768]{2,1,0:T(8,128)S(1)} %get-tuple-element.102, f32[256]{0:T(256)S(1)} %add_rsqrt_fusion.1, f32[256]{0:T(256)S(1)} %broadcast_multiply_fusion.9, f32[768]{0:T(1024)S(1)} %get-tuple-element.123, ...), kind=kOutput, calls=%fused_computation.218 | convolution fusion | flops 1211496448 | bytes 8675328 | tf_op jit(solution)/shard_map/qec,pc->qep/dot_general | solution.py:587
  97.0 1.8 convert_reduce_fusion.5
  99.5 2.7 convolution_convert_fusion.2
  102.4 0.7 multiply_reduce_fusion.1
  103.1 1.0 multiply_convert_fusion.1
  105.7 2.1 multiply_reduce_fusion.4
  108.1 0.7 copy-done.2
  109.1 1.1 copy-done.9
  110.2 3.0 convert_reduce_fusion.1
  113.2 5.5 %multiply_reduce_fusion.5 = (f32[768]{0:T(1024)}, f32[256]{0:T(256)S(1)}, f32[256]{0:T(256)S(1)}, f32[768]{0:T(1024)}, f32[1,256,768]{2,1,0:T(8,128)S(1)}) fusion(f32[1,256,768]{2,1,0:T(8,128)S(1)} %get-tuple-element.94, f32[256]{0:T(256)S(1)} %add_rsqrt_fusion.3, f32[256]{0:T(256)S(1)} %broadcast_multiply_fusion.11, f32[768]{0:T(1024)S(1)} %get-tuple-element.122, ...), kind=kOutput, calls=%fused_computation.222 | convolution fusion | flops 1211299840 | bytes 9457664 | tf_op jit(solution)/shard_map/qec,pc->qep/dot_general | solution.py:587
  118.7 0.9 convert_reduce_fusion.7
  119.6 0.7 copy-done.42
  121.0 2.6 convolution_convert_fusion
  123.9 0.7 multiply_reduce_fusion
  125.2 0.7 copy-done.13
  127.7 2.1 fusion.126
  129.8 6.7 %fusion.104 = bf16[1,3072,256]{1,2,0:T(8,128)(2,1)S(1)} fusion(f32[256,3072]{1,0:T(8,128)S(1)} %copy-done.5), kind=kLoop, calls=%fused_computation.148 | loop fusion | flops 51118080 | bytes 4718592 | tf_op jit(solution)/shard_map/stack | solution.py:835
  136.5 6.9 %fusion.105 = bf16[1,3072,256]{1,2,0:T(8,128)(2,1)S(1)} fusion(f32[256,3072]{1,0:T(8,128)S(1)} %copy-done.3), kind=kLoop, calls=%fused_computation.149 | loop fusion | flops 51118080 | bytes 4718592 | tf_op jit(solution)/shard_map/stack | solution.py:835
  143.7 2.8 copy.97.act_t_ref
  146.6 1.3 copy.90
  147.8 1.1 maximum_bitcast_fusion.1
  149.4 1.6 pad_maximum_fusion.2.a_ref
  151.0 1.0 pad_maximum_fusion.3.bd_ref
  152.5 2.0 pad_maximum_fusion.1.bu_ref
  155.9 1.6 maximum_maximum_fusion.bq_ref
  157.5 1.0 pad_maximum_fusion.4.bo_ref
  159.2 0.7 pad_maximum_fusion.6.vec_ref
  159.9 166.3 %shard_map.299 = (f32[12,3,4,8,128]{4,3,2,1,0:T(8,128)}, f32[2,128]{1,0:T(2,128)}) custom-call(bf16[2,3072,256]{2,1,0:T(8,128)(2,1)} %copy.97.act_t_ref, bf16[2,3,256,768]{3,2,1,0:T(8,128)(2,1)} %pad_maximum_fusion.2.a_ref, bf16[3,768,768]{2,1,0:T(8,128)(2,1)} %constant.113.clone.perm_ref, bf16[2,256,768]{2,1,0:T(8,128)(2,1)} %pad_maximum_fusion.3.bd_ref, ...), custom_call_target="tpu_custom_call" | custom-call | tf_op jit(solution)/shard_map/pallas_call | solution.py:389
  326.3 1.0 fusion.219
  327.4 0.7 reshape.1285
  328.1 1.3 slice.235
  329.4 0.7 reshape.1286
  330.1 1.5 fusion.221
  331.6 0.9 slice.268
  332.6 0.8 reshape.1287
  333.4 0.6 slice.242
  334.0 0.9 slice.269
  335.0 0.7 copy.101
  (300 shorter events, 16.0 us)
Async XLA Ops:
  13.9 5.6 %copy-start.12 = (bf16[1,256,768]{1,2,0:T(8,128)(2,1)}, bf16[1,256,768]{1,2,0:T(8,128)(2,1)S(1)}, u32[]{:S(2)}) copy-start(bf16[1,256,768]{1,2,0:T(8,128)(2,1)S(1)} %copy.73) | copy-start | bytes 1179652
  17.6 3.2 copy-start.83
  21.5 13.9 %slice-start.9 = ((s8[7077888]{0:T(1024)(128)(4,1)}), s8[4194304]{0:T(1024)(128)(4,1)S(1)}, s32[]{:S(2)}) async-start(s8[7077888]{0:T(1024)(128)(4,1)} %bitcast.482), calls=%async_computation.9 | async-start | bytes 8388608
  21.7 10.6 %slice-start = ((s8[9437184]{0:T(1024)(128)(4,1)}), s8[4194304]{0:T(1024)(128)(4,1)S(1)}, s32[]{:S(2)}) async-start(s8[9437184]{0:T(1024)(128)(4,1)} %bitcast.433), calls=%async_computation | async-start | bytes 8388608
  21.9 10.3 %copy-start.15 = (bf16[1,256,768]{2,1,0:T(8,128)(2,1)}, bf16[1,256,768]{2,1,0:T(8,128)(2,1)S(1)}, u32[]{:S(2)}) copy-start(bf16[1,256,768]{2,1,0:T(8,128)(2,1)S(1)} %fusion.188) | copy-start | bytes 1179652
  22.0 10.4 %slice-start.1 = ((s8[9437184]{0:T(1024)(128)(4,1)}), s8[4194304]{0:T(1024)(128)(4,1)S(1)}, s32[]{:S(2)}) async-start(s8[9437184]{0:T(1024)(128)(4,1)} %bitcast.433), calls=%async_computation.1 | async-start | bytes 8388608
  22.0 10.4 %slice-start.2 = ((s8[9437184]{0:T(1024)(128)(4,1)}), s8[1048576]{0:T(1024)(128)(4,1)S(1)}, s32[]{:S(2)}) async-start(s8[9437184]{0:T(1024)(128)(4,1)} %bitcast.433), calls=%async_computation.2 | async-start | bytes 2097152
  22.0 10.4 %copy-start.58 = (f32[768]{0:T(1024)S(1)}, f32[768]{0:T(1024)}, u32[]{:S(2)}) copy-start(f32[768]{0:T(1024)} %get-tuple-element.50) | copy-start | bytes 9220
  22.0 13.3 %slice-start.10 = ((s8[7077888]{0:T(1024)(128)(4,1)}), s8[2883584]{0:T(1024)(128)(4,1)S(1)}, s32[]{:S(2)}) async-start(s8[7077888]{0:T(1024)(128)(4,1)} %bitcast.482), calls=%async_computation.10 | async-start | bytes 5767168
  32.3 2.6 copy-start.8
  32.4 3.0 copy-start.70
  37.7 5.5 %copy-start.20 = (bf16[1,256,768]{1,2,0:T(8,128)(2,1)}, bf16[1,256,768]{1,2,0:T(8,128)(2,1)S(1)}, u32[]{:S(2)}) copy-start(bf16[1,256,768]{1,2,0:T(8,128)(2,1)S(1)} %copy.77) | copy-start | bytes 1179652
  37.7 3.0 copy-start.51
  37.9 5.3 %copy-start.22 = (bf16[1,256,768]{1,2,0:T(8,128)(2,1)}, bf16[1,256,768]{1,2,0:T(8,128)(2,1)S(1)}, u32[]{:S(2)}) copy-start(bf16[1,256,768]{1,2,0:T(8,128)(2,1)S(1)} %copy.78) | copy-start | bytes 1179652
  40.7 2.6 copy-start.84
  43.3 12.5 %slice-start.3 = ((s8[9437184]{0:T(1024)(128)(4,1)}), s8[4194304]{0:T(1024)(128)(4,1)S(1)}, s32[]{:S(2)}) async-start(s8[9437184]{0:T(1024)(128)(4,1)} %bitcast.435), calls=%async_computation.3 | async-start | bytes 8388608
  44.4 9.6 %copy-start.19 = (bf16[1,256,768]{2,1,0:T(8,128)(2,1)}, bf16[1,256,768]{2,1,0:T(8,128)(2,1)S(1)}, u32[]{:S(2)}) copy-start(bf16[1,256,768]{2,1,0:T(8,128)(2,1)S(1)} %fusion.189) | copy-start | bytes 1179652
  44.4 11.3 %slice-start.4 = ((s8[9437184]{0:T(1024)(128)(4,1)}), s8[4194304]{0:T(1024)(128)(4,1)S(1)}, s32[]{:S(2)}) async-start(s8[9437184]{0:T(1024)(128)(4,1)} %bitcast.435), calls=%async_computation.4 | async-start | bytes 8388608
  44.5 11.3 %slice-start.5 = ((s8[9437184]{0:T(1024)(128)(4,1)}), s8[1048576]{0:T(1024)(128)(4,1)S(1)}, s32[]{:S(2)}) async-start(s8[9437184]{0:T(1024)(128)(4,1)} %bitcast.435), calls=%async_computation.5 | async-start | bytes 2097152
  54.1 3.3 copy-start.11
  55.8 3.1 copy-start
  55.8 27.2 %copy-start.71 = (f32[256]{0:T(256)S(1)}, f32[256]{0:T(256)}, u32[]{:S(2)}) copy-start(f32[256]{0:T(256)} %get-tuple-element.119) | copy-start | bytes 3076
  84.5 7.0 %copy-start.36 = (bf16[1,256,768]{2,1,0:T(8,128)(2,1)}, bf16[1,256,768]{2,1,0:T(8,128)(2,1)S(1)}, u32[]{:S(2)}) copy-start(bf16[1,256,768]{2,1,0:T(8,128)(2,1)S(1)} %get-tuple-element.65) | copy-start | bytes 1179652
  91.5 5.5 %copy-start.32 = (bf16[256,3072]{1,0:T(8,128)(2,1)}, bf16[256,3072]{1,0:T(8,128)(2,1)S(1)}, u32[]{:S(2)}) copy-start(bf16[256,3072]{1,0:T(8,128)(2,1)S(1)} %get-tuple-element.115) | copy-start | bytes 4718596
  91.5 7.3 %copy-start.85 = (bf16[2,768,768]{2,1,0:T(8,128)(2,1)S(1)}, bf16[2,768,768]{2,1,0:T(8,128)(2,1)}, u32[]{:S(2)}) copy-start(bf16[2,768,768]{2,1,0:T(8,128)(2,1)} %param.26) | copy-start | bytes 7077892
  98.8 3.4 %copy-start.38 = (bf16[1,256,768]{2,1,0:T(8,128)(2,1)}, bf16[1,256,768]{2,1,0:T(8,128)(2,1)S(1)}, u32[]{:S(2)}) copy-start(bf16[1,256,768]{2,1,0:T(8,128)(2,1)S(1)} %get-tuple-element.67) | copy-start | bytes 1179652
  99.5 2.8 copy-start.10
  99.5 2.9 copy-start.52
  99.5 6.2 %slice-start.11 = ((s8[7077888]{0:T(1024)(128)(4,1)}), s8[4194304]{0:T(1024)(128)(4,1)S(1)}, s32[]{:S(2)}) async-start(s8[7077888]{0:T(1024)(128)(4,1)} %bitcast.484), calls=%async_computation.11 | async-start | bytes 8388608
  102.2 3.5 %copy-start.53 = (bf16[12,64,256]{2,1,0:T(8,128)(2,1)}, bf16[12,64,256]{2,1,0:T(8,128)(2,1)S(1)}, u32[]{:S(2)}) copy-start(bf16[12,64,256]{2,1,0:T(8,128)(2,1)S(1)} %convolution_convert_fusion.2) | copy-start | bytes 1179652
  102.4 3.3 slice-start.12
  103.1 2.6 copy-start.44
  103.1 5.0 %slice-start.6 = ((s8[9437184]{0:T(1024)(128)(4,1)}), s8[4194304]{0:T(1024)(128)(4,1)S(1)}, s32[]{:S(2)}) async-start(s8[9437184]{0:T(1024)(128)(4,1)} %bitcast.437), calls=%async_computation.6 | async-start | bytes 8388608
  104.6 3.5 %slice-start.7 = ((s8[9437184]{0:T(1024)(128)(4,1)}), s8[4194304]{0:T(1024)(128)(4,1)S(1)}, s32[]{:S(2)}) async-start(s8[9437184]{0:T(1024)(128)(4,1)} %bitcast.437), calls=%async_computation.7 | async-start | bytes 8388608
  105.2 2.6 copy-start.24
  105.7 3.2 copy-start.2
  105.7 3.4 %slice-start.8 = ((s8[9437184]{0:T(1024)(128)(4,1)}), s8[1048576]{0:T(1024)(128)(4,1)S(1)}, s32[]{:S(2)}) async-start(s8[9437184]{0:T(1024)(128)(4,1)} %bitcast.437), calls=%async_computation.8 | async-start | bytes 2097152
  105.7 4.5 %copy-start.9 = (f32[256,3072]{1,0:T(8,128)S(1)}, f32[256,3072]{1,0:T(8,128)}, u32[]{:S(2)}) copy-start(f32[256,3072]{1,0:T(8,128)} %copy-done.8) | copy-start | bytes 9437188
  108.1 5.1 %copy-start.40 = (bf16[1,256,768]{2,1,0:T(8,128)(2,1)}, bf16[1,256,768]{2,1,0:T(8,128)(2,1)S(1)}, u32[]{:S(2)}) copy-start(bf16[1,256,768]{2,1,0:T(8,128)(2,1)S(1)} %get-tuple-element.60) | copy-start | bytes 1179652
  113.2 5.5 %copy-start.34 = (bf16[256,3072]{1,0:T(8,128)(2,1)}, bf16[256,3072]{1,0:T(8,128)(2,1)S(1)}, u32[]{:S(2)}) copy-start(bf16[256,3072]{1,0:T(8,128)(2,1)S(1)} %get-tuple-element.117) | copy-start | bytes 4718596
  113.2 7.1 %copy-start.86 = (bf16[2,768,768]{2,1,0:T(8,128)(2,1)S(1)}, bf16[2,768,768]{2,1,0:T(8,128)(2,1)}, u32[]{:S(2)}) copy-start(bf16[2,768,768]{2,1,0:T(8,128)(2,1)} %param.26) | copy-start | bytes 7077892
  121.0 2.8 copy-start.7
  121.0 2.9 copy-start.49
  123.7 3.3 copy-start.55
  123.9 3.8 %slice-start.13 = ((s8[7077888]{0:T(1024)(128)(4,1)}), s8[4194304]{0:T(1024)(128)(4,1)S(1)}, s32[]{:S(2)}) async-start(s8[7077888]{0:T(1024)(128)(4,1)} %bitcast.486), calls=%async_computation.13 | async-start | bytes 8388608
  124.6 3.1 slice-start.14
  129.8 6.7 %copy-start.3 = (f32[256,3072]{1,0:T(8,128)S(1)}, f32[256,3072]{1,0:T(8,128)}, u32[]{:S(2)}) copy-start(f32[256,3072]{1,0:T(8,128)} %copy-done.1) | copy-start | bytes 9437188
  143.7 4.1 %copy-start.18 = (bf16[1,256,768]{2,1,0:T(8,128)(2,1)S(1)}, bf16[1,256,768]{2,1,0:T(8,128)(2,1)}, u32[]{:S(2)}) copy-start(bf16[1,256,768]{2,1,0:T(8,128)(2,1)} %copy-done.17) | copy-start | bytes 1179652
  146.6 2.6 copy-start.16
  146.6 2.6 copy-start.46
  149.3 2.6 copy-start.33
  149.3 3.1 copy-start.35
  152.5 2.5 copy-start.56
  155.8 2.7 copy-start.62
  155.8 2.7 copy-start.76
  155.9 2.7 copy-start.74
  155.9 2.7 copy-start.61
  155.9 2.9 copy-start.66
  155.9 3.0 copy-start.63
  155.9 3.0 copy-start.79
  155.9 3.0 copy-start.78
  155.9 3.0 copy-start.77
  155.9 3.0 copy-start.75
  326.3 7.2 %copy-start.57 = (f32[2,128]{1,0:T(2,128)S(1)}, f32[2,128]{1,0:T(2,128)}, u32[]{:S(2)}) copy-start(f32[2,128]{1,0:T(2,128)} %get-tuple-element.22) | copy-start | bytes 3076
  (38 other events, 67.3 us)

commit v3 on v1

v3 whole, which is shorter than its diff:
```python
import jax
import jax.numpy as jnp
import ml_dtypes
import numpy as np
from jax import lax
from jax.experimental import pallas as pl
from jax.experimental.pallas import tpu as pltpu
from jax.sharding import PartitionSpec as P

eps_norm = 1e-06

f32, bf16 = jnp.float32, jnp.bfloat16
MESH = pl.DeviceIdType.MESH
TRIPLES = 12
SLOTS = 3
ORDERS = (("x", "y", "z"), ("y", "z", "x"), ("z", "x", "y"))


def my_place():
    b = lax.axis_index("batch")
    return {"z": b // 8, "x": lax.rem(b // 2, 4), "c": lax.rem(b, 2), "y": lax.axis_index("tile")}


def device_at(place):
    return {"batch": (place["z"] * 4 + place["x"]) * 2 + place["c"], "tile": place["y"]}


def neighbour(place, axis, step):
    there = dict(place)
    if axis == "c":
        there["c"] = 1 - place["c"]
    else:
        there[axis] = lax.rem(place[axis] + step + 4, 4)
    return device_at(there)


GROUP = tuple((flip, step) for flip in (0, 1) for step in range(4) if flip or step)
VECTORS = tuple((768 * k, 768, 6) for k in range(6)) + ((4608, 1536, 12), (6144, 3072, 24))


def in_group(place, flip, step):
    there = dict(place)
    there["c"] = lax.rem(place["c"] + flip, 2)
    there["y"] = lax.rem(place["y"] + step, 4)
    return device_at(there)


def gelu_parts(inner):
    half = 0.5 * (1.0 + lax.erf(inner * 0.7071067811865476))
    return inner * half, half


def lanes_of(j, width):
    return pl.ds(pl.multiple_of(j * width, width), width)


def rows_of(i, height):
    return pl.ds(pl.multiple_of(i * height, height), height)


NT = (((1,), (1,)), ((), ()))
TN = (((0,), (0,)), ((), ()))


def head_halves(pair):
    first = lax.broadcasted_iota(jnp.int32, pair.shape, 1) < 64
    nothing = jnp.zeros_like(pair)
    return jnp.concatenate([jnp.where(first, pair, nothing), jnp.where(first, nothing, pair)], axis=0)


def pair_probs(q, k, keymask):
    scores = lax.dot_general(head_halves(q * 0.125), k, NT, preferred_element_type=f32) + keymask
    expo = jnp.exp(scores - jnp.max(scores, axis=1, keepdims=True))
    return expo * (1.0 / jnp.sum(expo, axis=1, keepdims=True))


def forward_kernel(
    x_ref, count_ref, wq_ref, bq_ref, wo_ref, bo_ref, g1_ref, s1_ref, wu_ref, bu_ref, wd_ref, bd_ref, g2_ref, s2_ref,
    emb_ref, xb_out, qkv_out, ctx_out, n1_out, r1_out, inner_out, n2_out, r2_out,
    wq, wo, wu, wd, vq, vo, v1, t1, vu, vd, v2, t2, xf, mid_f, mid_b, pool,
    act, xb, qkv, ctx, n1, r1, inner, n2, r2, load_sem, save_sem,
):
    def load(k, layer):
        src, dst = ((wq_ref, wq), (wo_ref, wo), (wu_ref, wu), (wd_ref, wd))[k]
        return pltpu.make_async_copy(src.at[layer], dst.at[layer], load_sem.at[k, layer])

    for layer in range(2):
        for k in range(4):
            load(k, layer).start()

    saves = ((xb, xb_out), (qkv, qkv_out), (ctx, ctx_out), (n1, n1_out), (r1, r1_out), (inner, inner_out), (n2, n2_out), (r2, r2_out))

    def save(k, layer):
        src, dst = saves[k]
        return pltpu.make_async_copy(src.at[layer], dst.at[layer], save_sem.at[k, layer])

    for src, dst in ((bo_ref, vo), (g1_ref, v1), (s1_ref, t1), (bu_ref, vu), (bd_ref, vd), (g2_ref, v2), (s2_ref, t2)):
        for layer in range(2):
            dst[layer] = src[layer : layer + 1, :].astype(f32)
    for layer in range(2):
        vq[layer, :, 0:768] = bq_ref[layer : layer + 1, 0:768].astype(f32)
        vq[layer, :, 768:1536] = jnp.zeros((1, 768), f32)
        vq[layer, :, 1536:2304] = bq_ref[layer : layer + 1, 768:1536].astype(f32)
    xf[...] = x_ref[0].astype(f32)
    count = count_ref[0]
    keymask = jnp.where(lax.broadcasted_iota(jnp.int32, (1, 256), 1) < count, 0.0, -1e9)

    def norm(z, layer, normed_ref, scaled_ref, gain, shift, rows):
        center = z - jnp.mean(z, axis=1, keepdims=True)
        scaled = lax.rsqrt(jnp.mean(center * center, axis=1, keepdims=True) + eps_norm)
        normed = center * scaled
        normed_ref[layer, rows, :] = normed
        scaled_ref[layer, rows, :] = scaled
        return normed * gain[layer] + shift[layer]

    def one_layer(layer, _):
        xb[layer] = xf[...].astype(bf16)
        save(0, layer).start()
        load(0, layer).wait()

        def project(j, _):
            cols = lanes_of(j, 2304)
            mixed = jnp.dot(xb[layer], wq[layer, :, cols], preferred_element_type=f32) + vq[layer, :, cols]
            qkv[layer, :, cols] = mixed.astype(bf16)
            return 0

        lax.fori_loop(0, 1, project, 0)
        save(1, layer).start()

        def attend(pair, _):
            q, k, v = (qkv[layer, :, lanes_of(pair + 6 * third, 128)] for third in range(3))
            probs = pair_probs(q, k, keymask).astype(bf16)
            both = jnp.dot(probs, v, preferred_element_type=f32)
            first = lax.broadcasted_iota(jnp.int32, (256, 128), 1) < 64
            ctx[layer, :, lanes_of(pair, 128)] = jnp.where(first, both[:256], both[256:]).astype(bf16)
            return 0

        lax.fori_loop(0, 6, attend, 0, unroll=6)
        save(2, layer).start()
        load(1, layer).wait()

        def mix(j, _):
            cols = lanes_of(j, 768)
            xf[:, cols] += jnp.dot(ctx[layer], wo[layer, :, cols], preferred_element_type=f32) + vo[layer, :, cols]
            return 0

        lax.fori_loop(0, 1, mix, 0)

        def norm_one(i, _):
            rows = rows_of(i, 64)
            mid = norm(xf[rows, :], layer, n1, r1, v1, t1, rows)
            mid_f[rows, :] = mid
            mid_b[rows, :] = mid.astype(bf16)
            return 0

        lax.fori_loop(0, 4, norm_one, 0, unroll=4)
        save(3, layer).start()
        save(4, layer).start()
        load(2, layer).wait()

        def expand(j, _):
            cols = lanes_of(j, 1024)
            value = jnp.dot(mid_b[...], wu[layer, :, cols], preferred_element_type=f32) + vu[layer, :, cols]
            inner[layer, :, cols] = value
            act[:, cols] = gelu_parts(value)[0].astype(bf16)
            return 0

        lax.fori_loop(0, 3, expand, 0)
        save(5, layer).start()
        load(3, layer).wait()

        def shrink(j, _):
            cols = lanes_of(j, 768)
            mid_f[:, cols] += jnp.dot(act[...], wd[layer, :, cols], preferred_element_type=f32) + vd[layer, :, cols]
            return 0

        lax.fori_loop(0, 1, shrink, 0)

        def norm_two(i, total):
            rows = rows_of(i, 64)
            result = norm(mid_f[rows, :], layer, n2, r2, v2, t2, rows)
            xf[rows, :] = result
            place = lax.broadcasted_iota(jnp.int32, (64, 1), 0) + i * 64
            return total + jnp.sum(jnp.where(place < count, result, 0.0), axis=0, keepdims=True)

        total = lax.fori_loop(0, 4, norm_two, jnp.zeros((1, 768), f32), unroll=4)
        pool[layer] = total / count.astype(f32)
        save(6, layer).start()
        save(7, layer).start()
        return 0

    lax.fori_loop(0, 2, one_layer, 0)
    for layer in range(2):
        emb_ref[0, layer : layer + 1, :] = pool[layer]
    for layer in range(2):
        for k in range(8):
            save(k, layer).wait()


SAVED = ((768, "b"), (2304, "b"), (768, "b"), (768, "f"), (1, "f"), (3072, "f"), (768, "f"), (1, "f"))


def run_forward(slots, counts, weights):
    vmem = pl.BlockSpec(memory_space=pltpu.VMEM)
    smem = pl.BlockSpec(memory_space=pltpu.SMEM)
    hbm = pl.BlockSpec(memory_space=pl.ANY)
    kept = [((2, 256, width), bf16 if kind == "b" else f32) for width, kind in SAVED]
    places = [vmem, smem, hbm, vmem, hbm, vmem, vmem, vmem, hbm, vmem, hbm, vmem, vmem, vmem]
    widths = (2304, 768, 768, 768, 3072, 768, 768, 768)
    out = pl.pallas_call(
        forward_kernel,
        out_shape=[jax.ShapeDtypeStruct((1, 2, 768), f32)] + [jax.ShapeDtypeStruct(s, t) for s, t in kept],
        in_specs=places,
        out_specs=[vmem] + [hbm] * len(kept),
        scratch_shapes=[
            pltpu.VMEM((2, 768, 2304), bf16),
            pltpu.VMEM((2, 768, 768), bf16),
            pltpu.VMEM((2, 768, 3072), bf16),
            pltpu.VMEM((2, 3072, 768), bf16),
        ]
        + [pltpu.VMEM((2, 1, width), f32) for width in widths]
        + [pltpu.VMEM((256, 768), f32), pltpu.VMEM((256, 768), f32), pltpu.VMEM((256, 768), bf16), pltpu.VMEM((2, 1, 768), f32)]
        + [pltpu.VMEM((256, 3072), bf16)]
        + [pltpu.VMEM(s, t) for s, t in kept]
        + [pltpu.SemaphoreType.DMA((4, 2)), pltpu.SemaphoreType.DMA((8, 2))],
        compiler_params=pltpu.CompilerParams(vmem_limit_bytes=62 * 1024 * 1024),
    )(slots, counts, *weights)
    return out[0], out[1:]


def pairing_kernel(emb_ref, companion_ref, widths_ref, divisor_ref, demb_ref, loss_ref, every, send_sem, recv_sem, core_s, core_r):
    place = my_place()
    core = place["c"]
    barrier = pltpu.get_barrier_semaphore()
    for axis in ("x", "y", "z"):
        for step in (1, 2, 3):
            pl.semaphore_signal(barrier, inc=1, device_id=neighbour(place, axis, step), device_id_type=MESH)
    pl.semaphore_signal(barrier, inc=1, device_id=neighbour(place, "c", 1), device_id_type=MESH)
    pl.semaphore_wait(barrier, 10)

    def slab(o, phase):
        done = ORDERS[o][:phase]
        at = tuple(pl.ds(0, 4) if axis in done else place[axis] for axis in ("z", "x", "c", "y"))
        return every.at[(o,) + at]

    def copies(o, phase):
        return [
            pltpu.make_async_remote_copy(
                src_ref=slab(o, phase), dst_ref=slab(o, phase),
                send_sem=send_sem.at[o, phase, step - 1], recv_sem=recv_sem.at[o, phase, step - 1],
                device_id=neighbour(place, ORDERS[o][phase], step), device_id_type=MESH,
            )
            for step in (1, 2, 3)
        ]

    for o in range(3):
        for e in range(2):
            for r in range(2):
                at = 256 * o + 128 * r
                every[o, place["z"], place["x"], core, place["y"], e * 2 + r : e * 2 + r + 1, :] = emb_ref[0, e : e + 1, at : at + 128]
        for copy in copies(o, 0):
            copy.start()
    for phase in range(3):
        for o in range(3):
            for copy in copies(o, phase):
                copy.wait()
            if phase < 2:
                for copy in copies(o, phase + 1):
                    copy.start()
    mine = every.at[:, :, :, core]
    swap = pltpu.make_async_remote_copy(
        src_ref=mine, dst_ref=mine, send_sem=core_s, recv_sem=core_r,
        device_id=neighbour(place, "c", 1), device_id_type=MESH,
    )
    swap.start()
    swap.wait()

    me = ((place["z"] * 4 + place["x"]) * 2 + core) * 4 + place["y"]
    row = lax.broadcasted_iota(jnp.int32, (128, 128), 0)
    col = lax.broadcasted_iota(jnp.int32, (128, 128), 1)
    rows = lax.broadcasted_iota(jnp.int32, (128, 1), 0)
    lane = lax.broadcasted_iota(jnp.int32, (1, 768), 1)
    companion = companion_ref[...]
    divisor = divisor_ref[0]
    partner = (col == companion).astype(f32)
    is_me = rows == me
    loss = jnp.zeros((128, 1), f32)
    keeps = [(lane < widths_ref[p]).astype(f32) for p in range(4)]
    for e in range(2):
        embed = jnp.concatenate(
            [every[o].reshape(128, 4, 128)[:, e * 2 + r, :] for o in range(3) for r in range(2)], axis=1
        )
        high = embed.astype(bf16)
        low = (embed - high.astype(f32)).astype(bf16)
        own = jnp.sum(jnp.where(is_me, embed, 0.0), axis=0, keepdims=True)
        total = jnp.zeros((1, 768), f32)
        for p in range(4):
            keep = keeps[p]
            keep_low = keep.astype(bf16)
            high_p, low_p = high * keep_low, low * keep_low
            nt = (((1,), (1,)), ((), ()))
            gram = (
                lax.dot_general(high_p, high, nt, preferred_element_type=f32)
                + lax.dot_general(high_p, low, nt, preferred_element_type=f32)
                + lax.dot_general(low_p, high, nt, preferred_element_type=f32)
            )
            diagonal = jnp.where(row == col, gram, 0.0)
            inverse = lax.rsqrt(jnp.sum(diagonal, axis=1, keepdims=True) + eps_norm)
            inverse_row = lax.rsqrt(jnp.sum(diagonal, axis=0, keepdims=True) + eps_norm)
            sims = gram * inverse * inverse_row / divisor
            sims = jnp.where(row == col, -1e30, sims)
            top = jnp.max(sims, axis=1, keepdims=True)
            lse = top + jnp.log(jnp.sum(jnp.exp(sims - top), axis=1, keepdims=True))
            loss = loss + (lse - jnp.sum(sims * partner, axis=1, keepdims=True))
            to_me = jnp.sum(jnp.where(col == me, sims, 0.0), axis=1, keepdims=True)
            lse_me = jnp.sum(jnp.where(is_me, lse, 0.0), axis=0, keepdims=True)
            chosen = (companion == me).astype(f32)
            weight = jnp.exp(to_me - lse_me) + jnp.exp(to_me - lse) - 2.0 * chosen
            dunit = jnp.sum(embed * (weight * inverse), axis=0, keepdims=True) * keep
            inverse_me = jnp.sum(jnp.where(is_me, inverse, 0.0), axis=0, keepdims=True)
            unit_me = own * keep * inverse_me
            inside = dunit - unit_me * jnp.sum(unit_me * dunit, axis=1, keepdims=True)
            total = total + inside * inverse_me
        demb_ref[e : e + 1, :] = total / (8.0 * divisor)
    loss_ref[...] = loss / 8.0


def pairing_cost_term(averaged_layer_states, positive_companion, leading_dimension_counts, affinity_divisor):
    vmem = pl.BlockSpec(memory_space=pltpu.VMEM)
    smem = pl.BlockSpec(memory_space=pltpu.SMEM)
    demb, loss = pl.pallas_call(
        pairing_kernel,
        out_shape=(jax.ShapeDtypeStruct((2, 768), f32), jax.ShapeDtypeStruct((128, 1), f32)),
        in_specs=[vmem, vmem, smem, smem],
        out_specs=(vmem, vmem),
        scratch_shapes=[
            pltpu.VMEM((3, 4, 4, 2, 4, 4, 128), f32),
            pltpu.SemaphoreType.DMA((3, 3, 3)),
            pltpu.SemaphoreType.DMA((3, 3, 3)),
            pltpu.SemaphoreType.DMA,
            pltpu.SemaphoreType.DMA,
        ],
        compiler_params=pltpu.CompilerParams(
            collective_id=2, has_side_effects=True, vmem_limit_bytes=32 * 1024 * 1024
        ),
    )(averaged_layer_states, positive_companion[:, None], leading_dimension_counts, affinity_divisor)
    return loss, demb


def permutations():
    rows = np.arange(768).reshape(4, 4, 2, 4, 6)
    names = {"z": 0, "x": 1, "c": 2, "y": 3}
    out = np.zeros((3, 768, 768), np.float32)
    for o, (d1, d2, d3) in enumerate(ORDERS):
        taken = rows.transpose(2, names[d1], names[d2], names[d3], 4).reshape(-1)
        out[o, np.arange(768), taken] = 1
    return out.astype(ml_dtypes.bfloat16)


def lane_places():
    out = np.zeros((9216, 128), np.float32)
    lane = 0
    for start, width, keep in VECTORS:
        q = np.arange(width)
        out[start + q, lane + q % keep] = 1
        lane += keep
    return out.astype(ml_dtypes.bfloat16)


def backward_kernel(
    count_ref, demb_ref, g1_ref, t1_ref, g2_ref, wq_ref, wo_ref, wu_ref, wd_ref,
    xb_ref, qkv_ref, ctx_ref, n1_ref, r1_ref, inner_ref, n2_ref, r2_ref, perm_ref, spread_ref,
    out_ref, vec_out_ref, dx_ref,
    weight, perm, spread, xb, qkv, ctx, n1, r1, inner, n2, r2, gains, grad, d_outer, d_att, d_ctx, act_t, d_inner, d_qkv, vectors,
    apt, half, send, got0, got1a, got1b, half2, got2a, got2b, half3, got3a, got3b, rows24,
    vec_src, vec_z, vec_x, vec_mid, vec_cy,
    weight_sem, load_sem, table_sem, sems_s, sems_r, sem0_s, sem0_r, vec_s, vec_r,
):
    place = my_place()
    core = place["c"]
    saved = {
        "xb": (xb_ref, xb, 0), "qkv": (qkv_ref, qkv, 1), "ctx": (ctx_ref, ctx, 2), "n1": (n1_ref, n1, 3), "r1": (r1_ref, r1, 4),
        "inner": (inner_ref, inner, 5), "n2": (n2_ref, n2, 6), "r2": (r2_ref, r2, 7),
    }

    def load(name, layer):
        src, dst, k = saved[name]
        return pltpu.make_async_copy(src.at[layer], dst, load_sem.at[k])

    def weights(k, layer):
        slot = lax.rem((1 - layer) * 3 + k, 2)
        blocks = []
        for m in range(4):
            cols = pl.ds(768 * m, 768)
            if k == 0:
                src = wd_ref.at[layer, cols]
            elif k == 1:
                src = wu_ref.at[layer, :, cols]
            else:
                src = wq_ref.at[layer, :, cols] if m < 3 else wo_ref.at[layer]
            blocks.append(pltpu.make_async_copy(src, weight.at[slot, cols], weight_sem.at[slot, m]))
        return slot, blocks

    def fetch_weights(k, layer):
        for copy in weights(k, layer)[1]:
            copy.start()

    def ready_weights(k, layer):
        slot, blocks = weights(k, layer)
        for copy in blocks:
            copy.wait()
        return slot

    tables = (
        pltpu.make_async_copy(perm_ref, perm, table_sem.at[0]),
        pltpu.make_async_copy(spread_ref, spread, table_sem.at[1]),
    )
    for name in ("n2", "r2", "inner"):
        load(name, 1).start()
    fetch_weights(0, 1)
    for name in ("n1", "r1"):
        load(name, 1).start()
    tables[0].start()
    fetch_weights(1, 1)
    for name in ("xb", "ctx", "qkv"):
        load(name, 1).start()
    tables[1].start()

    barrier = pltpu.get_barrier_semaphore()
    for axis in ("x", "z"):
        for step in (1, 2, 3):
            pl.semaphore_signal(barrier, inc=1, device_id=neighbour(place, axis, step), device_id_type=MESH)
    for flip, step in GROUP:
        pl.semaphore_signal(barrier, inc=1, device_id=in_group(place, flip, step), device_id_type=MESH)

    half3[...] = jnp.zeros_like(half3)
    for k, src in enumerate((g1_ref, t1_ref, g2_ref)):
        for layer in range(2):
            gains[k, layer] = src[layer : layer + 1, :].astype(f32)
    count = count_ref[0]
    keymask = jnp.where(lax.broadcasted_iota(jnp.int32, (1, 256), 1) < count, 0.0, -1e9)
    places = lax.broadcasted_iota(jnp.int32, (256, 1), 0)
    pooled = jnp.where(places < count, 1.0, 0.0) / count.astype(f32)

    def norm_back(normed, scaled, gain, rounded, at_gain, at_shift, at_bias, layer):
        sums = [jnp.zeros((1, 768), f32) for _ in range(3)]
        for i in range(4):
            rows = pl.ds(64 * i, 64)
            dy, n = grad[rows, :], normed[rows, :]
            dn = dy * gain
            inside = dn - jnp.mean(dn, axis=1, keepdims=True) - n * jnp.mean(dn * n, axis=1, keepdims=True)
            dz = scaled[rows, :] * inside
            low = dz.astype(bf16)
            grad[rows, :] = dz
            rounded[rows, :] = low
            for k, term in enumerate((dy * n, dy, low.astype(f32))):
                sums[k] = sums[k] + jnp.sum(term, axis=0, keepdims=True)
        for at, total in zip((at_gain, at_shift, at_bias), sums):
            vectors[layer, :, at : at + 768] = total

    def begin_layer(layer):
        load("n2", layer).wait()
        load("r2", layer).wait()
        own = demb_ref[0:1, :]

        @pl.when(layer == 1)
        def _():
            grad[...] = pooled * demb_ref[1:2, :]

        @pl.when(layer == 0)
        def _():
            grad[...] += pooled * own

        norm_back(n2, r2, gains[2, layer], d_outer, 3072, 3840, 2304, layer)

        @pl.when(layer == 1)
        def _():
            load("n2", 0).start()
            load("r2", 0).start()

        load("inner", layer).wait()

        def turn(j, _):
            value = inner[:, lanes_of(j, 256)]
            act_t[lanes_of(j, 256), :] = gelu_parts(value)[0].T.astype(bf16)
            return 0

        lax.fori_loop(0, 12, turn, 0, unroll=2)

    def through_expand(layer):
        slot = ready_weights(0, layer)

        def chunk(j, _):
            cols = lanes_of(j, 512)
            d_act = lax.dot_general(d_outer[...], weight[slot, cols, :], NT, preferred_element_type=f32)
            value = inner[:, cols]
            slope = gelu_parts(value)[1] + value * (jnp.exp(-0.5 * value * value) * 0.3989422804014327)
            low = (d_act * slope).astype(bf16)
            d_inner[:, cols] = low
            at = pl.ds(pl.multiple_of(6144 + j * 512, 512), 512)
            vectors[layer, :, at] = jnp.sum(low.astype(f32), axis=0, keepdims=True)
            return 0

        lax.fori_loop(0, 6, chunk, 0, unroll=2)

        @pl.when(layer == 1)
        def _():
            load("inner", 0).start()

        fetch_weights(2, layer)
        load("n1", layer).wait()
        load("r1", layer).wait()
        permute((n1[...] * gains[0, layer] + gains[1, layer]).astype(bf16), 0)

    def permute(operand, which):
        for o in range(3):
            apt[o, which] = lax.dot_general(perm[o], operand, NT, preferred_element_type=f32).astype(bf16)

    def through_mixer(layer):
        slot = ready_weights(1, layer)
        for m in range(4):
            cols = pl.ds(768 * m, 768)
            grad[...] += lax.dot_general(d_inner[:, cols], weight[slot, cols, :], NT, preferred_element_type=f32)
        norm_back(n1, r1, gains[0, layer], d_att, 768, 1536, 0, layer)

        @pl.when(layer == 1)
        def _():
            fetch_weights(0, 0)
            load("n1", 0).start()
            load("r1", 0).start()

        slot = ready_weights(2, layer)
        d_ctx[...] = lax.dot_general(d_att[...], weight[slot, 2304:3072, :], NT, preferred_element_type=f32).astype(bf16)

    def through_attention(layer, first_pair, pairs):
        def pair_back(i, _):
            pair = first_pair + i
            at = [lanes_of(pair + 6 * third, 128) for third in range(3)]
            q, k, v = (qkv[:, cols] for cols in at)
            probs = pair_probs(q, k, keymask)
            dc = head_halves(d_ctx[:, at[0]])
            dp = lax.dot_general(dc, v, NT, preferred_element_type=f32)
            ds = (probs * (dp - jnp.sum(dp * probs, axis=1, keepdims=True))).astype(bf16)
            dq = jnp.dot(
                jnp.concatenate([ds[:256], ds[256:]], axis=1), head_halves(k * 0.125), preferred_element_type=f32
            ).astype(bf16)
            dk = lax.dot_general(ds, head_halves(q * 0.125), TN, preferred_element_type=f32).astype(bf16)
            dv = lax.dot_general(probs.astype(bf16), dc, TN, preferred_element_type=f32).astype(bf16)
            for cols, value in zip(at, (dq, dk, dv)):
                d_qkv[:, cols] = value
            for start, value in ((4608, dq), (5376, dv)):
                where = pl.ds(pl.multiple_of(start + pair * 128, 128), 128)
                vectors[layer, :, where] = jnp.sum(value.astype(f32), axis=0, keepdims=True)
            return 0

        lax.fori_loop(0, pairs, pair_back, 0, unroll=2)

    def through_projection(layer):
        slot = lax.rem((1 - layer) * 3 + 2, 2)
        for m in range(3):
            cols = pl.ds(768 * m, 768)
            grad[...] += lax.dot_general(d_qkv[:, cols], weight[slot, cols, :], NT, preferred_element_type=f32)

        @pl.when(layer == 1)
        def _():
            fetch_weights(1, 0)
            load("qkv", 0).start()

        @pl.when(layer == 0)
        def _():
            dx_ref[0] = grad[...]

    def store_rows(o, slot, mine, tile0, value):
        for j in range(value.shape[1] // 128):
            part = value[:, 128 * j : 128 * (j + 1)].reshape(16, 3, 8, 128)
            if mine:
                half[o, slot, :, tile0 + 3 * j : tile0 + 3 * j + 3] = part
            else:
                send[o, :, tile0 + 3 * j : tile0 + 3 * j + 3] = part

    def product(o, slot, which, ref, at, width, tile0):
        for mine in (True, False):
            c = core if mine else 1 - core
            lhs = apt[o, which, pl.ds(pl.multiple_of(c * 384, 128), 384), :]
            for w in range(0, width, 256):
                value = jnp.dot(lhs, ref[:, at + w : at + w + 256], preferred_element_type=f32)
                store_rows(o, slot, mine, tile0 + 3 * (w // 128), value)

    def product_shrink(slot, k):
        def block(z, _):
            for mine in (True, False):
                c = core if mine else 1 - core
                lhs = jnp.concatenate(
                    [act_t[pl.ds(pl.multiple_of(z * 768 + x * 192 + c * 96, 32), 96), :] for x in range(4)], axis=0
                )
                value = jnp.dot(lhs, d_outer[:, 384 * k : 384 * (k + 1)], preferred_element_type=f32)
                for x in range(4):
                    for y in range(4):
                        for j in range(3):
                            p = {"x": x, "y": y, "z": z}
                            d1, d2, d3 = (p[axis] for axis in ORDERS[j])
                            row = x * 96 + (y * 3 + j) * 8
                            for ct in range(3):
                                tile = value[row : row + 8, 128 * ct : 128 * ct + 128]
                                if mine:
                                    half[j, slot, d1 * 4 + d2, d3 * 3 + ct] = tile
                                else:
                                    send[j, d1 * 4 + d2, d3 * 3 + ct] = tile
            return 0

        lax.fori_loop(0, 4, block, 0)

    def make(u):
        slot = lax.rem(u, 4)
        layer = 1 - u // 6
        kind = lax.rem(u, 6)

        def to_other_core():
            for o in range(3):
                copy0(o, u).start()

        @pl.when(kind == 0)
        def _():
            begin_layer(layer)
            product_shrink(slot, 0)
            to_other_core()

        @pl.when(kind == 1)
        def _():
            product_shrink(slot, 1)
            to_other_core()

            @pl.when(u == 1)
            def _():
                tables[0].wait()

            through_expand(layer)

        @pl.when(kind == 2)
        def _():
            for o in range(3):
                product(o, slot, 0, d_inner, o * 512, 512, 0)
            to_other_core()
            through_mixer(layer)

        @pl.when(kind == 3)
        def _():
            for o in range(3):
                product(o, slot, 0, d_inner, (3 + o) * 512, 512, 0)
            to_other_core()
            load("xb", layer).wait()
            permute(xb[...], 0)
            load("ctx", layer).wait()
            permute(ctx[...], 1)

            @pl.when(layer == 1)
            def _():
                load("xb", 0).start()
                load("ctx", 0).start()

            load("qkv", layer).wait()
            through_attention(layer, 0, 4)

        @pl.when(kind == 4)
        def _():
            for o in range(3):
                product(o, slot, 0, d_qkv, o * 768, 512, 0)
            to_other_core()
            through_attention(layer, 4, 2)
            through_projection(layer)

        @pl.when(kind == 5)
        def _():
            for o in range(3):
                product(o, slot, 0, d_qkv, o * 768 + 512, 256, 0)
                product(o, slot, 1, d_att, o * 256, 256, 6)
            to_other_core()

    def exchange(o, k, slot, src_up, src_down, got):
        axis = ORDERS[o][k // 2]
        return [
            pltpu.make_async_remote_copy(
                src_ref=src, dst_ref=got.at[o, slot, way],
                send_sem=sems_s.at[o, k, way, slot], recv_sem=sems_r.at[o, k, way, slot],
                device_id=neighbour(place, axis, step), device_id_type=MESH,
            )
            for way, (src, step) in enumerate(((src_up, 1), (src_down, -1)))
        ]

    def spots(o, phase):
        a = place[ORDERS[o][phase]]
        return a, lax.rem(a + 1, 4), lax.rem(a + 2, 4), lax.rem(a + 3, 4)

    def copy0(o, u):
        slot = lax.rem(u, 2)
        return pltpu.make_async_remote_copy(
            src_ref=send.at[o], dst_ref=got0.at[o, slot], send_sem=sem0_s.at[o], recv_sem=sem0_r.at[o, slot],
            device_id=neighbour(place, "c", 1), device_id_type=MESH,
        )

    def step_a(o, phase, u):
        slot = lax.rem(u, SLOTS)
        a, up, far, down = spots(o, phase)
        if phase == 0:
            src, got = (half.at[o, lax.rem(u, 4), pl.ds(far * 4, 2)], half.at[o, lax.rem(u, 4), pl.ds(far * 4 + 2, 2)]), got1a
        elif phase == 1:
            src, got = (half2.at[o, slot, far, pl.ds(0, 6)], half2.at[o, slot, far, pl.ds(6, 6)]), got2a
        else:
            src, got = (half3.at[o, slot, far, pl.ds(0, 2)], half3.at[o, slot, far, pl.ds(2, 2)]), got3a
        return exchange(o, 2 * phase, slot, src[0], src[1], got)

    def step_b(o, phase, u):
        slot = lax.rem(u, SLOTS)
        a, up, far, down = spots(o, phase)
        if phase == 0:
            src, got = (half.at[o, lax.rem(u, 4), pl.ds(up * 4, 4)], half.at[o, lax.rem(u, 4), pl.ds(down * 4, 4)]), got1b
        elif phase == 1:
            src, got = (half2.at[o, slot, up], half2.at[o, slot, down]), got2b
        else:
            src, got = (half3.at[o, slot, up], half3.at[o, slot, down]), got3b
        return exchange(o, 2 * phase + 1, slot, src[0], src[1], got)

    def add_a(o, phase, u):
        slot = lax.rem(u, SLOTS)
        a, up, far, down = spots(o, phase)
        if phase == 0:
            for i in range(2):
                half[o, lax.rem(u, 4), up * 4 + i] += got1a[o, slot, 0, i]
                half[o, lax.rem(u, 4), down * 4 + 2 + i] += got1a[o, slot, 1, i]
        elif phase == 1:
            half2[o, slot, up, 0:6] += got2a[o, slot, 0]
            half2[o, slot, down, 6:12] += got2a[o, slot, 1]
        else:
            half3[o, slot, up, 0:2] += got3a[o, slot, 0]
            half3[o, slot, down, 2:4] += got3a[o, slot, 1]

    def add_b(o, phase, u):
        slot = lax.rem(u, SLOTS)
        a, up, far, down = spots(o, phase)
        if phase == 0:
            for i in range(4):
                half2[o, slot, i] = half[o, lax.rem(u, 4), a * 4 + i] + got1b[o, slot, 0, i] + got1b[o, slot, 1, i]
        elif phase == 1:
            total = half2[o, slot, a] + got2b[o, slot, 0] + got2b[o, slot, 1]

            @pl.when(lax.rem(u, 6) < 2)
            def _():
                for k in range(4):
                    half3[o, slot, k, 0:3] = total[3 * k : 3 * k + 3]

            @pl.when(lax.rem(u, 6) >= 2)
            def _():
                for ct in range(4):
                    rows24[o, ct] = total[3 * ct : 3 * ct + 3].reshape(24, 128)
                for k in range(4):
                    for ct in range(4):
                        half3[o, slot, k, ct, 0:6, :] = rows24[o, ct, 6 * k : 6 * k + 6, :]
        else:
            out_ref[u, o] = half3[o, slot, a] + got3b[o, slot, 0] + got3b[o, slot, 1]

    def spread_vectors():
        for layer in range(2):
            total = jnp.zeros((128, 128), f32)
            for start, width, keep in VECTORS:
                d = lax.broadcasted_iota(jnp.int32, (128, width), 0) * keep
                q = lax.broadcasted_iota(jnp.int32, (128, width), 1)
                own = jnp.where((q >= d) & (q < d + keep), vectors[layer, :, start : start + width], 0.0)
                high = own.astype(bf16)
                low = (own - high.astype(f32)).astype(bf16)
                lanes = spread[start : start + width, :]
                total += jnp.dot(high, lanes, preferred_element_type=f32)
                total += jnp.dot(low, lanes, preferred_element_type=f32)
            total = total.reshape(4, 4, 8, 128)
            for z in range(4):
                for x in range(4):
                    vec_src[z, x, layer] = total[z, x]

    def vector_copy(k, src, dst, device):
        return pltpu.make_async_remote_copy(
            src_ref=src, dst_ref=dst, send_sem=vec_s.at[k], recv_sem=vec_r.at[k], device_id=device, device_id_type=MESH
        )

    def copies_z():
        return [
            vector_copy(i, vec_src.at[lax.rem(place["z"] + i + 1, 4)], vec_z.at[i], neighbour(place, "z", i + 1))
            for i in range(3)
        ]

    def copies_x():
        return [
            vector_copy(3 + i, vec_src.at[place["z"], lax.rem(place["x"] + i + 1, 4)], vec_x.at[i], neighbour(place, "x", i + 1))
            for i in range(3)
        ]

    def copies_group():
        return [
            vector_copy(6 + i, vec_mid, vec_cy.at[i], in_group(place, flip, step))
            for i, (flip, step) in enumerate(GROUP)
        ]

    def vectors_start():
        tables[1].wait()
        spread_vectors()
        for copy in copies_z():
            copy.start()

    def vectors_second():
        for copy in copies_z():
            copy.wait()
        for x in range(4):
            vec_src[place["z"], x] += vec_z[0, x] + vec_z[1, x] + vec_z[2, x]
        for copy in copies_x():
            copy.start()

    def vectors_third():
        for copy in copies_x():
            copy.wait()
        vec_mid[...] = vec_src[place["z"], place["x"]] + vec_x[0] + vec_x[1] + vec_x[2]
        for copy in copies_group():
            copy.start()

    def vectors_last():
        for copy in copies_group():
            copy.wait()
        total = vec_mid[...]
        for i in range(7):
            total += vec_cy[i]
        mine = lax.broadcasted_iota(jnp.int32, (2, 8, 128), 1) == core * 4 + place["y"]
        vec_out_ref[...] = jnp.sum(jnp.where(mine, total, 0.0), axis=1)

    def when(u, job):
        @pl.when((u >= 0) & (u < TRIPLES))
        def _():
            job(u)

    def tick(now, _):
        t = now - 3

        def enter(u):
            slot = lax.rem(u, SLOTS)
            for o in range(3):
                copy0(o, u).wait()

                def add(i, _):
                    half[o, lax.rem(u, 4), i] += got0[o, lax.rem(u, 2), i]
                    return 0

                lax.fori_loop(0, 16, add, 0)
                for copy in step_a(o, 0, u):
                    copy.start()

        def second(phase):
            def job(u):
                for o in range(3):
                    for copy in step_a(o, phase, u):
                        copy.wait()
                    add_a(o, phase, u)
                    for copy in step_b(o, phase, u):
                        copy.start()
            return job

        def third(phase):
            def job(u):
                for o in range(3):
                    for copy in step_b(o, phase, u):
                        copy.wait()
                    add_b(o, phase, u)
                    if phase < 2:
                        for copy in step_a(o, phase + 1, u):
                            copy.start()
            return job

        when(t + 3, make)
        when(t + 1, second(0))
        when(t, third(0))
        when(t - 1, second(1))
        when(t - 2, third(1))
        when(t - 3, second(2))
        when(t - 4, third(2))

        when(t + 3, enter)
        for k, job in enumerate((vectors_start, vectors_second, vectors_third, vectors_last)):
            pl.when(now == TRIPLES + k)(job)
        return 0

    pl.semaphore_wait(barrier, 13)
    lax.fori_loop(0, TRIPLES + 7, tick, 0)


def finish_kernel(out_ref, vec_ref, loss_ref, dx_ref, *outs):
    loss_out, dx_out, qkv_out, qv_out, mixer_out, bias_out, gain_out, shift_out, up_out, ffn_out, down_out, downbias_out, fingain_out, finshift_out, sem = outs
    copy = pltpu.make_async_copy(dx_ref, dx_out, sem)
    copy.start()
    for layer in range(2):
        first = 6 * (1 - layer)
        for k in range(2):
            for o in range(3):
                for ct in range(3):
                    down_out[layer, 8 * o : 8 * o + 8, 384 * k + 128 * ct : 384 * k + 128 * ct + 128] = out_ref[first + k, o, ct]
                for ct in range(4):
                    at = (k * 3 + o) * 512 + 128 * ct
                    up_out[layer, :, at : at + 128] = out_ref[first + 2 + k, o, ct, 0:6, :]
        for o in range(3):
            for ct in range(4):
                at = o * 768 + 128 * ct
                qkv_out[layer, :, at : at + 128] = out_ref[first + 4, o, ct, 0:6, :]
            for ct in range(2):
                at = o * 768 + 512 + 128 * ct
                qkv_out[layer, :, at : at + 128] = out_ref[first + 5, o, ct, 0:6, :]
                at = o * 256 + 128 * ct
                mixer_out[layer, :, at : at + 128] = out_ref[first + 5, o, 2 + ct, 0:6, :]
    lane = 0
    for (_, _, keep), dst in zip(
        VECTORS, (bias_out, gain_out, shift_out, downbias_out, fingain_out, finshift_out, qv_out, ffn_out)
    ):
        dst[...] = vec_ref[:, lane : lane + keep]
        lane += keep
    rows = lax.broadcasted_iota(jnp.int32, (128, 1), 0)
    for k in range(4):
        loss_out[k] = jnp.sum(jnp.where(rows == lax.axis_index("batch") * 4 + k, loss_ref[...], 0.0))
    copy.wait()


def run_backward(counts, demb, loss, weights, saved):
    triple, _, mixer, _, gain_one, shift_one, expand, _, shrink, _, gain_two, _ = weights
    xb, qkv, ctx, n1, r1, inner, n2, r2 = saved
    tile = (8, 128)
    vmem = pl.BlockSpec(memory_space=pltpu.VMEM)
    smem = pl.BlockSpec(memory_space=pltpu.SMEM)
    hbm = pl.BlockSpec(memory_space=pl.ANY)
    out, vec_out, dx = pl.pallas_call(
        backward_kernel,
        out_shape=(
            jax.ShapeDtypeStruct((TRIPLES, 3, 4) + tile, f32),
            jax.ShapeDtypeStruct((2, 128), f32),
            jax.ShapeDtypeStruct((1, 256, 768), f32),
        ),
        in_specs=[smem] + [vmem] * 4 + [hbm] * 14,
        out_specs=(vmem, vmem, vmem),
        scratch_shapes=[
            pltpu.VMEM((2, 3072, 768), bf16),
            pltpu.VMEM((3, 768, 768), bf16),
            pltpu.VMEM((9216, 128), bf16),
            pltpu.VMEM((256, 768), bf16),
            pltpu.VMEM((256, 2304), bf16),
            pltpu.VMEM((256, 768), bf16),
            pltpu.VMEM((256, 768), f32),
            pltpu.VMEM((256, 1), f32),
            pltpu.VMEM((256, 3072), f32),
            pltpu.VMEM((256, 768), f32),
            pltpu.VMEM((256, 1), f32),
            pltpu.VMEM((3, 2, 1, 768), f32),
            pltpu.VMEM((256, 768), f32),
            pltpu.VMEM((256, 768), bf16),
            pltpu.VMEM((256, 768), bf16),
            pltpu.VMEM((256, 768), bf16),
            pltpu.VMEM((3072, 256), bf16),
            pltpu.VMEM((256, 3072), bf16),
            pltpu.VMEM((256, 2304), bf16),
            pltpu.VMEM((2, 1, 9216), f32),
            pltpu.VMEM((3, 2, 768, 256), bf16),
            pltpu.VMEM((3, 4, 16, 12) + tile, f32),
            pltpu.VMEM((3, 16, 12) + tile, f32),
            pltpu.VMEM((3, 2, 16, 12) + tile, f32),
            pltpu.VMEM((3, SLOTS, 2, 2, 12) + tile, f32),
            pltpu.VMEM((3, SLOTS, 2, 4, 12) + tile, f32),
            pltpu.VMEM((3, SLOTS, 4, 12) + tile, f32),
            pltpu.VMEM((3, SLOTS, 2, 6) + tile, f32),
            pltpu.VMEM((3, SLOTS, 2, 12) + tile, f32),
            pltpu.VMEM((3, SLOTS, 4, 4) + tile, f32),
            pltpu.VMEM((3, SLOTS, 2, 2) + tile, f32),
            pltpu.VMEM((3, SLOTS, 2, 4) + tile, f32),
            pltpu.VMEM((3, 4, 24, 128), f32),
            pltpu.VMEM((4, 4, 2) + tile, f32),
            pltpu.VMEM((3, 4, 2) + tile, f32),
            pltpu.VMEM((3, 2) + tile, f32),
            pltpu.VMEM((2,) + tile, f32),
            pltpu.VMEM((7, 2) + tile, f32),
            pltpu.SemaphoreType.DMA((2, 4)),
            pltpu.SemaphoreType.DMA((8,)),
            pltpu.SemaphoreType.DMA((2,)),
            pltpu.SemaphoreType.DMA((3, 6, 2, SLOTS)),
            pltpu.SemaphoreType.DMA((3, 6, 2, SLOTS)),
            pltpu.SemaphoreType.DMA((3,)),
            pltpu.SemaphoreType.DMA((3, 2)),
            pltpu.SemaphoreType.DMA((13,)),
            pltpu.SemaphoreType.DMA((13,)),
        ],
        compiler_params=pltpu.CompilerParams(
            collective_id=1, has_side_effects=True, vmem_limit_bytes=63 * 1024 * 1024
        ),
    )(
        counts, demb, gain_one, shift_one, gain_two, triple, mixer, expand, shrink,
        xb, qkv, ctx, n1, r1, inner, n2, r2, jnp.asarray(permutations()), jnp.asarray(lane_places()),
    )
    shapes = [(4,), (1, 256, 768), (2, 6, 2304), (2, 12), (2, 6, 768), (2, 6), (2, 6), (2, 6), (2, 6, 3072), (2, 24), (2, 24, 768), (2, 6), (2, 6), (2, 6)]
    return pl.pallas_call(
        finish_kernel,
        out_shape=[jax.ShapeDtypeStruct(s, f32) for s in shapes],
        in_specs=[vmem, vmem, vmem, hbm],
        out_specs=[smem, hbm] + [vmem] * 12,
        scratch_shapes=[pltpu.SemaphoreType.DMA],
        compiler_params=pltpu.CompilerParams(vmem_limit_bytes=32 * 1024 * 1024),
    )(out, vec_out, loss, dx)


def body(
    slot_state_vectors,
    sequence_token_counts,
    positive_companion,
    leading_dimension_counts,
    affinity_divisor,
    triple_projection_matrix,
    probe_payload_shift,
    mixer_projection_matrix,
    mixer_projection_shift,
    mixer_scale_factor,
    mixer_shift_term,
    expand_layer_matrix,
    expand_layer_shift,
    shrink_layer_matrix,
    shrink_layer_shift,
    closing_scale_factor,
    closing_shift_term,
):
    weights = (
        triple_projection_matrix,
        probe_payload_shift,
        mixer_projection_matrix,
        mixer_projection_shift,
        mixer_scale_factor,
        mixer_shift_term,
        expand_layer_matrix,
        expand_layer_shift,
        shrink_layer_matrix,
        shrink_layer_shift,
        closing_scale_factor,
        closing_shift_term,
    )
    averaged_layer_states, saved = run_forward(slot_state_vectors, sequence_token_counts, weights)
    loss, demb = pairing_cost_term(
        averaged_layer_states, positive_companion, leading_dimension_counts, affinity_divisor
    )
    row_losses, *grads = run_backward(sequence_token_counts, demb, loss, weights, saved)
    return (row_losses, averaged_layer_states, *grads)


def solution(mesh):
    return jax.shard_map(
        body,
        mesh=mesh,
        in_specs=(
            P(("batch", "tile"), None, None),
            P(("batch", "tile")),
            P(),
            P(),
            P(),
            P(),
            P(),
            P(),
            P(),
            P(),
            P(),
            P(),
            P(),
            P(),
            P(),
            P(),
            P(),
        ),
        out_specs=(
            P("batch"),
            P(("batch", "tile"), None, None),
            P(("batch", "tile"), None, None),
            P(None, ("batch", "tile"), None),
            P(None, ("batch", "tile")),
            P(None, ("batch", "tile"), None),
            P(None, ("batch", "tile")),
            P(None, ("batch", "tile")),
            P(None, ("batch", "tile")),
            P(None, ("batch", "tile"), None),
            P(None, ("batch", "tile")),
            P(None, ("batch", "tile"), None),
            P(None, ("batch", "tile")),
            P(None, ("batch", "tile")),
            P(None, ("batch", "tile")),
        ),
        check_vma=False,
    )
```

time: 651 us -> 189 us (0.29); the launches traced: 643 us -> 189 us
  waiting for transfers between devices: 170 us -> 0 us
  blocking collectives: 95.6 us -> 0 us
  matrix products: 81.1 us -> 0 us
  other arithmetic: 68.2 us -> 0 us
  local copies, waits for them, and re-layouts: 44.6 us -> 6.95 us
  between operations: 17.7 us -> 2.01 us
  Pallas kernels: 165 us -> 180 us
    unnamed x4 -> x0, waiting for transfers between devices: 170 us -> none
    all_gather x5 -> x0, blocking collectives: 77.3 us -> none  [the longest x3 35.8 us: combined_all(): gathered = jax.tree.map(lambda a: lax.all_gather(a, axis), part)]
    dot_general x29 -> x0, matrix products: 74 us -> none  [the longest x2 19.4 us: layer_forward(): jnp.einsum('ncm,mj->ncj', middle_reduced, expand_layer_matrix, preferred_...]
    another operation x19 -> x0, other arithmetic: 38.5 us -> none  [the longest x10 33.7 us: body(): jnp.stack([pf, pb])]
    unnamed x1 -> x0, blocking collectives: 18.3 us -> none
    pallas_call x1 -> x4, Pallas kernels: 165 us -> 180 us  [the longest x1 136 us: run_backward(): pl.pallas_call(backward_kernel, out_shape=(jax.ShapeDtypeStruct((TRIPLES,...]
    unnamed x300 -> x15, local copies, waits for them, and re-layouts: 20.9 us -> 6.19 us
    convert_element_type x14 -> x0, other arithmetic: 10 us -> none  [the longest x1 1.4 us: layer_forward(): expand_layer_shift.astype(jnp.float32)]
  transfers between devices with their start and end apart: 2 -> 0, of which waited for: 2 -> 0; matrix products, arithmetic and copies ran while one was open for 7% -> 0% of each run, Pallas kernels for 0% -> 0%
where the time goes in v3:
time: 189 us
  Pallas kernels  180 us (95%)
  local copies, waits for them, and re-layouts  6.95 us (4%)
  between operations  2.01 us (1%)
    pallas_call x1, Pallas kernels, run_backward(): pl.pallas_call(backward_kernel, out_shape=(jax.ShapeDtypeStruct((TRIPLES,...  136 us
    pallas_call x1, Pallas kernels, pairing_cost_term(): pl.pallas_call(pairing_kernel, out_shape=(jax.ShapeDtypeStruct((2, 768),...  22.7 us
    pallas_call x1, Pallas kernels, run_forward(): pl.pallas_call(forward_kernel, out_shape=[jax.ShapeDtypeStruct((1, 2, 768...  19.9 us
    unnamed x15, local copies, waits for them, and re-layouts  6.19 us

profile of v3, /device:TPU:0, one launch (start us, length us, event | category | flops | bytes accessed | tf_op | source)
XLA Modules:
  0.0 188.7 jit_solution(3137929948988117812)
XLA Ops:
  1.9 0.8 copy.34.companion_ref
  2.7 0.0 copy-start.5
  2.7 19.9 %shard_map.298 = (f32[1,2,768]{2,1,0:T(2,128)}, bf16[2,256,768]{2,1,0:T(8,128)(2,1)}, bf16[2,256,2304]{2,1,0:T(8,128)(2,1)}, bf16[2,256,768]{2,1,0:T(8,128)(2,1)...) custom-call(bf16[1,256,768]{2,1,0:T(8,128)(2,1)} %x_ref.1, ...), custom_call_target="tpu_custom_call" | custom-call | tf_op jit(solution)/shard_map/pallas_call | solution.py:210
  22.6 0.0 copy-done.5
  22.6 0.0 copy-start.3
  22.6 0.7 copy-done.3
  23.3 22.7 %shard_map.299 = (f32[2,768]{1,0:T(2,128)S(1)}, f32[128,1]{1,0:T(8,128)S(1)}) custom-call(f32[1,2,768]{2,1,0:T(2,128)S(1)} %copy-done.3, s32[128,1]{1,0:T(8,128)S(1)} %copy.34.companion_ref, s32[4]{0:T(128)S(1)} %copy-done.5, f32[1]{0:T(128)S(6)} %copy.39.divisor_ref), custom_call_target="tpu_custom_call" | custom-call | tf_op jit(solution)/shard_map/pallas_call | solution.py:331
  46.0 0.0 copy-start.2
  46.0 0.6 copy-done.2
  46.6 135.6 %shard_map.300 = (f32[12,3,4,8,128]{4,3,2,1,0:T(8,128)}, f32[2,128]{1,0:T(2,128)}, f32[1,256,768]{2,1,0:T(8,128)}) custom-call(s32[1]{0:T(128)S(6)} %copy.38.count_ref, f32[2,768]{1,0:T(2,128)} %copy-done.2, bf16[2,768]{1,0:T(2,128)(2,1)} %g1_ref.3, bf16[2,768]{1,0:T(2,128)(2,1)} %t1_ref.1, bf16[2,768]{1,0:T(2,128)(2,1)} %g2_ref.3, ...), custom_call_target="tpu_custom_call" | custom-call | tf_op jit(solution)/shard_map/pallas_call | solution.py:931
  182.2 0.0 copy-start
  182.2 1.1 copy-done
  183.3 0.0 copy-start.1
  183.3 1.1 copy-done.1
  184.4 0.0 copy-start.4
  184.4 0.6 copy-done.4
  185.0 1.6 shard_map.301
  186.6 0.6 copy.36
  187.2 0.7 copy.35
  187.9 0.8 copy.37
Async XLA Ops:
  2.7 19.9 %copy-start.5 = (s32[4]{0:T(128)S(1)}, s32[4]{0:T(128)}, u32[]{:S(2)}) copy-start(s32[4]{0:T(128)} %widths_ref.1) | copy-start | bytes 52
  22.6 0.7 copy-start.3
  46.0 0.6 copy-start.2
  182.2 1.1 copy-start
  183.3 1.1 copy-start.1
  184.4 0.6 copy-start.4

commit v4 on v3

v4 whole, which is shorter than its diff:
```python
import jax
import jax.numpy as jnp
import ml_dtypes
import numpy as np
from jax import lax
from jax.experimental import pallas as pl
from jax.experimental.pallas import tpu as pltpu
from jax.sharding import PartitionSpec as P

eps_norm = 1e-06

f32, bf16 = jnp.float32, jnp.bfloat16
MESH = pl.DeviceIdType.MESH
TRIPLES = 12
SLOTS = 3
DIRECT = 10
ORDERS = (("x", "y", "z"), ("y", "z", "x"), ("z", "x", "y"))


def my_place():
    b = lax.axis_index("batch")
    return {"z": b // 8, "x": lax.rem(b // 2, 4), "c": lax.rem(b, 2), "y": lax.axis_index("tile")}


def device_at(place):
    return {"batch": (place["z"] * 4 + place["x"]) * 2 + place["c"], "tile": place["y"]}


def neighbour(place, axis, step):
    there = dict(place)
    if axis == "c":
        there["c"] = 1 - place["c"]
    else:
        there[axis] = lax.rem(place[axis] + step + 4, 4)
    return device_at(there)


GROUP = tuple((flip, step) for flip in (0, 1) for step in range(4) if flip or step)
VECTORS = tuple((768 * k, 768, 6) for k in range(6)) + ((4608, 1536, 12), (6144, 3072, 24))


def in_group(place, flip, step):
    there = dict(place)
    there["c"] = lax.rem(place["c"] + flip, 2)
    there["y"] = lax.rem(place["y"] + step, 4)
    return device_at(there)


def gelu_parts(inner):
    half = 0.5 * (1.0 + lax.erf(inner * 0.7071067811865476))
    return inner * half, half


def lanes_of(j, width):
    return pl.ds(pl.multiple_of(j * width, width), width)


def rows_of(i, height):
    return pl.ds(pl.multiple_of(i * height, height), height)


NT = (((1,), (1,)), ((), ()))
TN = (((0,), (0,)), ((), ()))


def head_halves(pair):
    first = lax.broadcasted_iota(jnp.int32, pair.shape, 1) < 64
    nothing = jnp.zeros_like(pair)
    return jnp.concatenate([jnp.where(first, pair, nothing), jnp.where(first, nothing, pair)], axis=0)


def pair_probs(q, k, keymask):
    scores = lax.dot_general(head_halves(q * 0.125), k, NT, preferred_element_type=f32) + keymask
    expo = jnp.exp(scores - jnp.max(scores, axis=1, keepdims=True))
    return expo * (1.0 / jnp.sum(expo, axis=1, keepdims=True))


def whole_kernel(
    count_ref, companion_ref, widths_ref, divisor_ref,
    bq_ref, bo_ref, g1_ref, t1_ref, bu_ref, bd_ref, g2_ref, t2_ref,
    x_ref, wq_ref, wo_ref, wu_ref, wd_ref, perm_ref, spread_ref,
    out_ref, vec_out_ref, loss_ref, emb_ref, dx_ref,
    qkv_keep, ctx_keep, n1_keep, r1_keep, inner_keep, n2_keep, r2_keep,
    weight, perm, xb, qkv, ctx, n1, r1, inner, n2, r2, grad, d_outer, d_att, d_ctx, act_t, d_inner, d_qkv, vectors, apt,
    vq, vo, v1, t1, vu, vd, v2, t2, pool, d_emb, every,
    half, send, got0, got1a, got1b, half2, got2a, got2b, half3, got3a, got3b, rows24, got2d, got3d,
    vec_src, vec_z, vec_x, vec_mid, vec_cy,
    weight_sem, keep_sem, load_sem, table_sem, every_s, every_r, swap_s, swap_r,
    sems_s, sems_r, sem0_s, sem0_r, direct_s, direct_r, vec_s, vec_r,
):
    place = my_place()
    core = place["c"]


    kept = {
        "qkv": (qkv, qkv_keep, 0), "ctx": (ctx, ctx_keep, 1), "n1": (n1, n1_keep, 2), "r1": (r1, r1_keep, 3),
        "inner": (inner, inner_keep, 4), "n2": (n2, n2_keep, 5), "r2": (r2, r2_keep, 6),
    }

    def keep(name):
        here, there, k = kept[name]
        return pltpu.make_async_copy(here, there, keep_sem.at[k])

    def load(name):
        if name == "xb":
            return pltpu.make_async_copy(x_ref.at[0], xb, load_sem.at[7])
        here, there, k = kept[name]
        return pltpu.make_async_copy(there, here, load_sem.at[k])

    def weights(k, layer, slot):
        blocks = []
        for m in range(4):
            cols = pl.ds(768 * m, 768)
            if k == 0:
                src = wd_ref.at[layer, cols]
            elif k == 1:
                src = wu_ref.at[layer, :, cols]
            else:
                src = wq_ref.at[layer, :, cols] if m < 3 else wo_ref.at[layer]
            blocks.append(pltpu.make_async_copy(src, weight.at[slot, cols], weight_sem.at[slot, m]))
        return blocks

    def fetch_weights(k, layer, slot):
        for copy in weights(k, layer, slot):
            copy.start()

    def ready_weights(k, layer, slot):
        for copy in weights(k, layer, slot):
            copy.wait()

    def back_slot(k, layer):
        return lax.rem((1 - layer) * 3 + k + 1, 2)

    load("xb").start()
    fetch_weights(2, 0, 0)
    fetch_weights(1, 0, 1)
    perm_copy = pltpu.make_async_copy(perm_ref, perm, table_sem.at[0])
    spread_copy = pltpu.make_async_copy(spread_ref, weight.at[1, pl.ds(0, 1536)], table_sem.at[1])
    perm_copy.start()

    barrier = pltpu.get_barrier_semaphore()
    for axis in ("x", "z"):
        for step in (1, 2, 3):
            pl.semaphore_signal(barrier, inc=1, device_id=neighbour(place, axis, step), device_id_type=MESH)
    for flip, step in GROUP:
        pl.semaphore_signal(barrier, inc=1, device_id=in_group(place, flip, step), device_id_type=MESH)

    for src, dst in ((bo_ref, vo), (g1_ref, v1), (t1_ref, t1), (bu_ref, vu), (bd_ref, vd), (g2_ref, v2), (t2_ref, t2)):
        for layer in range(2):
            dst[layer] = src[layer : layer + 1, :].astype(f32)
    for layer in range(2):
        vq[layer, :, 0:768] = bq_ref[layer : layer + 1, 0:768].astype(f32)
        vq[layer, :, 768:1536] = jnp.zeros((1, 768), f32)
        vq[layer, :, 1536:2304] = bq_ref[layer : layer + 1, 768:1536].astype(f32)
    count = count_ref[0]
    keymask = jnp.where(lax.broadcasted_iota(jnp.int32, (1, 256), 1) < count, 0.0, -1e9)


    def slab(e, o, phase):
        done = ORDERS[o][:phase]
        at = tuple(pl.ds(0, 4) if axis in done else place[axis] for axis in ("z", "x", "c", "y"))
        return every.at[(e, o) + at]

    def gather_copies(e, o, phase):
        return [
            pltpu.make_async_remote_copy(
                src_ref=slab(e, o, phase), dst_ref=slab(e, o, phase),
                send_sem=every_s.at[e, o, phase, step - 1], recv_sem=every_r.at[e, o, phase, step - 1],
                device_id=neighbour(place, ORDERS[o][phase], step), device_id_type=MESH,
            )
            for step in (1, 2, 3)
        ]

    def swap_copy(e):
        mine = every.at[e, :, :, :, core]
        return pltpu.make_async_remote_copy(
            src_ref=mine, dst_ref=mine, send_sem=swap_s.at[e], recv_sem=swap_r.at[e],
            device_id=neighbour(place, "c", 1), device_id_type=MESH,
        )

    def gather_start(e):
        for o in range(3):
            for r in range(2):
                at = 256 * o + 128 * r
                every[e, o, place["z"], place["x"], core, place["y"], r : r + 1, :] = pool[e, :, at : at + 128]
            for copy in gather_copies(e, o, 0):
                copy.start()

    def gather_next(e, phase):
        for o in range(3):
            for copy in gather_copies(e, o, phase):
                copy.wait()
            if phase < 2:
                for copy in gather_copies(e, o, phase + 1):
                    copy.start()
        if phase == 2:
            swap_copy(e).start()


    def norm(z, layer, normed_ref, scaled_ref, gain, shift, rows):
        center = z - jnp.mean(z, axis=1, keepdims=True)
        scaled = lax.rsqrt(jnp.mean(center * center, axis=1, keepdims=True) + eps_norm)
        normed = center * scaled
        normed_ref[rows, :] = normed
        scaled_ref[rows, :] = scaled
        return normed * gain[layer] + shift[layer]

    def run_if(wanted):
        return (lambda job: job()) if wanted else (lambda job: None)

    def forward_layer(layer):
        is_first, is_last = layer == 0, layer == 1

        def free(*names):
            @run_if(is_last)
            def _():
                for name in names:
                    keep(name).wait()

        def store(*names):
            @run_if(is_first)
            def _():
                for name in names:
                    keep(name).start()

        @run_if(is_first)
        def _():
            load("xb").wait()
            grad[...] = xb[...].astype(f32)

        @run_if(is_last)
        def _():
            xb[...] = grad[...].astype(bf16)

        free("qkv")
        slot = (layer * 3) % 2
        blocks = weights(2, layer, slot)
        for m in range(3):
            cols = pl.ds(768 * m, 768)
            blocks[m].wait()
            mixed = jnp.dot(xb[...], weight[slot, cols, :], preferred_element_type=f32) + vq[layer, :, cols]
            qkv[:, cols] = mixed.astype(bf16)
        store("qkv")

        @run_if(is_last)
        def _():
            gather_next(0, 0)

        free("ctx")

        def attend(pair, _):
            q, k, v = (qkv[:, lanes_of(pair + 6 * third, 128)] for third in range(3))
            probs = pair_probs(q, k, keymask).astype(bf16)
            both = jnp.dot(probs, v, preferred_element_type=f32)
            first = lax.broadcasted_iota(jnp.int32, (256, 128), 1) < 64
            ctx[:, lanes_of(pair, 128)] = jnp.where(first, both[:256], both[256:]).astype(bf16)
            return 0

        lax.fori_loop(0, 6, attend, 0, unroll=6)
        store("ctx")

        @run_if(is_last)
        def _():
            gather_next(0, 1)

        blocks[3].wait()
        grad[...] += jnp.dot(ctx[...], weight[slot, 2304:3072, :], preferred_element_type=f32) + vo[layer]
        fetch_weights(0, layer, slot)
        free("n1", "r1", "n2", "r2")

        def norm_one(i, _):
            rows = rows_of(i, 64)
            mid = norm(grad[rows, :], layer, n1, r1, v1, t1, rows)
            n2[rows, :] = mid
            d_att[rows, :] = mid.astype(bf16)
            return 0

        lax.fori_loop(0, 4, norm_one, 0, unroll=4)
        store("n1", "r1")
        free("inner")
        slot = (layer * 3 + 1) % 2
        blocks = weights(1, layer, slot)
        for m in range(4):
            cols = pl.ds(768 * m, 768)
            blocks[m].wait()
            value = jnp.dot(d_att[...], weight[slot, cols, :], preferred_element_type=f32) + vu[layer, :, cols]
            inner[:, cols] = value
            d_inner[:, cols] = gelu_parts(value)[0].astype(bf16)
        store("inner")

        @run_if(is_first)
        def _():
            fetch_weights(2, 1, slot)

        @run_if(is_last)
        def _():
            gather_next(0, 2)

        slot = (layer * 3 + 2) % 2
        ready_weights(0, layer, slot)
        n2[...] += jnp.dot(d_inner[...], weight[slot], preferred_element_type=f32) + vd[layer]

        @run_if(is_first)
        def _():
            fetch_weights(1, 1, slot)

        def norm_two(i, total):
            rows = rows_of(i, 64)
            result = norm(n2[rows, :], layer, n2, r2, v2, t2, rows)
            grad[rows, :] = result
            spot = lax.broadcasted_iota(jnp.int32, (64, 1), 0) + i * 64
            return total + jnp.sum(jnp.where(spot < count, result, 0.0), axis=0, keepdims=True)

        total = lax.fori_loop(0, 4, norm_two, jnp.zeros((1, 768), f32), unroll=4)
        pool[layer] = total / count.astype(f32)
        store("n2", "r2")

        @run_if(is_first)
        def _():
            pl.semaphore_wait(barrier, 13)
            gather_start(0)

        @run_if(is_last)
        def _():
            swap_copy(0).wait()
            gather_start(1)


    def pairing(e, loss):
        me = ((place["z"] * 4 + place["x"]) * 2 + core) * 4 + place["y"]
        row = lax.broadcasted_iota(jnp.int32, (128, 128), 0)
        col = lax.broadcasted_iota(jnp.int32, (128, 128), 1)
        rows = lax.broadcasted_iota(jnp.int32, (128, 1), 0)
        lane = lax.broadcasted_iota(jnp.int32, (1, 768), 1)
        companion = companion_ref[...]
        divisor = divisor_ref[0]
        partner = (row == companion).astype(f32)
        mine = jnp.sum(jnp.where(lax.broadcasted_iota(jnp.int32, (1, 128), 1) == me, companion, 0), axis=1, keepdims=True)
        chosen = (rows == mine).astype(f32)
        is_me = rows == me
        embed = jnp.concatenate(
            [every[e, o].reshape(128, 2, 128)[:, r, :] for o in range(3) for r in range(2)], axis=1
        )
        high = embed.astype(bf16)
        low = (embed - high.astype(f32)).astype(bf16)
        own = pool[e]
        total = jnp.zeros((1, 768), f32)
        for p in range(4):
            keep_p = (lane < widths_ref[p]).astype(f32)
            keep_low = keep_p.astype(bf16)
            high_p, low_p = high * keep_low, low * keep_low
            gram = (
                lax.dot_general(high_p, high, NT, preferred_element_type=f32)
                + lax.dot_general(high_p, low, NT, preferred_element_type=f32)
                + lax.dot_general(low_p, high, NT, preferred_element_type=f32)
            )
            diagonal = jnp.where(row == col, gram, 0.0)
            inverse = lax.rsqrt(jnp.sum(diagonal, axis=1, keepdims=True) + eps_norm)
            inverse_row = lax.rsqrt(jnp.sum(diagonal, axis=0, keepdims=True) + eps_norm)
            sims = gram * inverse * inverse_row / divisor
            sims = jnp.where(row == col, -1e30, sims)
            top = jnp.max(sims, axis=1, keepdims=True)
            lse = top + jnp.log(jnp.sum(jnp.exp(sims - top), axis=1, keepdims=True))
            loss = loss + (lse - jnp.sum(sims * partner, axis=1, keepdims=True))
            to_me = jnp.sum(jnp.where(col == me, sims, 0.0), axis=1, keepdims=True)
            lse_me = jnp.sum(jnp.where(is_me, lse, 0.0), axis=0, keepdims=True)
            weight_j = jnp.exp(to_me - lse_me) + jnp.exp(to_me - lse) - 2.0 * chosen
            dunit = jnp.sum(embed * (weight_j * inverse), axis=0, keepdims=True) * keep_p
            inverse_me = jnp.sum(jnp.where(is_me, inverse, 0.0), axis=0, keepdims=True)
            unit_me = own * keep_p * inverse_me
            inside = dunit - unit_me * jnp.sum(unit_me * dunit, axis=1, keepdims=True)
            total = total + inside * inverse_me
        d_emb[e] = total / (8.0 * divisor)
        return loss


    def norm_back(normed, scaled, gain, rounded, at_gain, at_shift, at_bias, layer):
        sums = [jnp.zeros((1, 768), f32) for _ in range(3)]
        for i in range(4):
            rows = pl.ds(64 * i, 64)
            dy, n = grad[rows, :], normed[rows, :]
            dn = dy * gain
            inside = dn - jnp.mean(dn, axis=1, keepdims=True) - n * jnp.mean(dn * n, axis=1, keepdims=True)
            dz = scaled[rows, :] * inside
            low = dz.astype(bf16)
            grad[rows, :] = dz
            rounded[rows, :] = low
            for k, term in enumerate((dy * n, dy, low.astype(f32))):
                sums[k] = sums[k] + jnp.sum(term, axis=0, keepdims=True)
        for at, total in zip((at_gain, at_shift, at_bias), sums):
            vectors[layer, :, at : at + 768] = total

    def turn_active():
        def turn(j, _):
            value = inner[:, lanes_of(j, 256)]
            act_t[lanes_of(j, 256), :] = gelu_parts(value)[0].T.astype(bf16)
            return 0

        lax.fori_loop(0, 12, turn, 0, unroll=2)

    def permute(operand, which):
        for o in range(3):
            apt[o, which] = lax.dot_general(perm[o], operand, NT, preferred_element_type=f32).astype(bf16)

    def begin_layer(layer):
        spots = lax.broadcasted_iota(jnp.int32, (256, 1), 0)
        pooled = jnp.where(spots < count, 1.0, 0.0) / count.astype(f32)

        @pl.when(layer == 1)
        def _():
            grad[...] = pooled * d_emb[1]

        @pl.when(layer == 0)
        def _():
            grad[...] += pooled * d_emb[0]
            load("n2").wait()
            load("r2").wait()
            load("inner").wait()
            turn_active()

        norm_back(n2, r2, v2[layer], d_outer, 3072, 3840, 2304, layer)

        @pl.when(layer == 1)
        def _():
            load("n2").start()
            load("r2").start()

    def through_expand(layer):
        slot = back_slot(0, layer)

        @pl.when(layer == 0)
        def _():
            ready_weights(0, 0, slot)

        def chunk(j, _):
            cols = lanes_of(j, 512)
            d_act = lax.dot_general(d_outer[...], weight[slot, cols, :], NT, preferred_element_type=f32)
            value = inner[:, cols]
            slope = gelu_parts(value)[1] + value * (jnp.exp(-0.5 * value * value) * 0.3989422804014327)
            low = (d_act * slope).astype(bf16)
            d_inner[:, cols] = low
            at = pl.ds(pl.multiple_of(6144 + j * 512, 512), 512)
            vectors[layer, :, at] = jnp.sum(low.astype(f32), axis=0, keepdims=True)
            return 0

        lax.fori_loop(0, 6, chunk, 0, unroll=2)
        fetch_weights(2, layer, slot)

        @pl.when(layer == 1)
        def _():
            load("inner").start()

        @pl.when(layer == 0)
        def _():
            load("n1").wait()
            load("r1").wait()
            permute((n1[...] * v1[0] + t1[0]).astype(bf16), 0)

    def through_mixer(layer):
        slot = back_slot(1, layer)

        @pl.when(layer == 0)
        def _():
            ready_weights(1, 0, slot)

        for m in range(4):
            cols = pl.ds(768 * m, 768)
            grad[...] += lax.dot_general(d_inner[:, cols], weight[slot, cols, :], NT, preferred_element_type=f32)
        norm_back(n1, r1, v1[layer], d_att, 768, 1536, 0, layer)

        @pl.when(layer == 1)
        def _():
            fetch_weights(0, 0, slot)
            load("n1").start()
            load("r1").start()

        slot = back_slot(2, layer)
        ready_weights(2, layer, slot)
        d_ctx[...] = lax.dot_general(d_att[...], weight[slot, 2304:3072, :], NT, preferred_element_type=f32).astype(bf16)

    def through_attention(layer, first_pair, pairs):
        def pair_back(i, _):
            pair = first_pair + i
            at = [lanes_of(pair + 6 * third, 128) for third in range(3)]
            q, k, v = (qkv[:, cols] for cols in at)
            probs = pair_probs(q, k, keymask)
            dc = head_halves(d_ctx[:, at[0]])
            dp = lax.dot_general(dc, v, NT, preferred_element_type=f32)
            ds = (probs * (dp - jnp.sum(dp * probs, axis=1, keepdims=True))).astype(bf16)
            dq = jnp.dot(
                jnp.concatenate([ds[:256], ds[256:]], axis=1), head_halves(k * 0.125), preferred_element_type=f32
            ).astype(bf16)
            dk = lax.dot_general(ds, head_halves(q * 0.125), TN, preferred_element_type=f32).astype(bf16)
            dv = lax.dot_general(probs.astype(bf16), dc, TN, preferred_element_type=f32).astype(bf16)
            for cols, value in zip(at, (dq, dk, dv)):
                d_qkv[:, cols] = value
            for start, value in ((4608, dq), (5376, dv)):
                where = pl.ds(pl.multiple_of(start + pair * 128, 128), 128)
                vectors[layer, :, where] = jnp.sum(value.astype(f32), axis=0, keepdims=True)
            return 0

        lax.fori_loop(0, pairs, pair_back, 0, unroll=2)

    def through_projection(layer):
        slot = back_slot(2, layer)
        for m in range(3):
            cols = pl.ds(768 * m, 768)
            grad[...] += lax.dot_general(d_qkv[:, cols], weight[slot, cols, :], NT, preferred_element_type=f32)

        @pl.when(layer == 1)
        def _():
            fetch_weights(1, 0, slot)
            load("qkv").start()

        @pl.when(layer == 0)
        def _():
            dx_copy.start()

    dx_copy = pltpu.make_async_copy(grad, dx_ref.at[0], table_sem.at[2])

    def store_rows(o, slot, mine, tile0, value):
        for j in range(value.shape[1] // 128):
            part = value[:, 128 * j : 128 * (j + 1)].reshape(16, 3, 8, 128)
            if mine:
                half[o, slot, :, tile0 + 3 * j : tile0 + 3 * j + 3] = part
            else:
                send[o, :, tile0 + 3 * j : tile0 + 3 * j + 3] = part

    def product(o, slot, which, ref, at, width, tile0):
        for mine in (False, True):
            c = core if mine else 1 - core
            lhs = apt[o, which, pl.ds(pl.multiple_of(c * 384, 128), 384), :]
            for w in range(0, width, 256):
                value = jnp.dot(lhs, ref[:, at + w : at + w + 256], preferred_element_type=f32)
                store_rows(o, slot, mine, tile0 + 3 * (w // 128), value)

    def product_shrink(slot, k):
        def block(z, _):
            for mine in (False, True):
                c = core if mine else 1 - core
                lhs = jnp.concatenate(
                    [act_t[pl.ds(pl.multiple_of(z * 768 + x * 192 + c * 96, 32), 96), :] for x in range(4)], axis=0
                )
                value = jnp.dot(lhs, d_outer[:, 384 * k : 384 * (k + 1)], preferred_element_type=f32)
                for x in range(4):
                    for y in range(4):
                        for j in range(3):
                            p = {"x": x, "y": y, "z": z}
                            d1, d2, d3 = (p[axis] for axis in ORDERS[j])
                            row = x * 96 + (y * 3 + j) * 8
                            for ct in range(3):
                                tile = value[row : row + 8, 128 * ct : 128 * ct + 128]
                                if mine:
                                    half[j, slot, d1 * 4 + d2, d3 * 3 + ct] = tile
                                else:
                                    send[j, d1 * 4 + d2, d3 * 3 + ct] = tile
            return 0

        lax.fori_loop(0, 4, block, 0)

    def make(u):
        slot = lax.rem(u, SLOTS)
        layer = 1 - u // 6
        kind = lax.rem(u, 6)

        def to_other_core(o):
            copy0(o, u).start()

        @pl.when(kind == 0)
        def _():
            begin_layer(layer)
            product_shrink(slot, 0)
            for o in range(3):
                to_other_core(o)

        @pl.when(kind == 1)
        def _():
            product_shrink(slot, 1)
            for o in range(3):
                to_other_core(o)

        for k in range(2):
            @pl.when(kind == 2 + k)
            def _():
                for o in range(3):
                    product(o, slot, 0, d_inner, (k * 3 + o) * 512, 512, 0)
                    to_other_core(o)

        @pl.when(kind == 4)
        def _():
            for o in range(3):
                product(o, slot, 0, d_qkv, o * 768, 512, 0)
                to_other_core(o)

        @pl.when(kind == 5)
        def _():
            for o in range(3):
                product(o, slot, 0, d_qkv, o * 768 + 512, 256, 0)
                product(o, slot, 1, d_att, o * 256, 256, 6)
                to_other_core(o)

    def follow(u):
        layer = 1 - u // 6
        kind = lax.rem(u, 6)

        @pl.when(kind == 1)
        def _():
            through_expand(layer)

        @pl.when(kind == 2)
        def _():
            through_mixer(layer)

        @pl.when(kind == 3)
        def _():
            @pl.when(layer == 0)
            def _():
                load("xb").wait()
                load("ctx").wait()

            permute(xb[...], 0)
            permute(ctx[...], 1)

            @pl.when(layer == 1)
            def _():
                load("xb").start()
                load("ctx").start()

            @pl.when(layer == 0)
            def _():
                load("qkv").wait()

            through_attention(layer, 0, 4)

        @pl.when(kind == 4)
        def _():
            through_attention(layer, 4, 2)
            through_projection(layer)


    def exchange(o, k, slot, src_up, src_down, got):
        axis = ORDERS[o][k // 2]
        return [
            pltpu.make_async_remote_copy(
                src_ref=src, dst_ref=got.at[o, slot, way],
                send_sem=sems_s.at[o, k, way, slot], recv_sem=sems_r.at[o, k, way, slot],
                device_id=neighbour(place, axis, step), device_id_type=MESH,
            )
            for way, (src, step) in enumerate(((src_up, 1), (src_down, -1)))
        ]

    def spots(o, phase):
        a = place[ORDERS[o][phase]]
        return a, lax.rem(a + 1, 4), lax.rem(a + 2, 4), lax.rem(a + 3, 4)

    def copy0(o, u):
        slot = lax.rem(u, 2)
        return pltpu.make_async_remote_copy(
            src_ref=send.at[o], dst_ref=got0.at[o, slot], send_sem=sem0_s.at[o], recv_sem=sem0_r.at[o, slot],
            device_id=neighbour(place, "c", 1), device_id_type=MESH,
        )

    def step_a(o, phase, u):
        slot = lax.rem(u, SLOTS)
        a, up, far, down = spots(o, phase)
        if phase == 0:
            src, got = (half.at[o, slot, pl.ds(far * 4, 2)], half.at[o, slot, pl.ds(far * 4 + 2, 2)]), got1a
        elif phase == 1:
            src, got = (half2.at[o, slot, far, pl.ds(0, 6)], half2.at[o, slot, far, pl.ds(6, 6)]), got2a
        else:
            src, got = (half3.at[o, slot, far, pl.ds(0, 2)], half3.at[o, slot, far, pl.ds(2, 2)]), got3a
        return exchange(o, 2 * phase, slot, src[0], src[1], got)

    def step_b(o, phase, u):
        slot = lax.rem(u, SLOTS)
        a, up, far, down = spots(o, phase)
        if phase == 0:
            src, got = (half.at[o, slot, pl.ds(up * 4, 4)], half.at[o, slot, pl.ds(down * 4, 4)]), got1b
        elif phase == 1:
            src, got = (half2.at[o, slot, up], half2.at[o, slot, down]), got2b
        else:
            src, got = (half3.at[o, slot, up], half3.at[o, slot, down]), got3b
        return exchange(o, 2 * phase + 1, slot, src[0], src[1], got)

    def add_a(o, phase, u):
        slot = lax.rem(u, SLOTS)
        a, up, far, down = spots(o, phase)
        if phase == 0:
            for i in range(2):
                half[o, slot, up * 4 + i] += got1a[o, slot, 0, i]
                half[o, slot, down * 4 + 2 + i] += got1a[o, slot, 1, i]
        elif phase == 1:
            half2[o, slot, up, 0:6] += got2a[o, slot, 0]
            half2[o, slot, down, 6:12] += got2a[o, slot, 1]
        else:
            half3[o, slot, up, 0:2] += got3a[o, slot, 0]
            half3[o, slot, down, 2:4] += got3a[o, slot, 1]

    def add_b(o, phase, u):
        slot = lax.rem(u, SLOTS)
        a, up, far, down = spots(o, phase)
        if phase == 0:
            for i in range(4):
                half2[o, slot, i] = half[o, slot, a * 4 + i] + got1b[o, slot, 0, i] + got1b[o, slot, 1, i]
        elif phase == 1:
            to_third(o, slot, u, half2[o, slot, a] + got2b[o, slot, 0] + got2b[o, slot, 1])
        else:
            out_ref[u, o] = half3[o, slot, a] + got3b[o, slot, 0] + got3b[o, slot, 1]

    def to_third(o, slot, u, total):
        @pl.when(lax.rem(u, 6) < 2)
        def _():
            for k in range(4):
                half3[o, slot, k, 0:3] = total[3 * k : 3 * k + 3]

        @pl.when(lax.rem(u, 6) >= 2)
        def _():
            for ct in range(4):
                rows24[o, ct] = total[3 * ct : 3 * ct + 3].reshape(24, 128)
            for k in range(4):
                for ct in range(4):
                    half3[o, slot, k, ct, 0:6, :] = rows24[o, ct, 6 * k : 6 * k + 6, :]

    def direct(o, phase, u):
        slot, way = lax.rem(u, SLOTS), lax.rem(u, 2)
        a = place[ORDERS[o][phase]]
        src, got = ((half2, got2d), (half3, got3d))[phase - 1]
        return [
            pltpu.make_async_remote_copy(
                src_ref=src.at[o, slot, lax.rem(a + step, 4)], dst_ref=got.at[o, way, step - 1],
                send_sem=direct_s.at[o, phase - 1, way, step - 1], recv_sem=direct_r.at[o, phase - 1, way, step - 1],
                device_id=neighbour(place, ORDERS[o][phase], step), device_id_type=MESH,
            )
            for step in (1, 2, 3)
        ]

    def direct_second(u):
        slot, way = lax.rem(u, SLOTS), lax.rem(u, 2)
        for o in range(3):
            for copy in direct(o, 1, u):
                copy.wait()
            total = half2[o, slot, place[ORDERS[o][1]]]
            for i in range(3):
                total += got2d[o, way, i]
            to_third(o, slot, u, total)
            for copy in direct(o, 2, u):
                copy.start()

    def direct_third(u):
        slot, way = lax.rem(u, SLOTS), lax.rem(u, 2)
        for o in range(3):
            for copy in direct(o, 2, u):
                copy.wait()
            total = half3[o, slot, place[ORDERS[o][2]]]
            for i in range(3):
                total += got3d[o, way, i]
            out_ref[u, o] = total

    def spread_vectors():
        for layer in range(2):
            total = jnp.zeros((128, 128), f32)
            for start, width, keep in VECTORS:
                d = lax.broadcasted_iota(jnp.int32, (128, width), 0) * keep
                q = lax.broadcasted_iota(jnp.int32, (128, width), 1)
                own = jnp.where((q >= d) & (q < d + keep), vectors[layer, :, start : start + width], 0.0)
                high = own.astype(bf16)
                low = (own - high.astype(f32)).astype(bf16)
                for part in range(width // 768):
                    k = start // 768 + part
                    lanes = weight[1, 768 * (k // 6) : 768 * (k // 6 + 1), 128 * (k % 6) : 128 * (k % 6 + 1)]
                    at = slice(768 * part, 768 * (part + 1))
                    total += jnp.dot(high[:, at], lanes, preferred_element_type=f32)
                    total += jnp.dot(low[:, at], lanes, preferred_element_type=f32)
            total = total.reshape(4, 4, 8, 128)
            for z in range(4):
                for x in range(4):
                    vec_src[z, x, layer] = total[z, x]

    def vector_copy(k, src, dst, device):
        return pltpu.make_async_remote_copy(
            src_ref=src, dst_ref=dst, send_sem=vec_s.at[k], recv_sem=vec_r.at[k], device_id=device, device_id_type=MESH
        )

    def copies_z():
        return [
            vector_copy(i, vec_src.at[lax.rem(place["z"] + i + 1, 4)], vec_z.at[i], neighbour(place, "z", i + 1))
            for i in range(3)
        ]

    def copies_x():
        return [
            vector_copy(3 + i, vec_src.at[place["z"], lax.rem(place["x"] + i + 1, 4)], vec_x.at[i], neighbour(place, "x", i + 1))
            for i in range(3)
        ]

    def copies_group():
        return [
            vector_copy(6 + i, vec_mid, vec_cy.at[i], in_group(place, flip, step))
            for i, (flip, step) in enumerate(GROUP)
        ]

    def vectors_start():
        spread_copy.wait()
        spread_vectors()
        for copy in copies_z():
            copy.start()

    def vectors_second():
        for copy in copies_z():
            copy.wait()
        for x in range(4):
            vec_src[place["z"], x] += vec_z[0, x] + vec_z[1, x] + vec_z[2, x]
        for copy in copies_x():
            copy.start()

    def vectors_third():
        for copy in copies_x():
            copy.wait()
        vec_mid[...] = vec_src[place["z"], place["x"]] + vec_x[0] + vec_x[1] + vec_x[2]
        for copy in copies_group():
            copy.start()

    def vectors_last():
        for copy in copies_group():
            copy.wait()
        total = vec_mid[...]
        for i in range(7):
            total += vec_cy[i]
        mine = lax.broadcasted_iota(jnp.int32, (2, 8, 128), 1) == core * 4 + place["y"]
        vec_out_ref[...] = jnp.sum(jnp.where(mine, total, 0.0), axis=1)

    def when(u, first, last, job):
        @pl.when((u >= first) & (u < last))
        def _():
            job(u)

    def enter(u):
        slot = lax.rem(u, SLOTS)
        for o in range(3):
            copy0(o, u).wait()

            def add(i, _):
                half[o, slot, i] += got0[o, lax.rem(u, 2), i]
                return 0

            lax.fori_loop(0, 16, add, 0)
            for copy in step_a(o, 0, u):
                copy.start()

    def second(phase):
        def job(u):
            for o in range(3):
                for copy in step_a(o, phase, u):
                    copy.wait()
                add_a(o, phase, u)
                for copy in step_b(o, phase, u):
                    copy.start()
        return job

    def third(phase):
        def job(u):
            for o in range(3):
                for copy in step_b(o, phase, u):
                    copy.wait()
                add_b(o, phase, u)
                if phase == 0:
                    @pl.when(u < DIRECT)
                    def _():
                        for copy in step_a(o, 1, u):
                            copy.start()

                    @pl.when(u >= DIRECT)
                    def _():
                        for copy in direct(o, 1, u):
                            copy.start()
                elif phase == 1:
                    for copy in step_a(o, 2, u):
                        copy.start()
        return job

    def tick(u, _):
        when(u, 0, TRIPLES, make)
        when(u - 1, 0, TRIPLES, second(0))
        when(u - 2, 0, TRIPLES, third(0))
        when(u - 3, 0, DIRECT, second(1))
        when(u - 6, 0, DIRECT, third(2))
        when(u - 3, DIRECT, TRIPLES, direct_second)
        when(u - 4, 0, DIRECT, third(1))
        when(u - 4, DIRECT, TRIPLES, direct_third)
        when(u - 5, 0, DIRECT, second(2))
        when(u, 0, TRIPLES, enter)
        when(u, 0, TRIPLES, follow)

        @pl.when(u == TRIPLES - 1)
        def _():
            spread_copy.start()

        for k, job in enumerate((vectors_start, vectors_second, vectors_third, vectors_last)):
            pl.when(u == TRIPLES + k)(job)
        return 0


    forward_layer(0)
    forward_layer(1)
    for layer in range(2):
        emb_ref[0, layer : layer + 1, :] = pool[layer]
    half3[...] = jnp.zeros_like(half3)
    loss = pairing(0, jnp.zeros((128, 1), f32))
    gather_next(1, 0)
    turn_active()
    gather_next(1, 1)
    perm_copy.wait()
    permute(d_att[...], 0)
    gather_next(1, 2)
    swap_copy(1).wait()
    loss = pairing(1, loss)
    loss_ref[...] = loss / 8.0
    lax.fori_loop(0, DIRECT + 6, tick, 0)
    dx_copy.wait()


def permutations():
    rows = np.arange(768).reshape(4, 4, 2, 4, 6)
    names = {"z": 0, "x": 1, "c": 2, "y": 3}
    out = np.zeros((3, 768, 768), np.float32)
    for o, (d1, d2, d3) in enumerate(ORDERS):
        taken = rows.transpose(2, names[d1], names[d2], names[d3], 4).reshape(-1)
        out[o, np.arange(768), taken] = 1
    return out.astype(ml_dtypes.bfloat16)


def lane_places():
    out = np.zeros((9216, 128), np.float32)
    lane = 0
    for start, width, keep in VECTORS:
        q = np.arange(width)
        out[start + q, lane + q % keep] = 1
        lane += keep
    out = out.reshape(2, 6, 768, 128).transpose(0, 2, 1, 3).reshape(1536, 768)
    return out.astype(ml_dtypes.bfloat16)


def finish_kernel(out_hbm, vec_hbm, loss_hbm, dx_hbm, *refs):
    loss_out, dx_out, qkv_out, qv_out, mixer_out, bias_out, gain_out, shift_out, up_out, ffn_out, down_out, downbias_out, fingain_out, finshift_out = refs[:14]
    out_ref, vec_ref, loss_ref, sem = refs[14:]
    copies = [
        pltpu.make_async_copy(src, dst, sem.at[k])
        for k, (src, dst) in enumerate(((out_hbm, out_ref), (vec_hbm, vec_ref), (loss_hbm, loss_ref), (dx_hbm, dx_out)))
    ]
    for copy in copies:
        copy.start()
    for copy in copies[:3]:
        copy.wait()
    for layer in range(2):
        first = 6 * (1 - layer)
        for k in range(2):
            for o in range(3):
                for ct in range(3):
                    down_out[layer, 8 * o : 8 * o + 8, 384 * k + 128 * ct : 384 * k + 128 * ct + 128] = out_ref[first + k, o, ct]
                for ct in range(4):
                    at = (k * 3 + o) * 512 + 128 * ct
                    up_out[:, layer, at : at + 128] = out_ref[first + 2 + k, o, ct, 0:6, :]
        for o in range(3):
            for ct in range(4):
                at = o * 768 + 128 * ct
                qkv_out[:, layer, at : at + 128] = out_ref[first + 4, o, ct, 0:6, :]
            for ct in range(2):
                at = o * 768 + 512 + 128 * ct
                qkv_out[:, layer, at : at + 128] = out_ref[first + 5, o, ct, 0:6, :]
                at = o * 256 + 128 * ct
                mixer_out[:, layer, at : at + 128] = out_ref[first + 5, o, 2 + ct, 0:6, :]
    lane = 0
    for (_, _, keep), dst in zip(
        VECTORS, (bias_out, gain_out, shift_out, downbias_out, fingain_out, finshift_out, qv_out, ffn_out)
    ):
        dst[...] = vec_ref[:, lane : lane + keep]
        lane += keep
    rows = lax.broadcasted_iota(jnp.int32, (128, 1), 0)
    for k in range(4):
        loss_out[k] = jnp.sum(jnp.where(rows == lax.axis_index("batch") * 4 + k, loss_ref[...], 0.0))
    copies[3].wait()


def body(slots, counts, companion, widths, divisor, triple, bias_qv, mixer, bias_mixer, gain_one, shift_one, expand, bias_expand, shrink, bias_shrink, gain_two, shift_two):
    tile = (8, 128)
    vmem = pl.BlockSpec(memory_space=pltpu.VMEM)
    smem = pl.BlockSpec(memory_space=pltpu.SMEM)
    hbm = pl.BlockSpec(memory_space=pl.ANY)

    def vm(*shape, dtype=f32):
        return pltpu.VMEM(shape, dtype)

    dma = pltpu.SemaphoreType.DMA
    saved = [((256, 2304), bf16), ((256, 768), bf16), ((256, 768), f32), ((256, 1), f32), ((256, 3072), f32), ((256, 768), f32), ((256, 1), f32)]
    shapes = [((TRIPLES, 3, 4) + tile, f32), ((2, 128), f32), ((128, 1), f32), ((1, 2, 768), f32), ((1, 256, 768), f32)] + saved
    results = pl.pallas_call(
        whole_kernel,
        out_shape=[jax.ShapeDtypeStruct(s, t) for s, t in shapes],
        in_specs=[smem, vmem, smem, smem] + [vmem] * 8 + [hbm] * 7,
        out_specs=[vmem] * 4 + [hbm] * 8,
        scratch_shapes=[
            vm(2, 3072, 768, dtype=bf16), vm(3, 768, 768, dtype=bf16), vm(256, 768, dtype=bf16), vm(256, 2304, dtype=bf16),
            vm(256, 768, dtype=bf16), vm(256, 768), vm(256, 1), vm(256, 3072), vm(256, 768), vm(256, 1), vm(256, 768),
            vm(256, 768, dtype=bf16), vm(256, 768, dtype=bf16), vm(256, 768, dtype=bf16), vm(3072, 256, dtype=bf16),
            vm(256, 3072, dtype=bf16), vm(256, 2304, dtype=bf16), vm(2, 1, 9216), vm(3, 2, 768, 256, dtype=bf16),
            vm(2, 1, 2304), vm(2, 1, 768), vm(2, 1, 768), vm(2, 1, 768), vm(2, 1, 3072), vm(2, 1, 768), vm(2, 1, 768), vm(2, 1, 768),
            vm(2, 1, 768), vm(2, 1, 768), vm(2, 3, 4, 4, 2, 4, 2, 128),
            vm(3, SLOTS, 16, 12, *tile), vm(3, 16, 12, *tile), vm(3, 2, 16, 12, *tile),
            vm(3, SLOTS, 2, 2, 12, *tile), vm(3, SLOTS, 2, 4, 12, *tile),
            vm(3, SLOTS, 4, 12, *tile), vm(3, SLOTS, 2, 6, *tile), vm(3, SLOTS, 2, 12, *tile),
            vm(3, SLOTS, 4, 4, *tile), vm(3, SLOTS, 2, 2, *tile), vm(3, SLOTS, 2, 4, *tile), vm(3, 4, 24, 128),
            vm(3, 2, 3, 12, *tile), vm(3, 2, 3, 4, *tile),
            vm(4, 4, 2, *tile), vm(3, 4, 2, *tile), vm(3, 2, *tile), vm(2, *tile), vm(7, 2, *tile),
            dma((2, 4)), dma((7,)), dma((8,)), dma((3,)), dma((2, 3, 3, 3)), dma((2, 3, 3, 3)), dma((2,)), dma((2,)),
            dma((3, 6, 2, SLOTS)), dma((3, 6, 2, SLOTS)), dma((3,)), dma((3, 2)), dma((3, 2, 2, 3)), dma((3, 2, 2, 3)),
            dma((13,)), dma((13,)),
        ],
        compiler_params=pltpu.CompilerParams(
            collective_id=1, has_side_effects=True, vmem_limit_bytes=63 * 1024 * 1024
        ),
    )(
        counts, companion[None], widths, divisor,
        bias_qv, bias_mixer, gain_one, shift_one, bias_expand, bias_shrink, gain_two, shift_two,
        slots, triple, mixer, expand, shrink, jnp.asarray(permutations()), jnp.asarray(lane_places()),
    )
    out, vec_out, loss, embeddings, dx = results[:5]
    shapes = [(4,), (1, 256, 768), (6, 2, 2304), (2, 12), (6, 2, 768), (2, 6), (2, 6), (2, 6), (6, 2, 3072), (2, 24), (2, 24, 768), (2, 6), (2, 6), (2, 6)]
    loss, *rest = pl.pallas_call(
        finish_kernel,
        out_shape=[jax.ShapeDtypeStruct(s, f32) for s in shapes],
        in_specs=[hbm] * 4,
        out_specs=[smem, hbm] + [vmem] * 12,
        scratch_shapes=[vm(TRIPLES, 3, 4, *tile), vm(2, 128), vm(128, 1), dma((4,))],
        compiler_params=pltpu.CompilerParams(vmem_limit_bytes=32 * 1024 * 1024),
    )(out, vec_out, loss, dx)
    rest = [r.transpose(1, 0, 2) if r.shape[:2] == (6, 2) else r for r in rest]
    return (loss, embeddings, *rest)


def solution(mesh):
    return jax.shard_map(
        body,
        mesh=mesh,
        in_specs=(
            P(("batch", "tile"), None, None),
            P(("batch", "tile")),
            P(),
            P(),
            P(),
            P(),
            P(),
            P(),
            P(),
            P(),
            P(),
            P(),
            P(),
            P(),
            P(),
            P(),
            P(),
        ),
        out_specs=(
            P("batch"),
            P(("batch", "tile"), None, None),
            P(("batch", "tile"), None, None),
            P(None, ("batch", "tile"), None),
            P(None, ("batch", "tile")),
            P(None, ("batch", "tile"), None),
            P(None, ("batch", "tile")),
            P(None, ("batch", "tile")),
            P(None, ("batch", "tile")),
            P(None, ("batch", "tile"), None),
            P(None, ("batch", "tile")),
            P(None, ("batch", "tile"), None),
            P(None, ("batch", "tile")),
            P(None, ("batch", "tile")),
            P(None, ("batch", "tile")),
        ),
        check_vma=False,
    )
```

time: 189 us -> 206 us (1.090); the launches traced: 189 us -> 202 us
  Pallas kernels: 180 us -> 195 us
    pallas_call x4 -> x2, Pallas kernels: 180 us -> 195 us  [the longest x1 193 us: body(): pl.pallas_call(whole_kernel, out_shape=[jax.ShapeDtypeStruct(s, t) for s,...]
    unnamed x15 -> x9, local copies, waits for them, and re-layouts: 6.19 us -> 4.94 us
where the time goes in v4:
time: 206 us; the launch traced here: 202 us
  Pallas kernels  195 us (95%)
  local copies, waits for them, and re-layouts  4.94 us (2%)
  between operations  2.16 us (1%)
    pallas_call x1, Pallas kernels, body(): pl.pallas_call(whole_kernel, out_shape=[jax.ShapeDtypeStruct(s, t) for s,...  193 us
    unnamed x9, local copies, waits for them, and re-layouts  4.94 us

profile of v4, /device:TPU:0, one launch (start us, length us, event | category | flops | bytes accessed | tf_op | source)
XLA Modules:
  0.0 202.5 jit_solution(12479196320728843)
XLA Ops:
  1.9 193.4 %shard_map.298 = (f32[12,3,4,8,128]{4,3,2,1,0:T(8,128)}, f32[2,128]{1,0:T(2,128)}, f32[128,1]{1,0:T(8,128)}, f32[1,2,768]{2,1,0:T(2,128)}, f32[1,256,768]{2,1,0:...) custom-call(s32[1]{0:T(128)S(6)} %copy.35.count_ref, ...), custom_call_target="tpu_custom_call" | custom-call | tf_op jit(solution)/shard_map/pallas_call | solution.py:996
  195.4 0.0 copy-start
  195.4 1.1 copy-done
  196.5 0.0 copy-start.1
  196.5 1.1 copy-done.1
  197.6 0.0 copy-start.2
  197.6 0.8 copy-done.2
  198.4 0.0 copy-start.3
  198.4 0.6 copy-done.3
  199.1 1.9 shard_map.299
  201.0 1.3 copy.37
Async XLA Ops:
  195.4 1.1 copy-start
  196.5 1.1 copy-start.1
  197.6 0.8 copy-start.2
  198.4 0.6 copy-start.3

commit v5 on v4

--- a/solution.py
+++ b/solution.py
@@ -39,6 +39,19 @@
 VECTORS = tuple((768 * k, 768, 6) for k in range(6)) + ((4608, 1536, 12), (6144, 3072, 24))
 
 
+CHIPS = sorted(
+    ((z, x, y) for z in range(4) for x in range(4) for y in range(4) if z or x or y),
+    key=lambda steps: -sum(min(step, 4 - step) for step in steps),
+)
+
+
+def chip_at(place, steps):
+    there = dict(place)
+    for axis, step in zip("zxy", steps):
+        there[axis] = lax.rem(place[axis] + step, 4)
+    return device_at(there)
+
+
 def in_group(place, flip, step):
     there = dict(place)
     there["c"] = lax.rem(place["c"] + flip, 2)
@@ -79,17 +92,18 @@
     count_ref, companion_ref, widths_ref, divisor_ref,
     bq_ref, bo_ref, g1_ref, t1_ref, bu_ref, bd_ref, g2_ref, t2_ref,
     x_ref, wq_ref, wo_ref, wu_ref, wd_ref, perm_ref, spread_ref,
-    out_ref, vec_out_ref, loss_ref, emb_ref, dx_ref,
+    out_hbm, vec_hbm, loss_hbm, emb_hbm, dx_ref,
     qkv_keep, ctx_keep, n1_keep, r1_keep, inner_keep, n2_keep, r2_keep,
     weight, perm, xb, qkv, ctx, n1, r1, inner, n2, r2, grad, d_outer, d_att, d_ctx, act_t, d_inner, d_qkv, vectors, apt,
-    vq, vo, v1, t1, vu, vd, v2, t2, pool, d_emb, every,
-    half, send, got0, got1a, got1b, half2, got2a, got2b, half3, got3a, got3b, rows24, got2d, got3d,
+    vq, vo, v1, t1, vu, vd, v2, t2, pool, d_emb, every, out_ref, vec_out_ref, loss_row,
+    got0, got1a, got1b, half2, got2a, got2b, half3, got3a, got3b, rows24, got2d, got3d,
     vec_src, vec_z, vec_x, vec_mid, vec_cy,
     weight_sem, keep_sem, load_sem, table_sem, every_s, every_r, swap_s, swap_r,
     sems_s, sems_r, sem0_s, sem0_r, direct_s, direct_r, vec_s, vec_r,
 ):
     place = my_place()
     core = place["c"]
+    half = send = None
 
 
     kept = {
@@ -107,7 +121,7 @@
         here, there, k = kept[name]
         return pltpu.make_async_copy(there, here, load_sem.at[k])
 
-    def weights(k, layer, slot):
+    def weights(k, layer, slot, extra=None):
         blocks = []
         for m in range(4):
             cols = pl.ds(768 * m, 768)
@@ -117,31 +131,28 @@
                 src = wu_ref.at[layer, :, cols]
             else:
                 src = wq_ref.at[layer, :, cols] if m < 3 else wo_ref.at[layer]
-            blocks.append(pltpu.make_async_copy(src, weight.at[slot, cols], weight_sem.at[slot, m]))
+            dst, sem = (weight.at[slot, cols], weight_sem.at[slot, m]) if extra is None else (extra.at[slot, cols], weight_sem.at[2 + slot, m])
+            blocks.append(pltpu.make_async_copy(src, dst, sem))
         return blocks
 
-    def fetch_weights(k, layer, slot):
-        for copy in weights(k, layer, slot):
+    def fetch_weights(*use):
+        for copy in weights(*use):
             copy.start()
 
-    def ready_weights(k, layer, slot):
-        for copy in weights(k, layer, slot):
+    def ready_weights(*use):
+        for copy in weights(*use):
             copy.wait()
 
     def back_slot(k, layer):
         return lax.rem((1 - layer) * 3 + k + 1, 2)
 
     load("xb").start()
-    fetch_weights(2, 0, 0)
-    fetch_weights(1, 0, 1)
     perm_copy = pltpu.make_async_copy(perm_ref, perm, table_sem.at[0])
     spread_copy = pltpu.make_async_copy(spread_ref, weight.at[1, pl.ds(0, 1536)], table_sem.at[1])
-    perm_copy.start()
 
     barrier = pltpu.get_barrier_semaphore()
-    for axis in ("x", "z"):
-        for step in (1, 2, 3):
-            pl.semaphore_signal(barrier, inc=1, device_id=neighbour(place, axis, step), device_id_type=MESH)
+    for far in CHIPS:
+        pl.semaphore_signal(barrier, inc=1, device_id=chip_at(place, far), device_id_type=MESH)
     for flip, step in GROUP:
         pl.semaphore_signal(barrier, inc=1, device_id=in_group(place, flip, step), device_id_type=MESH)
 
@@ -156,45 +167,34 @@
     keymask = jnp.where(lax.broadcasted_iota(jnp.int32, (1, 256), 1) < count, 0.0, -1e9)
 
 
-    def slab(e, o, phase):
-        done = ORDERS[o][:phase]
-        at = tuple(pl.ds(0, 4) if axis in done else place[axis] for axis in ("z", "x", "c", "y"))
-        return every.at[(e, o) + at]
-
-    def gather_copies(e, o, phase):
-        return [
+    chip = (place["z"] * 4 + place["x"]) * 4 + place["y"]
+
+    def gather_start(e):
+        for r in range(6):
+            every[e, core, chip, r : r + 1, :] = pool[e, :, 128 * r : 128 * r + 128]
+        mine = every.at[e, core, chip]
+        for far in CHIPS:
             pltpu.make_async_remote_copy(
-                src_ref=slab(e, o, phase), dst_ref=slab(e, o, phase),
-                send_sem=every_s.at[e, o, phase, step - 1], recv_sem=every_r.at[e, o, phase, step - 1],
-                device_id=neighbour(place, ORDERS[o][phase], step), device_id_type=MESH,
-            )
-            for step in (1, 2, 3)
-        ]
+                src_ref=mine, dst_ref=mine, send_sem=every_s.at[e], recv_sem=every_r.at[e],
+                device_id=chip_at(place, far), device_id_type=MESH,
+            ).start()
 
     def swap_copy(e):
-        mine = every.at[e, :, :, :, core]
+        mine = every.at[e, core]
         return pltpu.make_async_remote_copy(
             src_ref=mine, dst_ref=mine, send_sem=swap_s.at[e], recv_sem=swap_r.at[e],
             device_id=neighbour(place, "c", 1), device_id_type=MESH,
         )
 
-    def gather_start(e):
-        for o in range(3):
-            for r in range(2):
-                at = 256 * o + 128 * r
-                every[e, o, place["z"], place["x"], core, place["y"], r : r + 1, :] = pool[e, :, at : at + 128]
-            for copy in gather_copies(e, o, 0):
-                copy.start()
-
-    def gather_next(e, phase):
-        for o in range(3):
-            for copy in gather_copies(e, o, phase):
-                copy.wait()
-            if phase < 2:
-                for copy in gather_copies(e, o, phase + 1):
-                    copy.start()
-        if phase == 2:
-            swap_copy(e).start()
+    def gather_swap(e):
+        others = every.at[e, core, pl.ds(0, 63)]
+        pltpu.make_async_copy(others, others, every_r.at[e]).wait()
+        swap_copy(e).start()
+
+    def gather_end(e):
+        others = every.at[e, core, pl.ds(0, 63)]
+        pltpu.make_async_copy(others, others, every_s.at[e]).wait()
+        swap_copy(e).wait()
 
 
     def norm(z, layer, normed_ref, scaled_ref, gain, shift, rows):
@@ -208,8 +208,11 @@
     def run_if(wanted):
         return (lambda job: job()) if wanted else (lambda job: None)
 
-    def forward_layer(layer):
+    def forward_layer(layer, extra):
         is_first, is_last = layer == 0, layer == 1
+        use_q = (2, layer, 0, extra)
+        use_u = (1, 0, 1, extra) if is_first else (1, 1, 0)
+        use_d = (0, layer, layer)
 
         def free(*names):
             @run_if(is_last)
@@ -233,18 +236,22 @@
             xb[...] = grad[...].astype(bf16)
 
         free("qkv")
-        slot = (layer * 3) % 2
-        blocks = weights(2, layer, slot)
+        blocks = weights(*use_q)
         for m in range(3):
             cols = pl.ds(768 * m, 768)
             blocks[m].wait()
-            mixed = jnp.dot(xb[...], weight[slot, cols, :], preferred_element_type=f32) + vq[layer, :, cols]
+            mixed = jnp.dot(xb[...], extra[0, cols, :], preferred_element_type=f32) + vq[layer, :, cols]
             qkv[:, cols] = mixed.astype(bf16)
         store("qkv")
 
+        @run_if(is_first)
+        def _():
+            fetch_weights(1, 0, 1, extra)
+            fetch_weights(0, 0, 0)
+
         @run_if(is_last)
         def _():
-            gather_next(0, 0)
+            perm_copy.start()
 
         free("ctx")
 
@@ -261,11 +268,16 @@
 
         @run_if(is_last)
         def _():
-            gather_next(0, 1)
+            gather_swap(0)
 
         blocks[3].wait()
-        grad[...] += jnp.dot(ctx[...], weight[slot, 2304:3072, :], preferred_element_type=f32) + vo[layer]
-        fetch_weights(0, layer, slot)
+        grad[...] += jnp.dot(ctx[...], extra[0, 2304:3072, :], preferred_element_type=f32) + vo[layer]
+
+        @run_if(is_first)
+        def _():
+            fetch_weights(2, 1, 0, extra)
+            fetch_weights(0, 1, 1)
+
         free("n1", "r1", "n2", "r2")
 
         def norm_one(i, _):
@@ -278,31 +290,22 @@
         lax.fori_loop(0, 4, norm_one, 0, unroll=4)
         store("n1", "r1")
         free("inner")
-        slot = (layer * 3 + 1) % 2
-        blocks = weights(1, layer, slot)
+        blocks = weights(*use_u)
+        expand = extra.at[1] if is_first else weight.at[0]
         for m in range(4):
             cols = pl.ds(768 * m, 768)
             blocks[m].wait()
-            value = jnp.dot(d_att[...], weight[slot, cols, :], preferred_element_type=f32) + vu[layer, :, cols]
+            value = jnp.dot(d_att[...], expand[cols, :], preferred_element_type=f32) + vu[layer, :, cols]
             inner[:, cols] = value
             d_inner[:, cols] = gelu_parts(value)[0].astype(bf16)
         store("inner")
 
+        ready_weights(*use_d)
+        n2[...] += jnp.dot(d_inner[...], weight[layer], preferred_element_type=f32) + vd[layer]
+
         @run_if(is_first)
         def _():
-            fetch_weights(2, 1, slot)
-
-        @run_if(is_last)
-        def _():
-            gather_next(0, 2)
-
-        slot = (layer * 3 + 2) % 2
-        ready_weights(0, layer, slot)
-        n2[...] += jnp.dot(d_inner[...], weight[slot], preferred_element_type=f32) + vd[layer]
-
-        @run_if(is_first)
-        def _():
-            fetch_weights(1, 1, slot)
+            fetch_weights(1, 1, 0)
 
         def norm_two(i, total):
             rows = rows_of(i, 64)
@@ -317,12 +320,12 @@
 
         @run_if(is_first)
         def _():
-            pl.semaphore_wait(barrier, 13)
+            pl.semaphore_wait(barrier, 70)
             gather_start(0)
 
         @run_if(is_last)
         def _():
-            swap_copy(0).wait()
+            gather_end(0)
             gather_start(1)
 
 
@@ -338,8 +341,9 @@
         mine = jnp.sum(jnp.where(lax.broadcasted_iota(jnp.int32, (1, 128), 1) == me, companion, 0), axis=1, keepdims=True)
         chosen = (rows == mine).astype(f32)
         is_me = rows == me
+        gathered = jnp.concatenate([every[e, c].reshape(16, 1, 4, 6, 128) for c in range(2)], axis=1).reshape(128, 6, 128)
         embed = jnp.concatenate(
-            [every[e, o].reshape(128, 2, 128)[:, r, :] for o in range(3) for r in range(2)], axis=1
+            [gathered[:, r, :] for r in range(6)], axis=1
         )
         high = embed.astype(bf16)
         low = (embed - high.astype(f32)).astype(bf16)
@@ -517,6 +521,10 @@
             dx_copy.start()
 
     dx_copy = pltpu.make_async_copy(grad, dx_ref.at[0], table_sem.at[2])
+    emb_copy = pltpu.make_async_copy(pool, emb_hbm, table_sem.at[3])
+    loss_copy = pltpu.make_async_copy(loss_row, loss_hbm, table_sem.at[4])
+    out_copy = pltpu.make_async_copy(out_ref, out_hbm, table_sem.at[5])
+    vec_copy = pltpu.make_async_copy(vec_out_ref, vec_hbm, table_sem.at[6])
 
     def store_rows(o, slot, mine, tile0, value):
         for j in range(value.shape[1] // 128):
@@ -559,7 +567,7 @@
         lax.fori_loop(0, 4, block, 0)
 
     def make(u):
-        slot = lax.rem(u, SLOTS)
+        slot = lax.rem(u, 4)
         layer = 1 - u // 6
         kind = lax.rem(u, 6)
 
@@ -640,14 +648,23 @@
 
     def exchange(o, k, slot, src_up, src_down, got):
         axis = ORDERS[o][k // 2]
-        return [
+        copies = [
             pltpu.make_async_remote_copy(
-                src_ref=src, dst_ref=got.at[o, slot, way],
-                send_sem=sems_s.at[o, k, way, slot], recv_sem=sems_r.at[o, k, way, slot],
+                src_ref=src, dst_ref=got.at[o, slot, way], send_sem=sems_s.at[o, k, slot], recv_sem=sems_r.at[o, k, slot],
                 device_id=neighbour(place, axis, step), device_id_type=MESH,
             )
             for way, (src, step) in enumerate(((src_up, 1), (src_down, -1)))
         ]
+        return copies, got.at[o, slot], sems_s.at[o, k, slot], sems_r.at[o, k, slot]
+
+    def begin(exchanged):
+        for copy in exchanged[0]:
+            copy.start()
+
+    def end(exchanged):
+        _, landed, sent_sem, landed_sem = exchanged
+        pltpu.make_async_copy(landed, landed, sent_sem).wait()
+        pltpu.make_async_copy(landed, landed, landed_sem).wait()
 
     def spots(o, phase):
         a = place[ORDERS[o][phase]]
@@ -664,7 +681,7 @@
         slot = lax.rem(u, SLOTS)
         a, up, far, down = spots(o, phase)
         if phase == 0:
-            src, got = (half.at[o, slot, pl.ds(far * 4, 2)], half.at[o, slot, pl.ds(far * 4 + 2, 2)]), got1a
+            src, got = (half.at[o, lax.rem(u, 4), pl.ds(far * 4, 2)], half.at[o, lax.rem(u, 4), pl.ds(far * 4 + 2, 2)]), got1a
         elif phase == 1:
             src, got = (half2.at[o, slot, far, pl.ds(0, 6)], half2.at[o, slot, far, pl.ds(6, 6)]), got2a
         else:
@@ -675,7 +692,7 @@
         slot = lax.rem(u, SLOTS)
         a, up, far, down = spots(o, phase)
         if phase == 0:
-            src, got = (half.at[o, slot, pl.ds(up * 4, 4)], half.at[o, slot, pl.ds(down * 4, 4)]), got1b
+            src, got = (half.at[o, lax.rem(u, 4), pl.ds(up * 4, 4)], half.at[o, lax.rem(u, 4), pl.ds(down * 4, 4)]), got1b
         elif phase == 1:
             src, got = (half2.at[o, slot, up], half2.at[o, slot, down]), got2b
         else:
@@ -687,8 +704,8 @@
         a, up, far, down = spots(o, phase)
         if phase == 0:
             for i in range(2):
-                half[o, slot, up * 4 + i] += got1a[o, slot, 0, i]
-                half[o, slot, down * 4 + 2 + i] += got1a[o, slot, 1, i]
+                half[o, lax.rem(u, 4), up * 4 + i] += got1a[o, slot, 0, i]
+                half[o, lax.rem(u, 4), down * 4 + 2 + i] += got1a[o, slot, 1, i]
         elif phase == 1:
             half2[o, slot, up, 0:6] += got2a[o, slot, 0]
             half2[o, slot, down, 6:12] += got2a[o, slot, 1]
@@ -701,7 +718,7 @@
         a, up, far, down = spots(o, phase)
         if phase == 0:
             for i in range(4):
-                half2[o, slot, i] = half[o, slot, a * 4 + i] + got1b[o, slot, 0, i] + got1b[o, slot, 1, i]
+                half2[o, slot, i] = half[o, lax.rem(u, 4), a * 4 + i] + got1b[o, slot, 0, i] + got1b[o, slot, 1, i]
         elif phase == 1:
             to_third(o, slot, u, half2[o, slot, a] + got2b[o, slot, 0] + got2b[o, slot, 1])
         else:
@@ -725,32 +742,30 @@
         slot, way = lax.rem(u, SLOTS), lax.rem(u, 2)
         a = place[ORDERS[o][phase]]
         src, got = ((half2, got2d), (half3, got3d))[phase - 1]
-        return [
+        copies = [
             pltpu.make_async_remote_copy(
                 src_ref=src.at[o, slot, lax.rem(a + step, 4)], dst_ref=got.at[o, way, step - 1],
-                send_sem=direct_s.at[o, phase - 1, way, step - 1], recv_sem=direct_r.at[o, phase - 1, way, step - 1],
+                send_sem=direct_s.at[o, phase - 1, way], recv_sem=direct_r.at[o, phase - 1, way],
                 device_id=neighbour(place, ORDERS[o][phase], step), device_id_type=MESH,
             )
             for step in (1, 2, 3)
         ]
+        return copies, got.at[o, way], direct_s.at[o, phase - 1, way], direct_r.at[o, phase - 1, way]
 
     def direct_second(u):
         slot, way = lax.rem(u, SLOTS), lax.rem(u, 2)
         for o in range(3):
-            for copy in direct(o, 1, u):
-                copy.wait()
+            end(direct(o, 1, u))
             total = half2[o, slot, place[ORDERS[o][1]]]
             for i in range(3):
                 total += got2d[o, way, i]
             to_third(o, slot, u, total)
-            for copy in direct(o, 2, u):
-                copy.start()
+            begin(direct(o, 2, u))
 
     def direct_third(u):
         slot, way = lax.rem(u, SLOTS), lax.rem(u, 2)
         for o in range(3):
-            for copy in direct(o, 2, u):
-                copy.wait()
+            end(direct(o, 2, u))
             total = half3[o, slot, place[ORDERS[o][2]]]
             for i in range(3):
                 total += got3d[o, way, i]
@@ -776,53 +791,43 @@
                 for x in range(4):
                     vec_src[z, x, layer] = total[z, x]
 
-    def vector_copy(k, src, dst, device):
-        return pltpu.make_async_remote_copy(
-            src_ref=src, dst_ref=dst, send_sem=vec_s.at[k], recv_sem=vec_r.at[k], device_id=device, device_id_type=MESH
-        )
+    def vector_copies(k, landed, pieces):
+        copies = [
+            pltpu.make_async_remote_copy(
+                src_ref=src, dst_ref=landed.at[i], send_sem=vec_s.at[k], recv_sem=vec_r.at[k], device_id=device, device_id_type=MESH
+            )
+            for i, (src, device) in enumerate(pieces)
+        ]
+        return copies, landed, vec_s.at[k], vec_r.at[k]
 
     def copies_z():
-        return [
-            vector_copy(i, vec_src.at[lax.rem(place["z"] + i + 1, 4)], vec_z.at[i], neighbour(place, "z", i + 1))
-            for i in range(3)
-        ]
+        return vector_copies(0, vec_z, [(vec_src.at[lax.rem(place["z"] + i, 4)], neighbour(place, "z", i)) for i in (1, 2, 3)])
 
     def copies_x():
-        return [
-            vector_copy(3 + i, vec_src.at[place["z"], lax.rem(place["x"] + i + 1, 4)], vec_x.at[i], neighbour(place, "x", i + 1))
-            for i in range(3)
-        ]
+        mine = place["z"]
+        return vector_copies(1, vec_x, [(vec_src.at[mine, lax.rem(place["x"] + i, 4)], neighbour(place, "x", i)) for i in (1, 2, 3)])
 
     def copies_group():
-        return [
-            vector_copy(6 + i, vec_mid, vec_cy.at[i], in_group(place, flip, step))
-            for i, (flip, step) in enumerate(GROUP)
-        ]
+        return vector_copies(2, vec_cy, [(vec_mid, in_group(place, flip, step)) for flip, step in GROUP])
 
     def vectors_start():
         spread_copy.wait()
         spread_vectors()
-        for copy in copies_z():
-            copy.start()
+        begin(copies_z())
 
     def vectors_second():
-        for copy in copies_z():
-            copy.wait()
+        end(copies_z())
         for x in range(4):
             vec_src[place["z"], x] += vec_z[0, x] + vec_z[1, x] + vec_z[2, x]
-        for copy in copies_x():
-            copy.start()
+        begin(copies_x())
 
     def vectors_third():
-        for copy in copies_x():
-            copy.wait()
+        end(copies_x())
         vec_mid[...] = vec_src[place["z"], place["x"]] + vec_x[0] + vec_x[1] + vec_x[2]
-        for copy in copies_group():
-            copy.start()
+        begin(copies_group())
 
     def vectors_last():
-        for copy in copies_group():
-            copy.wait()
+        end(copies_group())
         total = vec_mid[...]
         for i in range(7):
             total += vec_cy[i]
@@ -840,55 +845,48 @@
             copy0(o, u).wait()
 
             def add(i, _):
-                half[o, slot, i] += got0[o, lax.rem(u, 2), i]
+                half[o, lax.rem(u, 4), i] += got0[o, lax.rem(u, 2), i]
                 return 0
 
             lax.fori_loop(0, 16, add, 0)
-            for copy in step_a(o, 0, u):
-                copy.start()
+            begin(step_a(o, 0, u))
 
     def second(phase):
         def job(u):
             for o in range(3):
-                for copy in step_a(o, phase, u):
-                    copy.wait()
+                end(step_a(o, phase, u))
                 add_a(o, phase, u)
-                for copy in step_b(o, phase, u):
-                    copy.start()
+                begin(step_b(o, phase, u))
         return job
 
     def third(phase):
         def job(u):
             for o in range(3):
-                for copy in step_b(o, phase, u):
-                    copy.wait()
+                end(step_b(o, phase, u))
                 add_b(o, phase, u)
                 if phase == 0:
                     @pl.when(u < DIRECT)
                     def _():
-                        for copy in step_a(o, 1, u):
-                            copy.start()
+                        begin(step_a(o, 1, u))
 
                     @pl.when(u >= DIRECT)
                     def _():
-                        for copy in direct(o, 1, u):
-                            copy.start()
+                        begin(direct(o, 1, u))
                 elif phase == 1:
-                    for copy in step_a(o, 2, u):
-                        copy.start()
+                    begin(step_a(o, 2, u))
         return job
 
     def tick(u, _):
         when(u, 0, TRIPLES, make)
+        when(u - 3, 0, TRIPLES, third(0))
+        when(u - 4, 0, DIRECT, second(1))
+        when(u - 5, 0, DIRECT, third(1))
+        when(u - 6, 0, DIRECT, second(2))
+        when(u - 7, 0, DIRECT, third(2))
+        when(u - 4, DIRECT, TRIPLES, direct_second)
+        when(u - 5, DIRECT, TRIPLES, direct_third)
+        when(u, 0, TRIPLES, enter)
         when(u - 1, 0, TRIPLES, second(0))
-        when(u - 2, 0, TRIPLES, third(0))
-        when(u - 3, 0, DIRECT, second(1))
-        when(u - 6, 0, DIRECT, third(2))
-        when(u - 3, DIRECT, TRIPLES, direct_second)
-        when(u - 4, 0, DIRECT, third(1))
-        when(u - 4, DIRECT, TRIPLES, direct_third)
-        when(u - 5, 0, DIRECT, second(2))
-        when(u, 0, TRIPLES, enter)
         when(u, 0, TRIPLES, follow)
 
         @pl.when(u == TRIPLES - 1)
@@ -900,23 +898,33 @@
         return 0
 
 
-    forward_layer(0)
-    forward_layer(1)
-    for layer in range(2):
-        emb_ref[0, layer : layer + 1, :] = pool[layer]
+    def forward_both(extra):
+        fetch_weights(2, 0, 0, extra)
+        forward_layer(0, extra)
+        forward_layer(1, extra)
+
+    pl.run_scoped(forward_both, pltpu.VMEM((2, 3072, 768), bf16))
+    emb_copy.start()
     half3[...] = jnp.zeros_like(half3)
     loss = pairing(0, jnp.zeros((128, 1), f32))
-    gather_next(1, 0)
     turn_active()
-    gather_next(1, 1)
+    gather_swap(1)
     perm_copy.wait()
     permute(d_att[...], 0)
-    gather_next(1, 2)
-    swap_copy(1).wait()
-    loss = pairing(1, loss)
-    loss_ref[...] = loss / 8.0
-    lax.fori_loop(0, DIRECT + 6, tick, 0)
-    dx_copy.wait()
+    gather_end(1)
+    loss_row[...] = pairing(1, loss) / 8.0
+    loss_copy.start()
+
+    def reduce_all(half_ref, send_ref):
+        nonlocal half, send
+        half, send = half_ref, send_ref
+        lax.fori_loop(0, DIRECT + 7, tick, 0)
+
+    pl.run_scoped(reduce_all, pltpu.VMEM((3, 4, 16, 12, 8, 128), f32), pltpu.VMEM((3, 16, 12, 8, 128), f32))
+    out_copy.start()
+    vec_copy.start()
+    for copy in (dx_copy, emb_copy, loss_copy, out_copy, vec_copy):
+        copy.wait()
 
 
 def permutations():
@@ -940,17 +948,22 @@
     return out.astype(ml_dtypes.bfloat16)
 
 
-def finish_kernel(out_hbm, vec_hbm, loss_hbm, dx_hbm, *refs):
-    loss_out, dx_out, qkv_out, qv_out, mixer_out, bias_out, gain_out, shift_out, up_out, ffn_out, down_out, downbias_out, fingain_out, finshift_out = refs[:14]
-    out_ref, vec_ref, loss_ref, sem = refs[14:]
+def finish_kernel(out_hbm, vec_hbm, loss_hbm, emb_hbm, dx_hbm, *refs):
+    loss_out, emb_out, dx_out, qkv_out, qv_out, mixer_out, bias_out, gain_out, shift_out, up_out, ffn_out, down_out, downbias_out, fingain_out, finshift_out = refs[:15]
+    out_ref, vec_ref, loss_ref, emb_ref, dx_ref, sem = refs[15:]
     copies = [
         pltpu.make_async_copy(src, dst, sem.at[k])
-        for k, (src, dst) in enumerate(((out_hbm, out_ref), (vec_hbm, vec_ref), (loss_hbm, loss_ref), (dx_hbm, dx_out)))
+        for k, (src, dst) in enumerate(((out_hbm, out_ref), (vec_hbm, vec_ref), (loss_hbm, loss_ref), (emb_hbm, emb_ref), (dx_hbm, dx_ref)))
     ]
     for copy in copies:
         copy.start()
-    for copy in copies[:3]:
+    for copy in copies[:4]:
         copy.wait()
+    for layer in range(2):
+        emb_out[0, layer : layer + 1, :] = emb_ref[layer]
+    copies[4].wait()
+    last = pltpu.make_async_copy(dx_ref, dx_out, sem.at[4])
+    last.start()
     for layer in range(2):
         first = 6 * (1 - layer)
         for k in range(2):
@@ -978,7 +991,7 @@
     rows = lax.broadcasted_iota(jnp.int32, (128, 1), 0)
     for k in range(4):
         loss_out[k] = jnp.sum(jnp.where(rows == lax.axis_index("batch") * 4 + k, loss_ref[...], 0.0))
-    copies[3].wait()
+    last.wait()
 
 
 def body(slots, counts, companion, widths, divisor, triple, bias_qv, mixer, bias_mixer, gain_one, shift_one, expand, bias_expand, shrink, bias_shrink, gain_two, shift_two):
@@ -992,28 +1005,28 @@
 
     dma = pltpu.SemaphoreType.DMA
     saved = [((256, 2304), bf16), ((256, 768), bf16), ((256, 768), f32), ((256, 1), f32), ((256, 3072), f32), ((256, 768), f32), ((256, 1), f32)]
-    shapes = [((TRIPLES, 3, 4) + tile, f32), ((2, 128), f32), ((128, 1), f32), ((1, 2, 768), f32), ((1, 256, 768), f32)] + saved
+    shapes = [((TRIPLES, 3, 4) + tile, f32), ((2, 128), f32), ((128, 1), f32), ((2, 1, 768), f32), ((1, 256, 768), f32)] + saved
     results = pl.pallas_call(
         whole_kernel,
         out_shape=[jax.ShapeDtypeStruct(s, t) for s, t in shapes],
         in_specs=[smem, vmem, smem, smem] + [vmem] * 8 + [hbm] * 7,
-        out_specs=[vmem] * 4 + [hbm] * 8,
+        out_specs=[hbm] * 12,
         scratch_shapes=[
             vm(2, 3072, 768, dtype=bf16), vm(3, 768, 768, dtype=bf16), vm(256, 768, dtype=bf16), vm(256, 2304, dtype=bf16),
             vm(256, 768, dtype=bf16), vm(256, 768), vm(256, 1), vm(256, 3072), vm(256, 768), vm(256, 1), vm(256, 768),
             vm(256, 768, dtype=bf16), vm(256, 768, dtype=bf16), vm(256, 768, dtype=bf16), vm(3072, 256, dtype=bf16),
             vm(256, 3072, dtype=bf16), vm(256, 2304, dtype=bf16), vm(2, 1, 9216), vm(3, 2, 768, 256, dtype=bf16),
             vm(2, 1, 2304), vm(2, 1, 768), vm(2, 1, 768), vm(2, 1, 768), vm(2, 1, 3072), vm(2, 1, 768), vm(2, 1, 768), vm(2, 1, 768),
-            vm(2, 1, 768), vm(2, 1, 768), vm(2, 3, 4, 4, 2, 4, 2, 128),
-            vm(3, SLOTS, 16, 12, *tile), vm(3, 16, 12, *tile), vm(3, 2, 16, 12, *tile),
+            vm(2, 1, 768), vm(2, 1, 768), vm(2, 2, 64, 6, 128), vm(TRIPLES, 3, 4, *tile), vm(2, 128), vm(128, 1),
+            vm(3, 2, 16, 12, *tile),
             vm(3, SLOTS, 2, 2, 12, *tile), vm(3, SLOTS, 2, 4, 12, *tile),
             vm(3, SLOTS, 4, 12, *tile), vm(3, SLOTS, 2, 6, *tile), vm(3, SLOTS, 2, 12, *tile),
             vm(3, SLOTS, 4, 4, *tile), vm(3, SLOTS, 2, 2, *tile), vm(3, SLOTS, 2, 4, *tile), vm(3, 4, 24, 128),
             vm(3, 2, 3, 12, *tile), vm(3, 2, 3, 4, *tile),
             vm(4, 4, 2, *tile), vm(3, 4, 2, *tile), vm(3, 2, *tile), vm(2, *tile), vm(7, 2, *tile),
-            dma((2, 4)), dma((7,)), dma((8,)), dma((3,)), dma((2, 3, 3, 3)), dma((2, 3, 3, 3)), dma((2,)), dma((2,)),
-            dma((3, 6, 2, SLOTS)), dma((3, 6, 2, SLOTS)), dma((3,)), dma((3, 2)), dma((3, 2, 2, 3)), dma((3, 2, 2, 3)),
-            dma((13,)), dma((13,)),
+            dma((4, 4)), dma((7,)), dma((8,)), dma((7,)), dma((2,)), dma((2,)), dma((2,)), dma((2,)),
+            dma((3, 6, SLOTS)), dma((3, 6, SLOTS)), dma((3,)), dma((3, 2)), dma((3, 2, 2)), dma((3, 2, 2)),
+            dma((3,)), dma((3,)),
         ],
         compiler_params=pltpu.CompilerParams(
             collective_id=1, has_side_effects=True, vmem_limit_bytes=63 * 1024 * 1024
@@ -1024,15 +1037,15 @@
         slots, triple, mixer, expand, shrink, jnp.asarray(permutations()), jnp.asarray(lane_places()),
     )
     out, vec_out, loss, embeddings, dx = results[:5]
-    shapes = [(4,), (1, 256, 768), (6, 2, 2304), (2, 12), (6, 2, 768), (2, 6), (2, 6), (2, 6), (6, 2, 3072), (2, 24), (2, 24, 768), (2, 6), (2, 6), (2, 6)]
-    loss, *rest = pl.pallas_call(
+    shapes = [(4,), (1, 2, 768), (1, 256, 768), (6, 2, 2304), (2, 12), (6, 2, 768), (2, 6), (2, 6), (2, 6), (6, 2, 3072), (2, 24), (2, 24, 768), (2, 6), (2, 6), (2, 6)]
+    loss, embeddings, *rest = pl.pallas_call(
         finish_kernel,
         out_shape=[jax.ShapeDtypeStruct(s, f32) for s in shapes],
-        in_specs=[hbm] * 4,
-        out_specs=[smem, hbm] + [vmem] * 12,
-        scratch_shapes=[vm(TRIPLES, 3, 4, *tile), vm(2, 128), vm(128, 1), dma((4,))],
-        compiler_params=pltpu.CompilerParams(vmem_limit_bytes=32 * 1024 * 1024),
-    )(out, vec_out, loss, dx)
+        in_specs=[hbm] * 5,
+        out_specs=[smem, vmem, hbm] + [vmem] * 12,
+        scratch_shapes=[vm(TRIPLES, 3, 4, *tile), vm(2, 128), vm(128, 1), vm(2, 1, 768), vm(1, 256, 768), dma((5,))],
+        compiler_params=pltpu.CompilerParams(vmem_limit_bytes=63 * 1024 * 1024),
+    )(out, vec_out, loss, embeddings, dx)
     rest = [r.transpose(1, 0, 2) if r.shape[:2] == (6, 2) else r for r in rest]
     return (loss, embeddings, *rest)
 

time: 206 us -> 185 us (0.90)
  Pallas kernels: 195 us -> 181 us
  local copies, waits for them, and re-layouts: 4.94 us -> 0 us
    pallas_call x1, Pallas kernels: 193 us -> 178 us  [body(): pl.pallas_call(whole_kernel, out_shape=[jax.ShapeDtypeStruct(s, t) for s,...]
    unnamed x9 -> x0, local copies, waits for them, and re-layouts: 4.94 us -> none
where the time goes in v5:
time: 185 us; the launch traced here: 183 us
  Pallas kernels  181 us (98%)
  between operations  2.16 us (1%)
    pallas_call x1, Pallas kernels, body(): pl.pallas_call(whole_kernel, out_shape=[jax.ShapeDtypeStruct(s, t) for s,...  178 us

profile of v5, /device:TPU:0, one launch (start us, length us, event | category | flops | bytes accessed | tf_op | source)
XLA Modules:
  0.0 183.1 jit_solution(17334613122993770488)
XLA Ops:
  1.9 177.8 %shard_map.298 = (f32[12,3,4,8,128]{4,3,2,1,0:T(8,128)}, f32[2,128]{1,0:T(2,128)}, f32[128,1]{1,0:T(8,128)}, f32[2,1,768]{2,1,0:T(1,128)}, f32[1,256,768]{2,1,0:...) custom-call(s32[1]{0:T(128)S(6)} %copy.34.count_ref, ...), custom_call_target="tpu_custom_call" | custom-call | tf_op jit(solution)/shard_map/pallas_call | solution.py:1009
  179.8 3.1 %shard_map.299 = (f32[4]{0:T(128)}, f32[1,2,768]{2,1,0:T(2,128)}, f32[1,256,768]{2,1,0:T(8,128)}, f32[6,2,2304]{2,1,0:T(2,128)}, f32[2,12]{1,0:T(2,128)}, /*inde...) custom-call(f32[12,3,4,8,128]{4,3,2,1,0:T(8,128)} %get-tuple-element, ...), custom_call_target="tpu_custom_call" | custom-call | tf_op jit(solution)/shard_map/pallas_call | solution.py:1041

commit v6 on v5

--- a/solution.py
+++ b/solution.py
@@ -45,11 +45,12 @@
 )
 
 
-def chip_at(place, steps):
-    there = dict(place)
-    for axis, step in zip("zxy", steps):
-        there[axis] = lax.rem(place[axis] + step, 4)
-    return device_at(there)
+def for_other_chips(place, job):
+    for steps in CHIPS:
+        there = dict(place)
+        for axis, step in zip("zxy", steps):
+            there[axis] = lax.rem(place[axis] + step, 4)
+        job(device_at(there))
 
 
 def in_group(place, flip, step):
@@ -151,8 +152,7 @@
     spread_copy = pltpu.make_async_copy(spread_ref, weight.at[1, pl.ds(0, 1536)], table_sem.at[1])
 
     barrier = pltpu.get_barrier_semaphore()
-    for far in CHIPS:
-        pl.semaphore_signal(barrier, inc=1, device_id=chip_at(place, far), device_id_type=MESH)
+    for_other_chips(place, lambda there: pl.semaphore_signal(barrier, inc=1, device_id=there, device_id_type=MESH))
     for flip, step in GROUP:
         pl.semaphore_signal(barrier, inc=1, device_id=in_group(place, flip, step), device_id_type=MESH)
 
@@ -173,11 +173,9 @@
         for r in range(6):
             every[e, core, chip, r : r + 1, :] = pool[e, :, 128 * r : 128 * r + 128]
         mine = every.at[e, core, chip]
-        for far in CHIPS:
-            pltpu.make_async_remote_copy(
-                src_ref=mine, dst_ref=mine, send_sem=every_s.at[e], recv_sem=every_r.at[e],
-                device_id=chip_at(place, far), device_id_type=MESH,
-            ).start()
+        for_other_chips(place, lambda there: pltpu.make_async_remote_copy(
+            src_ref=mine, dst_ref=mine, send_sem=every_s.at[e], recv_sem=every_r.at[e], device_id=there, device_id_type=MESH
+        ).start())
 
     def swap_copy(e):
         mine = every.at[e, core]
@@ -205,33 +203,33 @@
         scaled_ref[rows, :] = scaled
         return normed * gain[layer] + shift[layer]
 
-    def run_if(wanted):
-        return (lambda job: job()) if wanted else (lambda job: None)
-
     def forward_layer(layer, extra):
         is_first, is_last = layer == 0, layer == 1
-        use_q = (2, layer, 0, extra)
-        use_u = (1, 0, 1, extra) if is_first else (1, 1, 0)
-        use_d = (0, layer, layer)
+        use_q, use_u, use_d = (2, layer, 0, extra), (1, layer, 1, extra), (0, layer, layer)
+
+        @pl.when(is_last)
+        def _():
+            pl.semaphore_wait(barrier, 70)
+            gather_start(0)
 
         def free(*names):
-            @run_if(is_last)
+            @pl.when(is_last)
             def _():
                 for name in names:
                     keep(name).wait()
 
         def store(*names):
-            @run_if(is_first)
+            @pl.when(is_first)
             def _():
                 for name in names:
                     keep(name).start()
 
-        @run_if(is_first)
+        @pl.when(is_first)
         def _():
             load("xb").wait()
             grad[...] = xb[...].astype(f32)
 
-        @run_if(is_last)
+        @pl.when(is_last)
         def _():
             xb[...] = grad[...].astype(bf16)
 
@@ -244,12 +242,12 @@
             qkv[:, cols] = mixed.astype(bf16)
         store("qkv")
 
-        @run_if(is_first)
+        @pl.when(is_first)
         def _():
             fetch_weights(1, 0, 1, extra)
             fetch_weights(0, 0, 0)
 
-        @run_if(is_last)
+        @pl.when(is_last)
         def _():
             perm_copy.start()
 
@@ -266,14 +264,14 @@
         lax.fori_loop(0, 6, attend, 0, unroll=6)
         store("ctx")
 
-        @run_if(is_last)
+        @pl.when(is_last)
         def _():
             gather_swap(0)
 
         blocks[3].wait()
         grad[...] += jnp.dot(ctx[...], extra[0, 2304:3072, :], preferred_element_type=f32) + vo[layer]
 
-        @run_if(is_first)
+        @pl.when(is_first)
         def _():
             fetch_weights(2, 1, 0, extra)
             fetch_weights(0, 1, 1)
@@ -291,19 +289,22 @@
         store("n1", "r1")
         free("inner")
         blocks = weights(*use_u)
-        expand = extra.at[1] if is_first else weight.at[0]
         for m in range(4):
             cols = pl.ds(768 * m, 768)
             blocks[m].wait()
-            value = jnp.dot(d_att[...], expand[cols, :], preferred_element_type=f32) + vu[layer, :, cols]
+            value = jnp.dot(d_att[...], extra[1, cols, :], preferred_element_type=f32) + vu[layer, :, cols]
             inner[:, cols] = value
             d_inner[:, cols] = gelu_parts(value)[0].astype(bf16)
         store("inner")
 
+        @pl.when(is_first)
+        def _():
+            fetch_weights(1, 1, 1, extra)
+
         ready_weights(*use_d)
         n2[...] += jnp.dot(d_inner[...], weight[layer], preferred_element_type=f32) + vd[layer]
 
-        @run_if(is_first)
+        @pl.when(is_first)
         def _():
             fetch_weights(1, 1, 0)
 
@@ -318,15 +319,9 @@
         pool[layer] = total / count.astype(f32)
         store("n2", "r2")
 
-        @run_if(is_first)
-        def _():
-            pl.semaphore_wait(barrier, 70)
-            gather_start(0)
-
-        @run_if(is_last)
+        @pl.when(is_last)
         def _():
             gather_end(0)
-            gather_start(1)
 
 
     def pairing(e, loss):
@@ -403,8 +398,11 @@
         lax.fori_loop(0, 12, turn, 0, unroll=2)
 
     def permute(operand, which):
-        for o in range(3):
+        def one(o, _):
             apt[o, which] = lax.dot_general(perm[o], operand, NT, preferred_element_type=f32).astype(bf16)
+            return 0
+
+        lax.fori_loop(0, 3, one, 0, unroll=3)
 
     def begin_layer(layer):
         spots = lax.broadcasted_iota(jnp.int32, (256, 1), 0)
@@ -466,6 +464,10 @@
         @pl.when(layer == 0)
         def _():
             ready_weights(1, 0, slot)
+
+        @pl.when(layer == 1)
+        def _():
+            ready_weights(1, 1, slot)
 
         for m in range(4):
             cols = pl.ds(768 * m, 768)
@@ -534,34 +536,39 @@
             else:
                 send[o, :, tile0 + 3 * j : tile0 + 3 * j + 3] = part
 
-    def product(o, slot, which, ref, at, width, tile0):
-        for mine in (False, True):
+    def product(mine, slot, uses):
+        c = core if mine else 1 - core
+
+        def one(o, _):
+            for which, ref, start, width, tile0 in uses:
+                lhs = apt[o, which, pl.ds(pl.multiple_of(c * 384, 128), 384), :]
+                for w in range(0, width, 256):
+                    cols = pl.ds(pl.multiple_of(start(o) + w, 256), 256)
+                    value = jnp.dot(lhs, ref[:, cols], preferred_element_type=f32)
+                    store_rows(o, slot, mine, tile0 + 3 * (w // 128), value)
+            return 0
+
+        lax.fori_loop(0, 3, one, 0, unroll=3)
+
+    def product_shrink(mine, slot, k):
+        def block(z, _):
             c = core if mine else 1 - core
-            lhs = apt[o, which, pl.ds(pl.multiple_of(c * 384, 128), 384), :]
-            for w in range(0, width, 256):
-                value = jnp.dot(lhs, ref[:, at + w : at + w + 256], preferred_element_type=f32)
-                store_rows(o, slot, mine, tile0 + 3 * (w // 128), value)
-
-    def product_shrink(slot, k):
-        def block(z, _):
-            for mine in (False, True):
-                c = core if mine else 1 - core
-                lhs = jnp.concatenate(
-                    [act_t[pl.ds(pl.multiple_of(z * 768 + x * 192 + c * 96, 32), 96), :] for x in range(4)], axis=0
-                )
-                value = jnp.dot(lhs, d_outer[:, 384 * k : 384 * (k + 1)], preferred_element_type=f32)
-                for x in range(4):
-                    for y in range(4):
-                        for j in range(3):
-                            p = {"x": x, "y": y, "z": z}
-                            d1, d2, d3 = (p[axis] for axis in ORDERS[j])
-                            row = x * 96 + (y * 3 + j) * 8
-                            for ct in range(3):
-                                tile = value[row : row + 8, 128 * ct : 128 * ct + 128]
-                                if mine:
-                                    half[j, slot, d1 * 4 + d2, d3 * 3 + ct] = tile
-                                else:
-                                    send[j, d1 * 4 + d2, d3 * 3 + ct] = tile
+            lhs = jnp.concatenate(
+                [act_t[pl.ds(pl.multiple_of(z * 768 + x * 192 + c * 96, 32), 96), :] for x in range(4)], axis=0
+            )
+            value = jnp.dot(lhs, d_outer[:, pl.ds(pl.multiple_of(384 * k, 128), 384)], preferred_element_type=f32)
+            for x in range(4):
+                for y in range(4):
+                    for j in range(3):
+                        p = {"x": x, "y": y, "z": z}
+                        d1, d2, d3 = (p[axis] for axis in ORDERS[j])
+                        row = x * 96 + (y * 3 + j) * 8
+                        for ct in range(3):
+                            tile = value[row : row + 8, 128 * ct : 128 * ct + 128]
+                            if mine:
+                                half[j, slot, d1 * 4 + d2, d3 * 3 + ct] = tile
+                            else:
+                                send[j, d1 * 4 + d2, d3 * 3 + ct] = tile
             return 0
 
         lax.fori_loop(0, 4, block, 0)
@@ -571,41 +578,33 @@
         layer = 1 - u // 6
         kind = lax.rem(u, 6)
 
-        def to_other_core(o):
-            copy0(o, u).start()
+        def both_halves(job):
+            job(False)
+            for o in range(3):
+                copy0(o, u).start()
+            job(True)
 
         @pl.when(kind == 0)
         def _():
             begin_layer(layer)
-            product_shrink(slot, 0)
-            for o in range(3):
-                to_other_core(o)
-
-        @pl.when(kind == 1)
-        def _():
-            product_shrink(slot, 1)
-            for o in range(3):
-                to_other_core(o)
-
-        for k in range(2):
-            @pl.when(kind == 2 + k)
-            def _():
-                for o in range(3):
-                    product(o, slot, 0, d_inner, (k * 3 + o) * 512, 512, 0)
-                    to_other_core(o)
+
+        @pl.when(kind < 2)
+        def _():
+            both_halves(lambda mine: product_shrink(mine, slot, kind))
+
+        @pl.when((kind == 2) | (kind == 3))
+        def _():
+            both_halves(lambda mine: product(mine, slot, [(0, d_inner, lambda o: (kind - 2) * 1536 + o * 512, 512, 0)]))
 
         @pl.when(kind == 4)
         def _():
-            for o in range(3):
-                product(o, slot, 0, d_qkv, o * 768, 512, 0)
-                to_other_core(o)
+            both_halves(lambda mine: product(mine, slot, [(0, d_qkv, lambda o: o * 768, 512, 0)]))
 
         @pl.when(kind == 5)
         def _():
-            for o in range(3):
-                product(o, slot, 0, d_qkv, o * 768 + 512, 256, 0)
-                product(o, slot, 1, d_att, o * 256, 256, 6)
-                to_other_core(o)
+            both_halves(lambda mine: product(
+                mine, slot, [(0, d_qkv, lambda o: o * 768 + 512, 256, 0), (1, d_att, lambda o: o * 256, 256, 6)]
+            ))
 
     def follow(u):
         layer = 1 - u // 6
@@ -771,25 +770,24 @@
                 total += got3d[o, way, i]
             out_ref[u, o] = total
 
-    def spread_vectors():
-        for layer in range(2):
-            total = jnp.zeros((128, 128), f32)
-            for start, width, keep in VECTORS:
-                d = lax.broadcasted_iota(jnp.int32, (128, width), 0) * keep
-                q = lax.broadcasted_iota(jnp.int32, (128, width), 1)
-                own = jnp.where((q >= d) & (q < d + keep), vectors[layer, :, start : start + width], 0.0)
-                high = own.astype(bf16)
-                low = (own - high.astype(f32)).astype(bf16)
-                for part in range(width // 768):
-                    k = start // 768 + part
-                    lanes = weight[1, 768 * (k // 6) : 768 * (k // 6 + 1), 128 * (k % 6) : 128 * (k % 6 + 1)]
-                    at = slice(768 * part, 768 * (part + 1))
-                    total += jnp.dot(high[:, at], lanes, preferred_element_type=f32)
-                    total += jnp.dot(low[:, at], lanes, preferred_element_type=f32)
-            total = total.reshape(4, 4, 8, 128)
-            for z in range(4):
-                for x in range(4):
-                    vec_src[z, x, layer] = total[z, x]
+    def spread_vectors(layer):
+        total = jnp.zeros((128, 128), f32)
+        for start, width, keep in VECTORS:
+            d = lax.broadcasted_iota(jnp.int32, (128, width), 0) * keep
+            q = lax.broadcasted_iota(jnp.int32, (128, width), 1)
+            own = jnp.where((q >= d) & (q < d + keep), vectors[layer, :, start : start + width], 0.0)
+            high = own.astype(bf16)
+            low = (own - high.astype(f32)).astype(bf16)
+            for part in range(width // 768):
+                k = start // 768 + part
+                lanes = weight[1, 768 * (k // 6) : 768 * (k // 6 + 1), 128 * (k % 6) : 128 * (k % 6 + 1)]
+                at = slice(768 * part, 768 * (part + 1))
+                total += jnp.dot(high[:, at], lanes, preferred_element_type=f32)
+                total += jnp.dot(low[:, at], lanes, preferred_element_type=f32)
+        total = total.reshape(4, 4, 8, 128)
+        for z in range(4):
+            for x in range(4):
+                vec_src[z, x, layer] = total[z, x]
 
     def vector_copies(k, landed, pieces):
         copies = [
@@ -810,9 +808,12 @@
     def copies_group():
         return vector_copies(2, vec_cy, [(vec_mid, in_group(place, flip, step)) for flip, step in GROUP])
 
+    def vectors_first():
+        spread_copy.wait()
+        spread_vectors(1)
+
     def vectors_start():
-        spread_copy.wait()
-        spread_vectors()
+        spread_vectors(0)
         begin(copies_z())
 
     def vectors_second():
@@ -889,30 +890,37 @@
         when(u - 1, 0, TRIPLES, second(0))
         when(u, 0, TRIPLES, follow)
 
-        @pl.when(u == TRIPLES - 1)
-        def _():
-            spread_copy.start()
-
-        for k, job in enumerate((vectors_start, vectors_second, vectors_third, vectors_last)):
-            pl.when(u == TRIPLES + k)(job)
+        for k, job in ((8, spread_copy.start), (9, vectors_first), (11, vectors_start), (12, vectors_second), (13, vectors_third), (14, vectors_last)):
+            pl.when(u == k)(job)
         return 0
 
 
     def forward_both(extra):
         fetch_weights(2, 0, 0, extra)
-        forward_layer(0, extra)
-        forward_layer(1, extra)
+
+        def layer_step(layer, _):
+            forward_layer(layer, extra)
+            return 0
+
+        lax.fori_loop(0, 2, layer_step, 0)
+        gather_start(1)
 
     pl.run_scoped(forward_both, pltpu.VMEM((2, 3072, 768), bf16))
     emb_copy.start()
     half3[...] = jnp.zeros_like(half3)
-    loss = pairing(0, jnp.zeros((128, 1), f32))
-    turn_active()
-    gather_swap(1)
-    perm_copy.wait()
-    permute(d_att[...], 0)
-    gather_end(1)
-    loss_row[...] = pairing(1, loss) / 8.0
+
+    def layer_loss(e, loss):
+        @pl.when(e == 1)
+        def _():
+            turn_active()
+            gather_swap(1)
+            perm_copy.wait()
+            permute(d_att[...], 0)
+            gather_end(1)
+
+        return pairing(e, loss)
+
+    loss_row[...] = lax.fori_loop(0, 2, layer_loss, jnp.zeros((128, 1), f32)) / 8.0
     loss_copy.start()
 
     def reduce_all(half_ref, send_ref):

time: 185 us -> 171 us (0.924)
  Pallas kernels: 181 us -> 168 us
    pallas_call x1, Pallas kernels: 178 us -> 165 us  [body(): pl.pallas_call(whole_kernel, out_shape=[jax.ShapeDtypeStruct(s, t) for s,...]
where the time goes in v6:
time: 171 us; the launch traced here: 170 us
  Pallas kernels  168 us (98%)
  between operations  2.11 us (1%)
    pallas_call x1, Pallas kernels, body(): pl.pallas_call(whole_kernel, out_shape=[jax.ShapeDtypeStruct(s, t) for s,...  165 us

profile of v6, /device:TPU:0, one launch (start us, length us, event | category | flops | bytes accessed | tf_op | source)
XLA Modules:
  0.0 170.4 jit_solution(14261990485664633889)
XLA Ops:
  1.9 165.3 %shard_map.298 = (f32[12,3,4,8,128]{4,3,2,1,0:T(8,128)}, f32[2,128]{1,0:T(2,128)}, f32[128,1]{1,0:T(8,128)}, f32[2,1,768]{2,1,0:T(1,128)}, f32[1,256,768]{2,1,0:...) custom-call(s32[1]{0:T(128)S(6)} %copy.34.count_ref, ...), custom_call_target="tpu_custom_call" | custom-call | tf_op jit(solution)/shard_map/pallas_call | solution.py:1017
  167.2 3.1 %shard_map.299 = (f32[4]{0:T(128)}, f32[1,2,768]{2,1,0:T(2,128)}, f32[1,256,768]{2,1,0:T(8,128)}, f32[6,2,2304]{2,1,0:T(2,128)}, f32[2,12]{1,0:T(2,128)}, /*inde...) custom-call(f32[12,3,4,8,128]{4,3,2,1,0:T(8,128)} %get-tuple-element, ...), custom_call_target="tpu_custom_call" | custom-call | tf_op jit(solution)/shard_map/pallas_call | solution.py:1049

commit v7 on v6

--- a/solution.py
+++ b/solution.py
@@ -344,15 +344,16 @@
         low = (embed - high.astype(f32)).astype(bf16)
         own = pool[e]
         total = jnp.zeros((1, 768), f32)
-        for p in range(4):
-            keep_p = (lane < widths_ref[p]).astype(f32)
-            keep_low = keep_p.astype(bf16)
-            high_p, low_p = high * keep_low, low * keep_low
-            gram = (
-                lax.dot_general(high_p, high, NT, preferred_element_type=f32)
-                + lax.dot_general(high_p, low, NT, preferred_element_type=f32)
-                + lax.dot_general(low_p, high, NT, preferred_element_type=f32)
-            )
+        keeps = [(lane < widths_ref[p]).astype(f32) for p in range(4)]
+        high_all = jnp.concatenate([high * keep_p.astype(bf16) for keep_p in keeps], axis=0)
+        low_all = jnp.concatenate([low * keep_p.astype(bf16) for keep_p in keeps], axis=0)
+        grams = (
+            lax.dot_general(high_all, high, NT, preferred_element_type=f32)
+            + lax.dot_general(high_all, low, NT, preferred_element_type=f32)
+            + lax.dot_general(low_all, high, NT, preferred_element_type=f32)
+        )
+        for p, keep_p in enumerate(keeps):
+            gram = grams[128 * p : 128 * (p + 1)]
             diagonal = jnp.where(row == col, gram, 0.0)
             inverse = lax.rsqrt(jnp.sum(diagonal, axis=1, keepdims=True) + eps_norm)
             inverse_row = lax.rsqrt(jnp.sum(diagonal, axis=0, keepdims=True) + eps_norm)
@@ -534,7 +535,7 @@
             if mine:
                 half[o, slot, :, tile0 + 3 * j : tile0 + 3 * j + 3] = part
             else:
-                send[o, :, tile0 + 3 * j : tile0 + 3 * j + 3] = part
+                send[o, lax.rem(slot, 2), :, tile0 + 3 * j : tile0 + 3 * j + 3] = part
 
     def product(mine, slot, uses):
         c = core if mine else 1 - core
@@ -568,7 +569,7 @@
                             if mine:
                                 half[j, slot, d1 * 4 + d2, d3 * 3 + ct] = tile
                             else:
-                                send[j, d1 * 4 + d2, d3 * 3 + ct] = tile
+                                send[j, lax.rem(slot, 2), d1 * 4 + d2, d3 * 3 + ct] = tile
             return 0
 
         lax.fori_loop(0, 4, block, 0)
@@ -670,9 +671,9 @@
         return a, lax.rem(a + 1, 4), lax.rem(a + 2, 4), lax.rem(a + 3, 4)
 
     def copy0(o, u):
-        slot = lax.rem(u, 2)
+        slot, way = lax.rem(u, SLOTS), lax.rem(u, 2)
         return pltpu.make_async_remote_copy(
-            src_ref=send.at[o], dst_ref=got0.at[o, slot], send_sem=sem0_s.at[o], recv_sem=sem0_r.at[o, slot],
+            src_ref=send.at[o, way], dst_ref=got0.at[o, slot], send_sem=sem0_s.at[o, way], recv_sem=sem0_r.at[o, slot],
             device_id=neighbour(place, "c", 1), device_id_type=MESH,
         )
 
@@ -846,7 +847,7 @@
             copy0(o, u).wait()
 
             def add(i, _):
-                half[o, lax.rem(u, 4), i] += got0[o, lax.rem(u, 2), i]
+                half[o, lax.rem(u, 4), i] += got0[o, slot, i]
                 return 0
 
             lax.fori_loop(0, 16, add, 0)
@@ -878,7 +879,11 @@
         return job
 
     def tick(u, _):
-        when(u, 0, TRIPLES, make)
+        def make_one(v, _):
+            make(v)
+            return 0
+
+        lax.fori_loop(jnp.where(u == 0, 0, jnp.maximum(u, 2)), jnp.where(u == 0, 2, jnp.minimum(u + 1, TRIPLES)), make_one, 0)
         when(u - 3, 0, TRIPLES, third(0))
         when(u - 4, 0, DIRECT, second(1))
         when(u - 5, 0, DIRECT, third(1))
@@ -928,7 +933,7 @@
         half, send = half_ref, send_ref
         lax.fori_loop(0, DIRECT + 7, tick, 0)
 
-    pl.run_scoped(reduce_all, pltpu.VMEM((3, 4, 16, 12, 8, 128), f32), pltpu.VMEM((3, 16, 12, 8, 128), f32))
+    pl.run_scoped(reduce_all, pltpu.VMEM((3, 4, 16, 12, 8, 128), f32), pltpu.VMEM((3, 2, 16, 12, 8, 128), f32))
     out_copy.start()
     vec_copy.start()
     for copy in (dx_copy, emb_copy, loss_copy, out_copy, vec_copy):
@@ -1026,14 +1031,14 @@
             vm(256, 3072, dtype=bf16), vm(256, 2304, dtype=bf16), vm(2, 1, 9216), vm(3, 2, 768, 256, dtype=bf16),
             vm(2, 1, 2304), vm(2, 1, 768), vm(2, 1, 768), vm(2, 1, 768), vm(2, 1, 3072), vm(2, 1, 768), vm(2, 1, 768), vm(2, 1, 768),
             vm(2, 1, 768), vm(2, 1, 768), vm(2, 2, 64, 6, 128), vm(TRIPLES, 3, 4, *tile), vm(2, 128), vm(128, 1),
-            vm(3, 2, 16, 12, *tile),
+            vm(3, SLOTS, 16, 12, *tile),
             vm(3, SLOTS, 2, 2, 12, *tile), vm(3, SLOTS, 2, 4, 12, *tile),
             vm(3, SLOTS, 4, 12, *tile), vm(3, SLOTS, 2, 6, *tile), vm(3, SLOTS, 2, 12, *tile),
             vm(3, SLOTS, 4, 4, *tile), vm(3, SLOTS, 2, 2, *tile), vm(3, SLOTS, 2, 4, *tile), vm(3, 4, 24, 128),
             vm(3, 2, 3, 12, *tile), vm(3, 2, 3, 4, *tile),
             vm(4, 4, 2, *tile), vm(3, 4, 2, *tile), vm(3, 2, *tile), vm(2, *tile), vm(7, 2, *tile),
             dma((4, 4)), dma((7,)), dma((8,)), dma((7,)), dma((2,)), dma((2,)), dma((2,)), dma((2,)),
-            dma((3, 6, SLOTS)), dma((3, 6, SLOTS)), dma((3,)), dma((3, 2)), dma((3, 2, 2)), dma((3, 2, 2)),
+            dma((3, 6, SLOTS)), dma((3, 6, SLOTS)), dma((3, 2)), dma((3, SLOTS)), dma((3, 2, 2)), dma((3, 2, 2)),
             dma((3,)), dma((3,)),
         ],
         compiler_params=pltpu.CompilerParams(

time: 171 us -> 169 us (0.988)
  no operation moved by 1% of the time
where the time goes in v7:
time: 169 us
  Pallas kernels  167 us (99%)
  between operations  2.11 us (1%)
    pallas_call x1, Pallas kernels, body(): pl.pallas_call(whole_kernel, out_shape=[jax.ShapeDtypeStruct(s, t) for s,...  164 us

profile of v7, /device:TPU:0, one launch (start us, length us, event | category | flops | bytes accessed | tf_op | source)
XLA Modules:
  0.0 169.0 jit_solution(1332927936105046985)
XLA Ops:
  1.9 163.8 %shard_map.298 = (f32[12,3,4,8,128]{4,3,2,1,0:T(8,128)}, f32[2,128]{1,0:T(2,128)}, f32[128,1]{1,0:T(8,128)}, f32[2,1,768]{2,1,0:T(1,128)}, f32[1,256,768]{2,1,0:...) custom-call(s32[1]{0:T(128)S(6)} %copy.34.count_ref, ...), custom_call_target="tpu_custom_call" | custom-call | tf_op jit(solution)/shard_map/pallas_call | solution.py:1022
  165.7 3.1 %shard_map.299 = (f32[4]{0:T(128)}, f32[1,2,768]{2,1,0:T(2,128)}, f32[1,256,768]{2,1,0:T(8,128)}, f32[6,2,2304]{2,1,0:T(2,128)}, f32[2,12]{1,0:T(2,128)}, /*inde...) custom-call(f32[12,3,4,8,128]{4,3,2,1,0:T(8,128)} %get-tuple-element, ...), custom_call_target="tpu_custom_call" | custom-call | tf_op jit(solution)/shard_map/pallas_call | solution.py:1054
